TPU v7x, 512 devices: a whole 4x4x16 slice. The times are simulated.
512 devices in a mesh: row: 8 (over z_lo), col: 8 (over x, core), depth: 8 (over y, z_hi).
Axes of the slice: x: 4, y: 4, z: 16 (z_hi: 2, z_lo: 8; z = z_hi * 8 + z_lo), core: 2. Of those that a mesh axis runs over, the one named last changes fastest.
Arguments:
- tokens: bfloat16 [512, 7424], P(('col', 'depth'), 'row'), may hold values from -6 to 6
- out_grad: bfloat16 [512, 7424], P(('col', 'depth'), 'row'), may hold values from -1.5 to 1.5
- up_weight: bfloat16 [7424, 29696], P('row', ('col', 'depth')), may hold values from -0.0625 to 0.0625
- down_weight: bfloat16 [29696, 7424], P(('col', 'depth'), 'row'), may hold values from -0.03125 to 0.03125
Outputs:
- token_grad: bfloat16 [512, 7424], P(('col', 'depth'), 'row')
- up_grad: float32 [7424, 29696], P('row', ('col', 'depth'))
- down_grad: float32 [29696, 7424], P(('col', 'depth'), 'row')
All inputs are finite; a program needn't handle non-finite values.
Results may differ from a plain program's by a relative error of at most 0.024.
Values may be sent and summed in bfloat16 or wider, within the bound.
No kernel may reach another device: no remote copies, remote signals or barrier semaphores. Data moves between devices by JAX's collectives and lax.ppermute only.
A program may use at most 192 MiB of HBM per device.

v0:
```python
import jax
import jax.numpy as jnp
from jax import lax
from jax.sharding import PartitionSpec as P


def gelu_slope(preact):
    normal_cdf = 0.5 * (1.0 + lax.erf(preact * 0.7071067811865476))
    return normal_cdf + preact * jnp.exp(-0.5 * preact * preact) * 0.3989422804014327


def rounded(partial_value):
    return lax.optimization_barrier(partial_value.astype(jnp.bfloat16)).astype(jnp.float32)


def against(leading, trailing):
    return lax.dot_general(
        leading, trailing, (((1,), (1,)), ((), ())), preferred_element_type=jnp.float32
    )


def activate(pre_sum, grad_sum):
    active = jax.nn.gelu(pre_sum, approximate=False).astype(jnp.bfloat16)
    hidden_grad = (grad_sum * gelu_slope(pre_sum)).astype(jnp.bfloat16)
    return (active, hidden_grad)


def on_device(tokens, out_grad, up_weight, down_weight):
    block_rows = tokens.shape[0]
    inputs_all, upstream_all = (
        lax.all_gather(tokens, ("col", "depth"), axis=0, tiled=True),
        lax.all_gather(out_grad, ("col", "depth"), axis=0, tiled=True),
    )
    hidden_width = up_weight.shape[1]
    sums_both = lax.psum_scatter(
        jnp.concatenate(
            [
                jnp.dot(inputs_all, up_weight, preferred_element_type=jnp.float32),
                against(upstream_all, down_weight),
            ],
            axis=1,
        ).astype(jnp.bfloat16),
        "row",
        scatter_dimension=0,
        tiled=True,
    ).astype(jnp.float32)
    active, hidden_grad = activate(sums_both[:, :hidden_width], sums_both[:, hidden_width:])
    active_all, hidden_all = (
        lax.all_gather(active, "row", axis=0, tiled=True),
        lax.all_gather(hidden_grad, "row", axis=0, tiled=True),
    )
    token_grad = lax.psum_scatter(
        against(hidden_all, up_weight), ("col", "depth"), scatter_dimension=0, tiled=True
    ).astype(jnp.bfloat16)
    groups = lax.axis_size("depth")
    columns = lax.axis_size("col")
    feature_width = tokens.shape[1]
    inputs_four = inputs_all.reshape(columns, groups, block_rows, feature_width)
    upstream_four = upstream_all.reshape(columns, groups, block_rows, feature_width)
    active_four = active_all.reshape(columns, groups, block_rows, hidden_width)
    hidden_four = hidden_all.reshape(columns, groups, block_rows, hidden_width)
    up_grad = jnp.zeros((feature_width, hidden_width), jnp.float32)
    down_grad = jnp.zeros((hidden_width, feature_width), jnp.float32)
    for group_index in range(groups):
        up_grad = up_grad + rounded(
            jnp.einsum(
                "ctd,ctf->df",
                inputs_four[:, group_index],
                hidden_four[:, group_index],
                preferred_element_type=jnp.float32,
            )
        )
        down_grad = down_grad + rounded(
            jnp.einsum(
                "ctf,ctd->fd",
                active_four[:, group_index],
                upstream_four[:, group_index],
                preferred_element_type=jnp.float32,
            )
        )
    return (token_grad, up_grad, down_grad)


def solution(mesh):
    return jax.shard_map(
        on_device,
        mesh=mesh,
        in_specs=(
            P(("col", "depth"), "row"),
            P(("col", "depth"), "row"),
            P("row", ("col", "depth")),
            P(("col", "depth"), "row"),
        ),
        out_specs=(
            P(("col", "depth"), "row"),
            P("row", ("col", "depth")),
            P(("col", "depth"), "row"),
        ),
        check_vma=False,
    )
```

profile of v0, /device:TPU:1, one launch (start us, length us, event | category | flops | bytes accessed | tf_op | source)
XLA Modules:
  0.0 1373.8 jit_solution(1092358099000445497)
XLA Ops:
  7.2 0.0 copy-start
  7.2 0.0 copy-start.9
  7.2 0.0 reduce-scatter.7.cloned.1.call-start
  7.2 323.5 %all_gather.13 = bf16[512,928]{1,0:T(8,128)(2,1)S(1)} all-gather(bf16[8,928]{1,0:T(8,128)(2,1)} %param.5), channel_id=1, replica_groups=mesh['row'=8,'col'=8,'depth'=8] {'col','depth'}, dimensions={0}, use_global_device_ids=true | all-gather | bytes 965120 | tf_op jit(solution)/shard_map/all_gather | solution.py:32
  330.8 0.0 copy-start.1
  330.8 316.1 %all_gather.12 = bf16[512,928]{1,0:T(8,128)(2,1)S(1)} all-gather(bf16[8,928]{1,0:T(8,128)(2,1)} %param.4), channel_id=1, replica_groups=mesh['row'=8,'col'=8,'depth'=8] {'col','depth'}, dimensions={0}, use_global_device_ids=true | all-gather | bytes 965120 | tf_op jit(solution)/shard_map/all_gather | solution.py:31
  646.9 0.0 copy-done.1
  646.9 0.0 copy-done.9
  646.9 0.7 convolution_convert_fusion
  647.6 0.0 copy-done
  647.6 0.7 convolution_convert_fusion.1
  648.3 0.1 pad_maximum_fusion
  648.4 1.3 copy.94
  649.7 0.0 reduce-scatter.7.cloned.1.call-update
  649.7 0.0 reduce-scatter.5.cloned.1.call-start
  649.8 88.0 %reduce-scatter.7.cloned.1.call-done = bf16[64,928]{1,0:T(8,128)(2,1)} async-done(((bf16[512,928]{1,0:T(8,128)(2,1)}), bf16[64,928]{1,0:T(8,128)(2,1)}) %reduce-scatter.7.cloned.1.call-update) | async-done | bytes 118800
  737.8 1.1 copy.95
  738.9 0.6 fusion.16
  739.5 0.1 copy.59
  739.6 42.4 %all_gather.14 = bf16[512,464]{1,0:T(8,128)(2,1)S(1)} all-gather(bf16[64,464]{1,0:T(8,128)(2,1)S(1)} %copy.59), channel_id=1, replica_groups=mesh['row'=8,'col'=8,'depth'=8] {'row'}, dimensions={0}, use_global_device_ids=true | all-gather | bytes 534528 | tf_op jit(solution)/shard_map/all_gather | solution.py:50
  782.0 2.1 fusion.24
  784.1 1.4 fusion.7
  785.4 1.4 fusion.6
  786.8 1.4 fusion.5
  788.2 1.4 fusion.4
  789.6 1.4 fusion.3
  791.0 1.4 fusion.2
  792.4 0.0 reduce-scatter.5.cloned.1.call-update
  792.5 0.4 fusion.1
  792.9 0.0 copy-start.3
  792.9 0.0 copy-start.4
  792.9 0.0 copy-start.5
  792.9 0.0 copy-start.6
  793.0 0.0 copy-start.7
  793.0 0.0 copy-start.8
  793.0 0.4 fusion
  793.4 0.7 copy-done.3
  794.1 0.3 copy-done.4
  794.4 0.3 copy-done.5
  794.7 0.3 copy-done.6
  795.0 0.3 copy-done.7
  795.3 0.3 copy-done.8
  795.5 1.7 convert_add_fusion.1
  797.3 1.7 copy.93
  799.0 0.1 copy.76
  799.1 43.2 %all_gather.15 = bf16[512,464]{1,0:T(8,128)(2,1)S(1)} all-gather(bf16[64,464]{1,0:T(8,128)(2,1)S(1)} %copy.76), channel_id=1, replica_groups=mesh['row'=8,'col'=8,'depth'=8] {'row'}, dimensions={0}, use_global_device_ids=true | all-gather | bytes 534528 | tf_op jit(solution)/shard_map/all_gather | solution.py:49
  842.3 0.0 copy-start.2
  842.3 1.4 bitcast_convert_fusion
  843.7 0.0 copy-done.2
  843.8 0.4 bitcast_convert_fusion.1
  844.2 0.4 bitcast_convert_fusion.2
  844.7 0.4 bitcast_convert_fusion.3
  845.1 0.4 bitcast_convert_fusion.4
  845.6 0.4 bitcast_convert_fusion.5
  846.0 0.4 bitcast_convert_fusion.6
  846.5 0.4 bitcast_convert_fusion.7
  846.9 3.0 convert_add_fusion
  849.9 515.7 %reduce-scatter.5.cloned.1.call-done = f32[8,928]{1,0:T(8,128)} async-done(((f32[512,928]{1,0:T(8,128)}), f32[8,928]{1,0:T(8,128)}) %reduce-scatter.5.cloned.1.call-update) | async-done | bytes 29712 | tf_op jit(solution)/shard_map/reduce_scatter | solution.py:52
  1365.6 1.4 convert_element_type.135
  (1 shorter events, 0.0 us)
Async XLA Ops:
  7.2 640.4 %copy-start = (bf16[928,464]{1,0:T(8,128)(2,1)S(1)}, bf16[928,464]{1,0:T(8,128)(2,1)}, u32[]{:S(2)}) copy-start(bf16[928,464]{1,0:T(8,128)(2,1)} %param.6) | copy-start | bytes 2583556
  7.2 639.7 %copy-start.9 = (bf16[464,928]{1,0:T(8,128)(2,1)S(1)}, bf16[464,928]{1,0:T(8,128)(2,1)}, u32[]{:S(2)}) copy-start(bf16[464,928]{1,0:T(8,128)(2,1)} %param.7) | copy-start | bytes 2583556
  7.2 730.6 %reduce-scatter.7.cloned.1.call-start = ((), (), s32[]{:S(2)}) async-start(), calls=%async_computation.3 | async-start | bytes 1179648
  330.8 316.1 %copy-start.1 = (bf16[512,928]{1,0:T(8,128)(2,1)}, bf16[512,928]{1,0:T(8,128)(2,1)S(1)}, u32[]{:S(2)}) copy-start(bf16[512,928]{1,0:T(8,128)(2,1)S(1)} %all_gather.13) | copy-start | bytes 2850820
  649.7 715.9 %reduce-scatter.5.cloned.1.call-start = ((), (), s32[]{:S(2)}) async-start(), calls=%async_computation.2 | async-start | bytes 2129920 | tf_op jit(solution)/shard_map/reduce_scatter | solution.py:52
  792.9 1.2 copy-start.3
  792.9 1.5 copy-start.4
  792.9 1.7 copy-start.5
  792.9 2.0 copy-start.6
  793.0 2.3 copy-start.7
  793.0 2.6 copy-start.8
  842.3 1.5 copy-start.2
Sparse Core Ops, SparseCore 0:
  649.8 87.9 reduce-scatter.6
  792.6 572.9 reduce-scatter.4
where the time goes:
time: 1380 us; the launch traced here: 1370 us
  blocking collectives  725 us (53%)
  waiting for transfers between devices  604 us (44%)
  matrix products  17.3 us (1%)
  between operations  14.3 us (1%)
    reduce_scatter x1, waiting for transfers between devices, on_device(): lax.psum_scatter(against(hidden_all, up_weight), ('col', 'depth'), scatte...  516 us
    all_gather x1, blocking collectives, on_device(): lax.all_gather(out_grad, ('col', 'depth'), axis=0, tiled=True)  324 us
    all_gather x1, blocking collectives, on_device(): lax.all_gather(tokens, ('col', 'depth'), axis=0, tiled=True)  316 us
    unnamed x3, waiting for transfers between devices  88.1 us
    all_gather x1, blocking collectives, on_device(): lax.all_gather(active, 'row', axis=0, tiled=True)  43.2 us
    all_gather x1, blocking collectives, on_device(): lax.all_gather(hidden_grad, 'row', axis=0, tiled=True)  42.4 us
  transfers between devices with their start and end apart: 2, of which 2 were waited for; matrix products, arithmetic and copies ran while one was open for 1% of the time, Pallas kernels for 0%

commit v1 on v0

v1 whole, which is shorter than its diff:
```python
import jax
import jax.numpy as jnp
from jax import lax
from jax.sharding import Mesh, PartitionSpec as P

AXES = ("za", "zb", "zc", "x", "core", "y", "far")
SIZES = (2, 2, 2, 4, 2, 4, 2)
ROW = ("za", "zb", "zc")
TOKENS_OVER = ("x", "core", "y", "far")
SWAP = [(0, 1), (1, 0)]


def gelu_cdf(preact):
    return 0.5 * (1.0 + lax.erf(preact * 0.7071067811865476))


def against(leading, trailing):
    return lax.dot_general(
        leading, trailing, (((1,), (1,)), ((), ())), preferred_element_type=jnp.float32
    )


def weight_grad(leading, trailing):
    return lax.dot_general(
        leading, trailing, (((0,), (0,)), ((), ())), preferred_element_type=jnp.float32
    )


def exchange_sum(blocks, axis):
    swapped = lax.all_to_all(blocks, axis, split_axis=0, concat_axis=0, tiled=True)
    return jnp.sum(swapped.astype(jnp.float32), axis=0)


def on_device(tokens, out_grad, up_weight, down_weight):
    rows, features = tokens.shape
    hidden = up_weight.shape[1]
    with jax.named_scope("gather_tokens"):
        own = jnp.concatenate([tokens, out_grad], axis=0)
        for axis in ("far", "y", "x"):
            own = lax.all_gather(own, axis, axis=0, tiled=True)
        other = lax.ppermute(own, "core", SWAP)
        own = own.reshape(-1, 2, rows, features)
        other = other.reshape(-1, 2, rows, features)
        inputs, upstream = (
            jnp.concatenate([own[:, i], other[:, i]], axis=0).reshape(-1, features)
            for i in range(2)
        )
    with jax.named_scope("row_sum"):
        partials = jnp.stack(
            [
                jnp.dot(inputs, up_weight, preferred_element_type=jnp.float32)
                .astype(jnp.bfloat16)
                .reshape(8, -1, hidden),
                against(upstream, down_weight).astype(jnp.bfloat16).reshape(8, -1, hidden),
            ],
            axis=1,
        )
        share = partials.shape[2]
        quarter = exchange_sum(partials.reshape(4, 2, 2, share, hidden), ("zb", "zc"))
        sums = exchange_sum(quarter.astype(jnp.bfloat16), "za")
    with jax.named_scope("activate"):
        preact, grad_active = sums[0], sums[1]
        cdf = gelu_cdf(preact)
        slope = cdf + preact * jnp.exp(-0.5 * preact * preact) * 0.3989422804014327
        both = jnp.stack([preact * cdf, grad_active * slope]).astype(jnp.bfloat16)[None]
    with jax.named_scope("row_gather"):
        both = lax.all_gather(both, "za", axis=0, tiled=True)
        both = lax.all_gather(both, ("zb", "zc"), axis=0, tiled=True)
        active = both[:, 0].reshape(-1, hidden)
        hidden_grad = both[:, 1].reshape(-1, hidden)
    with jax.named_scope("token_grad"):
        partial_grad = against(hidden_grad, up_weight).reshape(2, -1, features)
        arrived = lax.ppermute(partial_grad[1].astype(jnp.bfloat16), "core", SWAP)
        chip_sum = (partial_grad[0] + arrived.astype(jnp.float32)).astype(jnp.bfloat16)
        x_sum = exchange_sum(chip_sum.reshape(4, -1, features), "x").astype(jnp.bfloat16)
        token_grad = exchange_sum(x_sum.reshape(8, -1, features), ("y", "far"))
    with jax.named_scope("weight_grads"):
        up_grad = weight_grad(inputs, hidden_grad)
        down_grad = weight_grad(active, upstream)
    return (token_grad.astype(jnp.bfloat16), up_grad, down_grad)


def solution(mesh):
    fine = Mesh(mesh.devices.reshape(SIZES), AXES)
    return jax.shard_map(
        on_device,
        mesh=fine,
        in_specs=(P(TOKENS_OVER, ROW), P(TOKENS_OVER, ROW), P(ROW, TOKENS_OVER), P(TOKENS_OVER, ROW)),
        out_specs=(P(TOKENS_OVER, ROW), P(ROW, TOKENS_OVER), P(TOKENS_OVER, ROW)),
        check_vma=False,
    )
```

time: 1380 us -> 192 us (0.14)
  waiting for transfers between devices: 604 us -> 12.1 us
  blocking collectives: 725 us -> 136 us
  starting transfers between devices: 0.08 us -> 22.9 us
    all_gather x4 -> x5, blocking collectives: 725 us -> 70.7 us  [the longest x3 38.9 us: on_device(): own = lax.all_gather(own, axis, axis=0, tiled=True)]
    reduce_scatter x1 -> x0, waiting for transfers between devices: 516 us -> none  [on_device(): lax.psum_scatter(against(hidden_all, up_weight), ('col', 'depth'), scatte...]
    unnamed x3 -> x0, waiting for transfers between devices: 88.1 us -> none
    all_to_all x0 -> x3, blocking collectives: none -> 65.4 us  [exchange_sum(): lax.all_to_all(blocks, axis, split_axis=0, concat_axis=0, tiled=True)]
  transfers between devices with their start and end apart: 2 -> 3, of which waited for: 2 -> 3; matrix products, arithmetic and copies ran while one was open for 1% -> 3% of each run, Pallas kernels for 0% -> 0%
where the time goes in v1:
time: 192 us; the launch traced here: 191 us
  blocking collectives  136 us (71%)
  starting transfers between devices  22.9 us (12%)
  waiting for transfers between devices  12.1 us (6%)
  matrix products  9.49 us (5%)
  local copies, waits for them, and re-layouts  6.46 us (3%)
  other arithmetic  2.85 us (1%)
    all_to_all x3, blocking collectives, exchange_sum(): lax.all_to_all(blocks, axis, split_axis=0, concat_axis=0, tiled=True)  65.4 us
    all_gather x3, blocking collectives, on_device(): own = lax.all_gather(own, axis, axis=0, tiled=True)  38.9 us
    all_gather x1, blocking collectives, on_device(): both = lax.all_gather(both, ('zb', 'zc'), axis=0, tiled=True)  20.4 us
    all_gather x1, blocking collectives, on_device(): both = lax.all_gather(both, 'za', axis=0, tiled=True)  11.4 us
    ppermute x1, starting transfers between devices, on_device(): other = lax.ppermute(own, 'core', SWAP)  9.98 us
    all_to_all x1, starting transfers between devices, exchange_sum(): lax.all_to_all(blocks, axis, split_axis=0, concat_axis=0, tiled=True)  9.31 us
    all_to_all x1, waiting for transfers between devices, exchange_sum(): lax.all_to_all(blocks, axis, split_axis=0, concat_axis=0, tiled=True)  9.06 us
    dot_general x2, matrix products, weight_grad(): lax.dot_general(leading, trailing, (((0,), (0,)), ((), ())), preferred_el...  5.18 us
  transfers between devices with their start and end apart: 3, of which 3 were waited for; matrix products, arithmetic and copies ran while one was open for 3% of the time, Pallas kernels for 0%

profile of v1, /device:TPU:1, one launch (start us, length us, event | category | flops | bytes accessed | tf_op | source)
XLA Modules:
  0.0 190.7 jit_solution(5639801394472609073)
XLA Ops:
  0.6 0.0 copy-start
  0.6 0.8 pad_maximum_fusion.2
  1.5 16.4 %all_gather.15 = bf16[32,928]{1,0:T(8,128)(2,1)S(1)} all-gather(bf16[16,928]{1,0:T(8,128)(2,1)S(1)} %pad_maximum_fusion.2), channel_id=1, replica_groups=mesh['za'=2,'zb'=2,'zc'=2,'x'=4,'core'=2,'y'=4,'far'=2] {'far'}, dimensions={0}, use_global_device_ids=true | all-gather | bytes 89088 | tf_op jit(solution)/shard_map/gather_tokens/all_gather | solution.py:40
  17.9 9.9 %all_gather.16 = bf16[128,928]{1,0:T(8,128)(2,1)S(1)} all-gather(bf16[32,928]{1,0:T(8,128)(2,1)S(1)} %all_gather.15), channel_id=1, replica_groups=mesh['za'=2,'zb'=2,'zc'=2,'x'=4,'core'=2,'y'=4,'far'=2] {'y'}, dimensions={0}, use_global_device_ids=true | all-gather | bytes 296960 | tf_op jit(solution)/shard_map/gather_tokens/all_gather | solution.py:40
  27.8 12.6 %all_gather.17 = bf16[512,928]{1,0:T(8,128)(2,1)S(1)} all-gather(bf16[128,928]{1,0:T(8,128)(2,1)S(1)} %all_gather.16), channel_id=1, replica_groups=mesh['za'=2,'zb'=2,'zc'=2,'x'=4,'core'=2,'y'=4,'far'=2] {'x'}, dimensions={0}, use_global_device_ids=true | all-gather | bytes 1187840 | tf_op jit(solution)/shard_map/gather_tokens/all_gather | solution.py:40
  40.4 1.3 copy.40
  41.7 10.0 %collective-permute-start = (bf16[512,928]{0,1:T(8,128)(2,1)}, bf16[512,928]{0,1:T(8,128)(2,1)}, u32[]{:S(2)}, u32[]{:S(2)}) collective-permute-start(bf16[512,928]{0,1:T(8,128)(2,1)} %copy.40), channel_id=1, source_target_pairs={{0,8},{8,0},{1,9},{9,1},{2,10},{10,2},{3,11},{11,3},{4,12},{12,4},... | collective-permute-start | bytes 2850824 | tf_op jit(solution)/shard_map/gather_tokens/ppermute | solution.py:41
  51.6 0.9 slice_bitcast_fusion.3
  52.5 1.6 collective-permute-done
  54.1 1.5 copy.41
  55.6 0.0 copy-start.4
  55.6 0.9 slice_bitcast_fusion.2
  56.5 0.0 copy-start.1
  56.5 0.0 copy-done
  56.5 0.3 copy-done.4
  56.7 1.7 convolution_convert_fusion.1
  58.5 0.2 copy.43
  58.7 0.0 copy-done.1
  58.7 1.9 convolution_convert_fusion
  60.6 0.2 copy.44
  60.8 0.1 pad_maximum_fusion
  61.0 0.1 copy.45
  61.0 27.9 %all_to_all.20 = bf16[4,2,2,64,464]{4,3,1,2,0:T(8,128)(2,1)S(1)} all-to-all(bf16[4,2,2,64,464]{4,3,1,2,0:T(8,128)(2,1)S(1)} %copy.45), channel_id=1, replica_groups=mesh['za'=2,'zb'=2,'zc'=2,'x'=4,'core'=2,'y'=4,'far'=2] {'zb','zc'}, dimensions={0} | all-to-all | bytes 1900544 | tf_op jit(solution)/shard_map/row_sum/all_to_all | solution.py:30
  88.9 0.2 reduce_sum.45
  89.2 25.7 %all_to_all.21 = bf16[2,2,64,464]{3,2,1,0:T(8,128)(2,1)S(1)} all-to-all(bf16[2,2,64,464]{3,2,1,0:T(8,128)(2,1)S(1)} %copy.47), channel_id=1, replica_groups=mesh['za'=2,'zb'=2,'zc'=2,'x'=4,'core'=2,'y'=4,'far'=2] {'za'}, dimensions={0} | all-to-all | bytes 475136 | tf_op jit(solution)/shard_map/row_sum/all_to_all | solution.py:30
  115.0 0.1 fusion.9
  115.1 11.4 %all_gather.18 = bf16[2,2,64,464]{3,2,1,0:T(8,128)(2,1)S(1)} all-gather(bf16[1,2,64,464]{3,2,1,0:T(8,128)(2,1)S(1)} %pad_maximum_fusion.1), channel_id=1, replica_groups=mesh['za'=2,'zb'=2,'zc'=2,'x'=4,'core'=2,'y'=4,'far'=2] {'za'}, dimensions={0}, use_global_device_ids=true | all-gather | bytes 356352 | tf_op jit(solution)/shard_map/row_gather/all_gather | solution.py:67
  126.5 20.4 %all_gather.19 = bf16[8,2,64,464]{3,2,1,0:T(8,128)(2,1)S(1)} all-gather(bf16[2,2,64,464]{3,2,1,0:T(8,128)(2,1)S(1)} %all_gather.18), channel_id=1, replica_groups=mesh['za'=2,'zb'=2,'zc'=2,'x'=4,'core'=2,'y'=4,'far'=2] {'zb','zc'}, dimensions={0}, use_global_device_ids=true | all-gather | bytes 1187840 | tf_op jit(solution)/shard_map/row_gather/all_gather | solution.py:68
  146.8 0.9 fusion.15
  147.7 0.7 fusion.16
  148.4 0.1 slice.75
  148.5 3.6 %collective-permute-start.1 = (bf16[256,928]{0,1:T(8,128)(2,1)S(1)}, bf16[256,928]{0,1:T(8,128)(2,1)S(1)}, u32[]{:S(2)}, u32[]{:S(2)}) collective-permute-start(bf16[256,928]{0,1:T(8,128)(2,1)S(1)} %slice.75), channel_id=1, source_target_pairs={{0,8},{8,0},{1,9},{9,1},{2,10},{10,2},{3,11},{11,3},{4,12},{12,4},... | collective-permute-start | bytes 1425416 | tf_op jit(solution)/shard_map/token_grad/ppermute | solution.py:73
  152.1 1.4 collective-permute-done.1
  153.5 0.2 fusion
  153.7 0.2 copy.48
  153.9 11.8 %all_to_all.22 = bf16[4,64,928]{2,1,0:T(8,128)(2,1)S(1)} all-to-all(bf16[4,64,928]{2,1,0:T(8,128)(2,1)S(1)} %bitcast.40), channel_id=1, replica_groups=mesh['za'=2,'zb'=2,'zc'=2,'x'=4,'core'=2,'y'=4,'far'=2] {'x'}, dimensions={0} | all-to-all | bytes 950272 | tf_op jit(solution)/shard_map/token_grad/all_to_all | solution.py:30
  165.7 0.7 reduce_sum.47
  166.5 9.3 %all-to-all-start.3 = ((bf16[8,8,928]{2,1,0:T(8,128)(2,1)}), bf16[8,8,928]{2,1,0:T(8,128)(2,1)S(1)}, u32[]{:S(2)}, u32[]{:S(2)}) async-start(bf16[8,8,928]{2,1,0:T(8,128)(2,1)} %bitcast.14), calls=%async_computation.3 | async-start | bytes 262144 | tf_op jit(solution)/shard_map/token_grad/all_to_all | solution.py:30
  175.8 0.0 copy-start.2
  175.8 0.0 copy-start.3
  175.8 3.2 %fusion.2 = f32[928,464]{1,0:T(8,128)} fusion(bf16[512,464]{1,0:T(8,128)(2,1)S(1)} %bitcast.39, bf16[32,8,928]{2,1,0:T(8,128)(2,1)} %get-tuple-element.7, bf16[32,8,928]{2,1,0:T(8,128)(2,1)} %get-tuple-element.5), kind=kOutput, calls=%fused_computation.9 | convolution fusion | flops 441401344 | bytes 3147776 | tf_op jit(solution)/shard_map/weight_grads/dot_general | solution.py:24
  179.0 0.0 copy-done.2
  179.0 0.0 copy-done.3
  179.0 1.9 %fusion.1 = f32[464,928]{1,0:T(8,128)} fusion(bf16[512,464]{1,0:T(8,128)(2,1)S(1)} %bitcast.43, bf16[32,8,928]{2,1,0:T(8,128)(2,1)S(1)} %copy-done.2, bf16[32,8,928]{2,1,0:T(8,128)(2,1)S(1)} %get-tuple-element.6), kind=kOutput, calls=%fused_computation.8 | convolution fusion | flops 441401344 | bytes 3147776 | tf_op jit(solution)/shard_map/weight_grads/dot_general | solution.py:24
  181.0 9.1 %all-to-all-done.3 = bf16[8,8,928]{2,1,0:T(8,128)(2,1)S(1)} async-done(((bf16[8,8,928]{2,1,0:T(8,128)(2,1)}), bf16[8,8,928]{2,1,0:T(8,128)(2,1)S(1)}, u32[]{:S(2)}, u32[]{:S(2)}) %all-to-all-start.3) | async-done | bytes 118816 | tf_op jit(solution)/shard_map/token_grad/all_to_all | solution.py:30
  190.0 0.6 reduce_sum.48
  (3 shorter events, 0.1 us)
Async XLA Ops:
  0.6 55.8 %copy-start = (bf16[928,464]{1,0:T(8,128)(2,1)S(1)}, bf16[928,464]{1,0:T(8,128)(2,1)}, u32[]{:S(2)}) copy-start(bf16[928,464]{1,0:T(8,128)(2,1)} %param.6) | copy-start | bytes 2583556
  41.7 12.5 %collective-permute-start = (bf16[512,928]{0,1:T(8,128)(2,1)}, bf16[512,928]{0,1:T(8,128)(2,1)}, u32[]{:S(2)}, u32[]{:S(2)}) collective-permute-start(bf16[512,928]{0,1:T(8,128)(2,1)} %copy.40), channel_id=1, source_target_pairs={{0,8},{8,0},{1,9},{9,1},{2,10},{10,2},{3,11},{11,3},{4,12},{12,4},... | collective-permute-start | bytes 2850824 | tf_op jit(solution)/shard_map/gather_tokens/ppermute | solution.py:41
  55.6 1.2 copy-start.4
  56.5 2.2 %copy-start.1 = (bf16[32,8,928]{2,1,0:T(8,128)(2,1)}, bf16[32,8,928]{2,1,0:T(8,128)(2,1)S(1)}, u32[]{:S(2)}) copy-start(bf16[32,8,928]{2,1,0:T(8,128)(2,1)S(1)} %get-tuple-element.8) | copy-start | bytes 1425412
  148.5 5.0 %collective-permute-start.1 = (bf16[256,928]{0,1:T(8,128)(2,1)S(1)}, bf16[256,928]{0,1:T(8,128)(2,1)S(1)}, u32[]{:S(2)}, u32[]{:S(2)}) collective-permute-start(bf16[256,928]{0,1:T(8,128)(2,1)S(1)} %slice.75), channel_id=1, source_target_pairs={{0,8},{8,0},{1,9},{9,1},{2,10},{10,2},{3,11},{11,3},{4,12},{12,4},... | collective-permute-start | bytes 1425416 | tf_op jit(solution)/shard_map/token_grad/ppermute | solution.py:73
  166.5 23.6 %all-to-all-start.3 = ((bf16[8,8,928]{2,1,0:T(8,128)(2,1)}), bf16[8,8,928]{2,1,0:T(8,128)(2,1)S(1)}, u32[]{:S(2)}, u32[]{:S(2)}) async-start(bf16[8,8,928]{2,1,0:T(8,128)(2,1)} %bitcast.14), calls=%async_computation.3 | async-start | bytes 262144 | tf_op jit(solution)/shard_map/token_grad/all_to_all | solution.py:30
  175.8 3.3 %copy-start.2 = (bf16[32,8,928]{2,1,0:T(8,128)(2,1)S(1)}, bf16[32,8,928]{2,1,0:T(8,128)(2,1)}, u32[]{:S(2)}) copy-start(bf16[32,8,928]{2,1,0:T(8,128)(2,1)} %copy-done.1) | copy-start | bytes 1425412
  175.8 3.3 %copy-start.3 = (bf16[8,1,64,464]{3,2,1,0:T(8,128)(2,1)S(1)}, bf16[8,1,64,464]{3,2,1,0:T(8,128)(2,1)}, u32[]{:S(2)}) copy-start(bf16[8,1,64,464]{3,2,1,0:T(8,128)(2,1)} %get-tuple-element.3) | copy-start | bytes 1425412

commit v2 on v1

v2 whole, which is shorter than its diff:
```python
import functools

import jax
import jax.numpy as jnp
from jax import lax
from jax.experimental import pallas as pl
from jax.experimental.pallas import tpu as pltpu
from jax.sharding import Mesh, PartitionSpec as P

AXES = ("za", "zb", "zc", "x", "core", "y", "far")
SIZES = (2, 2, 2, 4, 2, 4, 2)
ROW = ("za", "zb", "zc")
TOKENS_OVER = ("x", "core", "y", "far")
SWAP = [(0, 1), (1, 0)]


def gelu_cdf(preact):
    return 0.5 * (1.0 + lax.erf(preact * 0.7071067811865476))


VMEM = pl.BlockSpec(memory_space=pltpu.VMEM)


def on_core(kernel, out_shape, flops, *operands):
    nbytes = 2 * sum(x.size for x in operands)
    return pl.pallas_call(
        kernel,
        out_shape=out_shape,
        in_specs=[VMEM] * len(operands),
        out_specs=[VMEM] * len(out_shape),
        compiler_params=pltpu.CompilerParams(vmem_limit_bytes=24 << 20),
        cost_estimate=pl.CostEstimate(flops=flops, bytes_accessed=nbytes, transcendentals=0),
    )(*operands)


def partials_kernel(own_ref, other_ref, up_ref, down_ref, parts_ref, inputs_ref, upstream_ref):
    for half, ref in enumerate((own_ref, other_ref)):
        for piece in range(2):
            block = 2 * half + piece
            rows = pl.ds(128 * block, 128)
            tokens = ref[8 * piece : 8 * piece + 8, 0].reshape(128, -1)
            grads = ref[8 * piece : 8 * piece + 8, 1].reshape(128, -1)
            inputs_ref[rows] = tokens
            upstream_ref[rows] = grads
            parts_ref[block, 0] = lax.dot_general(
                up_ref[...], tokens, (((0,), (1,)), ((), ())), preferred_element_type=jnp.float32
            ).astype(jnp.bfloat16)
            parts_ref[block, 1] = lax.dot_general(
                down_ref[...], grads, (((1,), (1,)), ((), ())), preferred_element_type=jnp.float32
            ).astype(jnp.bfloat16)


def token_grad_kernel(first, both_ref, up_ref, out_ref):
    for piece in range(2):
        out_ref[pl.ds(128 * piece, 128)] = lax.dot_general(
            both_ref[first + piece, 1],
            up_ref[...],
            (((0,), (1,)), ((), ())),
            preferred_element_type=jnp.float32,
        ).astype(jnp.bfloat16)


def total(blocks):
    acc = blocks[0].astype(jnp.float32)
    for i in range(1, blocks.shape[0]):
        acc = acc + blocks[i].astype(jnp.float32)
    return acc


def exchange_sum(blocks, axis):
    return total(lax.all_to_all(blocks, axis, split_axis=0, concat_axis=0, tiled=True))


def on_device(tokens, out_grad, up_weight, down_weight):
    rows, features = tokens.shape
    hidden = up_weight.shape[1]
    with jax.named_scope("gather_tokens"):
        pair = lax.all_gather(jnp.stack([tokens, out_grad]), "far", axis=1, tiled=True)
        copies = jnp.broadcast_to(pair[None], (16,) + pair.shape)
        own = lax.all_to_all(copies, ("x", "y"), split_axis=0, concat_axis=0, tiled=True)
        other = lax.ppermute(own, "core", SWAP)
    with jax.named_scope("row_sum"):
        held = jax.ShapeDtypeStruct((512, features), jnp.bfloat16)
        parts, inputs, upstream = on_core(
            partials_kernel,
            [jax.ShapeDtypeStruct((4, 2, hidden, 128), jnp.bfloat16), held, held],
            4 * 512 * features * hidden,
            own,
            other,
            up_weight,
            down_weight,
        )
        quarter = exchange_sum(parts, ("zb", "zc")).astype(jnp.bfloat16)
        preact, grad_active = total(lax.all_gather(quarter, "za", axis=0, tiled=False))
    with jax.named_scope("activate"):
        cdf = 0.5 * (1.0 + lax.erf(preact * 0.7071067811865476))
        slope = cdf + preact * jnp.exp(-0.5 * preact * preact) * 0.3989422804014327
        both = jnp.stack([preact * cdf, grad_active * slope]).astype(jnp.bfloat16)
    with jax.named_scope("row_gather"):
        both = lax.all_gather(both[None], ("zb", "zc"), axis=0, tiled=True)
    with jax.named_scope("token_grad"):
        half = jax.ShapeDtypeStruct((256, features), jnp.bfloat16)
        flops = 2 * 256 * features * hidden
        leaving, staying = (
            on_core(functools.partial(token_grad_kernel, first), [half], flops, both, up_weight)[0]
            for first in (2, 0)
        )
        arrived = lax.ppermute(leaving, "core", SWAP)
        chip_sum = staying.astype(jnp.float32) + arrived.astype(jnp.float32)
        plane_sum = exchange_sum(
            chip_sum.astype(jnp.bfloat16).reshape(16, -1, features), ("x", "y")
        )
        token_grad = exchange_sum(
            plane_sum.astype(jnp.bfloat16).reshape(2, rows, features), "far"
        )
    with jax.named_scope("weight_grads"):
        up_grad = jnp.einsum(
            "btd,bht->dh",
            inputs.reshape(4, -1, features),
            both[:, 1],
            preferred_element_type=jnp.float32,
        )
        down_grad = jnp.einsum(
            "bht,btd->hd",
            both[:, 0],
            upstream.reshape(4, -1, features),
            preferred_element_type=jnp.float32,
        )
    return (token_grad.astype(jnp.bfloat16), up_grad, down_grad)


def solution(mesh):
    fine = Mesh(mesh.devices.reshape(SIZES), AXES)
    return jax.shard_map(
        on_device,
        mesh=fine,
        in_specs=(P(TOKENS_OVER, ROW), P(TOKENS_OVER, ROW), P(ROW, TOKENS_OVER), P(TOKENS_OVER, ROW)),
        out_specs=(P(TOKENS_OVER, ROW), P(ROW, TOKENS_OVER), P(TOKENS_OVER, ROW)),
        check_vma=False,
    )
```

time: 192 us -> 170 us (0.89)
  blocking collectives: 136 us -> 111 us
  waiting for transfers between devices: 12.1 us -> 20.9 us
  local copies, waits for them, and re-layouts: 6.46 us -> 0.12 us
  matrix products: 9.49 us -> 3.93 us
  Pallas kernels: 0 us -> 3.54 us
    all_to_all x3 -> x1, blocking collectives: 65.4 us -> 25.9 us  [exchange_sum(): lax.all_to_all(blocks, axis, split_axis=0, concat_axis=0, tiled=True)]
    all_to_all x0 -> x1, blocking collectives: none -> 21.3 us  [on_device(): lax.all_to_all(copies, ('x', 'y'), split_axis=0, concat_axis=0, tiled=True)]
    all_to_all x1 -> x2, waiting for transfers between devices: 9.06 us -> 17.9 us  [exchange_sum(): lax.all_to_all(blocks, axis, split_axis=0, concat_axis=0, tiled=True)]
    all_gather x5 -> x3, blocking collectives: 70.7 us -> 63.5 us  [the longest x1 28.2 us: on_device(): lax.all_gather(quarter, 'za', axis=0, tiled=False)]
    dot_general x5 -> x2, matrix products: 9.49 us -> 3.93 us  [the longest x1 2.01 us: on_device(): jnp.einsum('btd,bht->dh', inputs.reshape(4, -1, features), both[:, 1], pr...]
    all_to_all x1 -> x2, starting transfers between devices: 9.31 us -> 14.7 us  [exchange_sum(): lax.all_to_all(blocks, axis, split_axis=0, concat_axis=0, tiled=True)]
    ppermute x1, starting transfers between devices: 9.98 us -> 5.26 us  [on_device(): other = lax.ppermute(own, 'core', SWAP)]
    pallas_call x0 -> x3, Pallas kernels: none -> 3.54 us  [on_core(): pl.pallas_call(kernel, out_shape=out_shape, in_specs=[VMEM] * len(operand...]
  transfers between devices with their start and end apart: 3 -> 4, of which waited for: 3 -> 4; matrix products, arithmetic and copies ran while one was open for 3% -> 2% of each run, Pallas kernels for 0% -> 0%
where the time goes in v2:
time: 170 us; the launch traced here: 168 us
  blocking collectives  111 us (65%)
  starting transfers between devices  23.5 us (14%)
  waiting for transfers between devices  20.9 us (12%)
  other arithmetic  4.49 us (3%)
  matrix products  3.93 us (2%)
  Pallas kernels  3.54 us (2%)
    all_gather x1, blocking collectives, on_device(): lax.all_gather(quarter, 'za', axis=0, tiled=False)  28.2 us
    all_to_all x1, blocking collectives, exchange_sum(): lax.all_to_all(blocks, axis, split_axis=0, concat_axis=0, tiled=True)  25.9 us
    all_to_all x1, blocking collectives, on_device(): lax.all_to_all(copies, ('x', 'y'), split_axis=0, concat_axis=0, tiled=True)  21.3 us
    all_gather x1, blocking collectives, on_device(): both = lax.all_gather(both[None], ('zb', 'zc'), axis=0, tiled=True)  18.8 us
    all_to_all x2, waiting for transfers between devices, exchange_sum(): lax.all_to_all(blocks, axis, split_axis=0, concat_axis=0, tiled=True)  17.9 us
    all_gather x1, blocking collectives, on_device(): lax.all_gather(jnp.stack([tokens, out_grad]), 'far', axis=1, tiled=True)  16.4 us
    all_to_all x2, starting transfers between devices, exchange_sum(): lax.all_to_all(blocks, axis, split_axis=0, concat_axis=0, tiled=True)  14.7 us
    ppermute x1, starting transfers between devices, on_device(): other = lax.ppermute(own, 'core', SWAP)  5.26 us
  transfers between devices with their start and end apart: 4, of which 4 were waited for; matrix products, arithmetic and copies ran while one was open for 2% of the time, Pallas kernels for 0%

profile of v2, /device:TPU:1, one launch (start us, length us, event | category | flops | bytes accessed | tf_op | source)
XLA Modules:
  0.0 167.9 jit_solution(11179190600002742320)
XLA Ops:
  0.6 0.0 copy-start
  0.6 0.0 copy-start.1
  0.7 0.9 pad_maximum_fusion.1
  1.5 16.4 %all_gather.10 = bf16[2,16,928]{2,1,0:T(8,128)(2,1)S(1)} all-gather(bf16[2,8,928]{2,1,0:T(8,128)(2,1)S(1)} %pad_maximum_fusion.1), channel_id=1, replica_groups=mesh['za'=2,'zb'=2,'zc'=2,'x'=4,'core'=2,'y'=4,'far'=2] {'far'}, dimensions={1}, use_global_device_ids=true | all-gather | bytes 89088 | tf_op jit(solution)/shard_map/gather_tokens/all_gather | solution.py:78
  17.9 0.1 broadcast_in_dim.2
  18.1 21.3 %all_to_all.20.own_ref = bf16[16,2,16,928]{3,2,1,0:T(8,128)(2,1)S(1)} all-to-all(bf16[16,2,16,928]{3,2,1,0:T(8,128)(2,1)S(1)} %broadcast_in_dim.2), channel_id=1, replica_groups=mesh['za'=2,'zb'=2,'zc'=2,'x'=4,'core'=2,'y'=4,'far'=2] {'x','y'}, dimensions={0} | all-to-all | bytes 1900544 | tf_op jit(solution)/shard_map/gather_tokens/all_to_all | solution.py:80
  39.3 5.3 %collective-permute-start = (bf16[16,2,16,928]{3,2,1,0:T(8,128)(2,1)S(1)}, bf16[16,2,16,928]{3,2,1,0:T(8,128)(2,1)S(1)}, u32[]{:S(2)}, u32[]{:S(2)}) collective-permute-start(bf16[16,2,16,928]{3,2,1,0:T(8,128)(2,1)S(1)} %all_to_all.20.own_ref), channel_id=1, source_target_pairs={{0,8},{8,0},{1,9},{9,1},{2,10},{10,2},{3,11},{11,3},{4,12},{12,4},... | collective-permute-start | bytes 2850824 | tf_op jit(solution)/shard_map/gather_tokens/ppermute | solution.py:81
  44.6 2.3 %collective-permute-done.other_ref = bf16[16,2,16,928]{3,2,1,0:T(8,128)(2,1)S(1)} collective-permute-done((bf16[16,2,16,928]{3,2,1,0:T(8,128)(2,1)S(1)}, bf16[16,2,16,928]{3,2,1,0:T(8,128)(2,1)S(1)}, u32[]{:S(2)}, u32[]{:S(2)}) %collective-permute-start) | collective-permute-done | bytes 950304 | tf_op jit(solution)/shard_map/gather_tokens/ppermute | solution.py:81
  46.9 0.0 copy-done
  46.9 0.0 copy-done.1
  46.9 2.2 %row_sum.1 = (bf16[4,2,464,128]{3,2,1,0:T(8,128)(2,1)S(1)}, bf16[512,928]{1,0:T(8,128)(2,1)S(1)}, bf16[512,928]{1,0:T(8,128)(2,1)S(1)}) custom-call(bf16[16,2,16,928]{3,2,1,0:T(8,128)(2,1)S(1)} %all_to_all.20.own_ref, bf16[16,2,16,928]{3,2,1,0:T(8,128)(2,1)S(1)} %collective-permute-done.other_ref, bf16[928,464]{1,0:T(8,128)(2,1)S(1)} %copy-done, ...), custom_call_target="tpu_custom_call" | custom-call | flops 881852416 | bytes 3622912 | tf_op jit(solution)/shard_map/row_sum/pallas_call | solution.py:26
  49.0 25.9 %all_to_all.21 = bf16[4,2,464,128]{3,2,1,0:T(8,128)(2,1)S(1)} all-to-all(bf16[4,2,464,128]{3,2,1,0:T(8,128)(2,1)S(1)} %get-tuple-element.6), channel_id=1, replica_groups=mesh['za'=2,'zb'=2,'zc'=2,'x'=4,'core'=2,'y'=4,'far'=2] {'zb','zc'}, dimensions={0} | all-to-all | bytes 1900544 | tf_op jit(solution)/shard_map/row_sum/all_to_all | solution.py:71
  74.9 0.1 add_convert_fusion.1
  75.0 28.2 %all_gather.11 = bf16[2,2,464,128]{3,2,1,0:T(8,128)(2,1)S(1)} all-gather(bf16[1,2,464,128]{3,2,1,0:T(8,128)(2,1)S(1)} %add_convert_fusion.1), channel_id=1, replica_groups=mesh['za'=2,'zb'=2,'zc'=2,'x'=4,'core'=2,'y'=4,'far'=2] {'za'}, dimensions={0}, use_global_device_ids=true | all-gather | bytes 712704 | tf_op jit(solution)/shard_map/row_sum/all_gather | solution.py:94
  103.3 0.1 fusion.6
  103.5 18.8 %all_gather.12.both_ref = bf16[4,2,464,128]{3,2,1,0:T(8,128)(2,1)S(1)} all-gather(bf16[1,2,464,128]{3,2,1,0:T(8,128)(2,1)S(1)} %pad_maximum_fusion), channel_id=1, replica_groups=mesh['za'=2,'zb'=2,'zc'=2,'x'=4,'core'=2,'y'=4,'far'=2] {'zb','zc'}, dimensions={0}, use_global_device_ids=true | all-gather | bytes 1187840 | tf_op jit(solution)/shard_map/row_gather/all_gather | solution.py:100
  122.3 0.7 token_grad.3
  123.0 3.6 %collective-permute-start.1 = (bf16[256,928]{1,0:T(8,128)(2,1)S(1)}, bf16[256,928]{1,0:T(8,128)(2,1)S(1)}, u32[]{:S(2)}, u32[]{:S(2)}) collective-permute-start(bf16[256,928]{1,0:T(8,128)(2,1)S(1)} %token_grad.3), channel_id=1, source_target_pairs={{0,8},{8,0},{1,9},{9,1},{2,10},{10,2},{3,11},{11,3},{4,12},{12,4},... | collective-permute-start | bytes 1425416 | tf_op jit(solution)/shard_map/token_grad/ppermute | solution.py:108
  126.6 0.7 token_grad.2
  127.3 0.8 collective-permute-done.1
  128.1 1.0 add_convert_fusion
  129.1 4.2 %all-to-all-start.2 = ((bf16[16,16,928]{2,1,0:T(8,128)(2,1)}), bf16[16,16,928]{2,1,0:T(8,128)(2,1)}, u32[]{:S(2)}, u32[]{:S(2)}) async-start(bf16[16,16,928]{2,1,0:T(8,128)(2,1)} %bitcast.58), calls=%async_computation.2 | async-start | bytes 1048576 | tf_op jit(solution)/shard_map/token_grad/all_to_all | solution.py:71
  133.4 2.0 %convolution_bitcast_fusion.1 = f32[928,464]{1,0:T(8,128)} fusion(bf16[4,128,928]{2,1,0:T(8,128)(2,1)S(1)} %bitcast.57, bf16[4,2,464,128]{3,2,1,0:T(8,128)(2,1)S(1)} %all_gather.12.both_ref), kind=kOutput, calls=%fused_computation.1 | convolution fusion | flops 440926208 | bytes 3246080 | tf_op jit(solution)/shard_map/weight_grads/btd,bht->dh/dot_general | solution.py:117
  135.4 8.2 %all-to-all-done.2 = bf16[16,16,928]{2,1,0:T(8,128)(2,1)} async-done(((bf16[16,16,928]{2,1,0:T(8,128)(2,1)}), bf16[16,16,928]{2,1,0:T(8,128)(2,1)}, u32[]{:S(2)}, u32[]{:S(2)}) %all-to-all-start.2) | async-done | bytes 475168 | tf_op jit(solution)/shard_map/token_grad/all_to_all | solution.py:71
  143.6 1.7 %fusion.8 = bf16[2,8,928]{2,1,0:T(8,128)(2,1)} fusion(bf16[16,16,928]{2,1,0:T(8,128)(2,1)} %all-to-all-done.2), kind=kLoop, calls=%fused_computation.22 | loop fusion | flops 475136 | bytes 504832 | tf_op jit(solution)/shard_map/token_grad/convert_element_type | solution.py:114
  145.3 10.4 %all-to-all-start.3 = ((bf16[2,8,928]{2,1,0:T(8,128)(2,1)}), bf16[2,8,928]{2,1,0:T(8,128)(2,1)S(1)}, u32[]{:S(2)}, u32[]{:S(2)}) async-start(bf16[2,8,928]{2,1,0:T(8,128)(2,1)} %fusion.8), calls=%async_computation.3 | async-start | bytes 65536 | tf_op jit(solution)/shard_map/token_grad/all_to_all | solution.py:71
  155.8 1.9 %convolution_bitcast_fusion = f32[464,928]{1,0:T(8,128)} fusion(bf16[4,128,928]{2,1,0:T(8,128)(2,1)S(1)} %bitcast.56, bf16[4,2,464,128]{3,2,1,0:T(8,128)(2,1)S(1)} %all_gather.12.both_ref), kind=kOutput, calls=%fused_computation | convolution fusion | flops 440926208 | bytes 3246080 | tf_op jit(solution)/shard_map/weight_grads/bht,btd->hd/dot_general | solution.py:123
  157.7 9.6 %all-to-all-done.3 = bf16[2,8,928]{2,1,0:T(8,128)(2,1)S(1)} async-done(((bf16[2,8,928]{2,1,0:T(8,128)(2,1)}), bf16[2,8,928]{2,1,0:T(8,128)(2,1)S(1)}, u32[]{:S(2)}, u32[]{:S(2)}) %all-to-all-start.3) | async-done | bytes 29728 | tf_op jit(solution)/shard_map/token_grad/all_to_all | solution.py:71
  167.3 0.6 fusion.9
  (2 shorter events, 0.1 us)
Async XLA Ops:
  0.6 46.2 %copy-start = (bf16[928,464]{1,0:T(8,128)(2,1)S(1)}, bf16[928,464]{1,0:T(8,128)(2,1)}, u32[]{:S(2)}) copy-start(bf16[928,464]{1,0:T(8,128)(2,1)} %up_ref.5) | copy-start | bytes 2583556
  0.6 46.2 %copy-start.1 = (bf16[464,928]{1,0:T(8,128)(2,1)S(1)}, bf16[464,928]{1,0:T(8,128)(2,1)}, u32[]{:S(2)}) copy-start(bf16[464,928]{1,0:T(8,128)(2,1)} %down_ref.1) | copy-start | bytes 2583556
  39.3 7.5 %collective-permute-start = (bf16[16,2,16,928]{3,2,1,0:T(8,128)(2,1)S(1)}, bf16[16,2,16,928]{3,2,1,0:T(8,128)(2,1)S(1)}, u32[]{:S(2)}, u32[]{:S(2)}) collective-permute-start(bf16[16,2,16,928]{3,2,1,0:T(8,128)(2,1)S(1)} %all_to_all.20.own_ref), channel_id=1, source_target_pairs={{0,8},{8,0},{1,9},{9,1},{2,10},{10,2},{3,11},{11,3},{4,12},{12,4},... | collective-permute-start | bytes 2850824 | tf_op jit(solution)/shard_map/gather_tokens/ppermute | solution.py:81
  123.0 5.1 %collective-permute-start.1 = (bf16[256,928]{1,0:T(8,128)(2,1)S(1)}, bf16[256,928]{1,0:T(8,128)(2,1)S(1)}, u32[]{:S(2)}, u32[]{:S(2)}) collective-permute-start(bf16[256,928]{1,0:T(8,128)(2,1)S(1)} %token_grad.3), channel_id=1, source_target_pairs={{0,8},{8,0},{1,9},{9,1},{2,10},{10,2},{3,11},{11,3},{4,12},{12,4},... | collective-permute-start | bytes 1425416 | tf_op jit(solution)/shard_map/token_grad/ppermute | solution.py:108
  129.1 14.5 %all-to-all-start.2 = ((bf16[16,16,928]{2,1,0:T(8,128)(2,1)}), bf16[16,16,928]{2,1,0:T(8,128)(2,1)}, u32[]{:S(2)}, u32[]{:S(2)}) async-start(bf16[16,16,928]{2,1,0:T(8,128)(2,1)} %bitcast.58), calls=%async_computation.2 | async-start | bytes 1048576 | tf_op jit(solution)/shard_map/token_grad/all_to_all | solution.py:71
  145.3 22.0 %all-to-all-start.3 = ((bf16[2,8,928]{2,1,0:T(8,128)(2,1)}), bf16[2,8,928]{2,1,0:T(8,128)(2,1)S(1)}, u32[]{:S(2)}, u32[]{:S(2)}) async-start(bf16[2,8,928]{2,1,0:T(8,128)(2,1)} %fusion.8), calls=%async_computation.3 | async-start | bytes 65536 | tf_op jit(solution)/shard_map/token_grad/all_to_all | solution.py:71

commit v3 on v2

v3 whole, which is shorter than its diff:
```python
import functools

import jax
import jax.numpy as jnp
from jax import lax
from jax.experimental import pallas as pl
from jax.experimental.pallas import tpu as pltpu
from jax.sharding import Mesh, PartitionSpec as P

AXES = ("za", "zb", "zc", "x", "core", "y", "far")
SIZES = (2, 2, 2, 4, 2, 4, 2)
ROW = ("za", "zb", "zc")
TOKENS_OVER = ("x", "core", "y", "far")
SWAP = [(0, 1), (1, 0)]


def gelu_cdf(preact):
    return 0.5 * (1.0 + lax.erf(preact * 0.7071067811865476))


VMEM = pl.BlockSpec(memory_space=pltpu.VMEM)
ANY = pl.BlockSpec(memory_space=pl.ANY)
PARAMS = pltpu.CompilerParams(vmem_limit_bytes=24 << 20)


def on_core(kernel, out_shape, *operands):
    return pl.pallas_call(
        kernel,
        out_shape=out_shape,
        in_specs=[VMEM] * len(operands),
        out_specs=VMEM,
        compiler_params=PARAMS,
    )(*operands)


def in_order(kernel, out_shape, *operands, held_in=None):
    n = len(operands)
    later = operands[-1]
    passed = jax.ShapeDtypeStruct(later.shape, later.dtype)
    if held_in is not None:
        later = pltpu.with_memory_space_constraint(later, held_in)
        passed = held_in(passed.shape, passed.dtype)
    return pl.pallas_call(
        kernel,
        out_shape=[out_shape, passed],
        in_specs=[VMEM] * (n - 1) + [ANY],
        out_specs=[VMEM, ANY],
        input_output_aliases={n - 1: 1},
        compiler_params=PARAMS,
    )(*operands[:-1], later)


def total_then_kernel(blocks_ref, later_ref, out_ref, later_out_ref):
    total_kernel(blocks_ref, out_ref)


def partials_kernel(array, own_ref, other_ref, weight_ref, parts_ref, rows_ref):
    step = pl.program_id(0)

    def product(ref):
        rows = ref[pl.ds(8 * (step % 2), 8), array].reshape(128, -1)
        rows_ref[...] = rows
        parts_ref[0] = lax.dot_general(
            weight_ref[...],
            rows,
            (((array,), (1,)), ((), ())),
            preferred_element_type=jnp.float32,
        ).astype(jnp.bfloat16)

    @pl.when(step < 2)
    def _():
        product(own_ref)

    @pl.when(step >= 2)
    def _():
        product(other_ref)


def partials(array, own, other, weight):
    features = own.shape[3]
    hidden = weight.shape[1 - array]
    return pl.pallas_call(
        functools.partial(partials_kernel, array),
        grid=(4,),
        out_shape=[
            pltpu.HBM((4, hidden, 128), jnp.bfloat16),
            pltpu.HBM((512, features), jnp.bfloat16),
        ],
        in_specs=[VMEM, VMEM, VMEM],
        out_specs=[
            pl.BlockSpec((1, hidden, 128), lambda i: (i, 0, 0)),
            pl.BlockSpec((128, features), lambda i: (i, 0)),
        ],
        compiler_params=PARAMS,
    )(own, other, weight)


def token_grad_kernel(first, hidden_grad_ref, up_ref, out_ref):
    for piece in range(2):
        out_ref[pl.ds(128 * piece, 128)] = lax.dot_general(
            hidden_grad_ref[first + piece],
            up_ref[...],
            (((0,), (1,)), ((), ())),
            preferred_element_type=jnp.float32,
        ).astype(jnp.bfloat16)


def total_kernel(blocks_ref, out_ref):
    acc = blocks_ref[0].astype(jnp.float32)
    for i in range(1, blocks_ref.shape[0]):
        acc = acc + blocks_ref[i].astype(jnp.float32)
    out_ref[...] = acc.astype(jnp.bfloat16)


def add_kernel(*refs):
    acc = refs[0][...].astype(jnp.float32)
    for ref in refs[1:-1]:
        acc = acc + ref[...].astype(jnp.float32)
    refs[-1][...] = acc.astype(jnp.bfloat16)


def hidden_grad_kernel(mine_ref, theirs_ref, slope_ref, active_ref, out_ref, active_out_ref):
    grad_active = mine_ref[...].astype(jnp.float32) + theirs_ref[...].astype(jnp.float32)
    out_ref[...] = (grad_active * slope_ref[...]).astype(jnp.bfloat16)


def on_device(tokens, out_grad, up_weight, down_weight):
    rows, features = tokens.shape
    hidden = up_weight.shape[1]

    def exchange(blocks, axis):
        return lax.all_to_all(blocks, axis, split_axis=0, concat_axis=0, tiled=True)

    def row_gather(part):
        return lax.all_gather(part[None], ("zb", "zc"), axis=0, tiled=True)

    quarter = jax.ShapeDtypeStruct((hidden, 128), jnp.bfloat16)
    with jax.named_scope("gather_tokens"):
        pair = lax.all_gather(jnp.stack([tokens, out_grad]), "far", axis=1, tiled=True)
        copies = jnp.broadcast_to(pair[None], (16,) + pair.shape)
        own = exchange(copies, ("x", "y"))
        other = lax.ppermute(own, "core", SWAP)
    with jax.named_scope("row_sums"):
        pre_parts, inputs = partials(0, own, other, up_weight)
        grad_parts, upstream = partials(1, own, other, down_weight)
        pre_mine, grad_parts = in_order(
            total_then_kernel,
            quarter,
            exchange(pre_parts, ("zb", "zc")),
            grad_parts,
            held_in=pltpu.HBM,
        )
        pre_theirs = lax.ppermute(pre_mine, "za", SWAP)
        grad_mine = on_core(total_kernel, quarter, exchange(grad_parts, ("zb", "zc")))
        grad_theirs = lax.ppermute(grad_mine, "za", SWAP)
    with jax.named_scope("activate"):
        preact = pre_mine.astype(jnp.float32) + pre_theirs.astype(jnp.float32)
        cdf = 0.5 * (1.0 + lax.erf(preact * 0.7071067811865476))
        slope = cdf + preact * jnp.exp(-0.5 * preact * preact) * 0.3989422804014327
        active = row_gather((preact * cdf).astype(jnp.bfloat16))
        hidden_grad, active = in_order(
            hidden_grad_kernel, quarter, grad_mine, grad_theirs, slope, active
        )
        hidden_grad = row_gather(hidden_grad)
    with jax.named_scope("token_grad"):
        half = jax.ShapeDtypeStruct((256, features), jnp.bfloat16)
        leaving, staying = (
            on_core(functools.partial(token_grad_kernel, first), half, hidden_grad, up_weight)
            for first in (2, 0)
        )
        arrived = lax.ppermute(leaving, "core", SWAP)
        chip_sum = on_core(add_kernel, half, staying, arrived)
        plane_sum = on_core(
            total_kernel,
            jax.ShapeDtypeStruct((2 * rows, features), jnp.bfloat16),
            exchange(chip_sum.reshape(16, -1, features), ("x", "y")),
        )
        both_sums = lax.all_gather(plane_sum, "far", axis=0, tiled=False)
        own_rows = lax.dynamic_slice_in_dim(
            both_sums, rows * lax.axis_index("far"), rows, axis=1
        ).astype(jnp.float32)
        token_grad = own_rows[0] + own_rows[1]
    with jax.named_scope("weight_grads"):
        up_grad = jnp.einsum(
            "btd,bht->dh",
            inputs.reshape(4, -1, features),
            hidden_grad,
            preferred_element_type=jnp.float32,
        )
        down_grad = jnp.einsum(
            "bht,btd->hd",
            active,
            upstream.reshape(4, -1, features),
            preferred_element_type=jnp.float32,
        )
    return (token_grad.astype(jnp.bfloat16), up_grad, down_grad)


def solution(mesh):
    fine = Mesh(mesh.devices.reshape(SIZES), AXES)
    return jax.shard_map(
        on_device,
        mesh=fine,
        in_specs=(P(TOKENS_OVER, ROW), P(TOKENS_OVER, ROW), P(ROW, TOKENS_OVER), P(TOKENS_OVER, ROW)),
        out_specs=(P(TOKENS_OVER, ROW), P(ROW, TOKENS_OVER), P(TOKENS_OVER, ROW)),
        check_vma=False,
    )
```

time: 170 us -> 163 us (0.959)
  blocking collectives: 111 us -> 79.8 us
  starting transfers between devices: 23.5 us -> 37.9 us
  waiting for transfers between devices: 20.9 us -> 27.8 us
  Pallas kernels: 3.54 us -> 8.35 us
  other arithmetic: 4.49 us -> 1.57 us
    all_to_all x2 -> x1, blocking collectives: 47.1 us -> 21.3 us  [exchange(): return lax.all_to_all(blocks, axis, split_axis=0, concat_axis=0, tiled=True)]
    ppermute x0 -> x2, starting transfers between devices: none -> 13.7 us  [the longest x1 7.7 us: on_device(): pre_theirs = lax.ppermute(pre_mine, 'za', SWAP)]
    pallas_call x0 -> x4, Pallas kernels: none -> 5.87 us  [the longest x2 5.77 us: partials(): pl.pallas_call(functools.partial(partials_kernel, array), grid=(4,), out_...]
    all_gather x2 -> x3, blocking collectives: 47.1 us -> 42.1 us  [the longest x2 30 us: row_gather(): return lax.all_gather(part[None], ('zb', 'zc'), axis=0, tiled=True)]
    ppermute x1, starting transfers between devices: 3.57 us -> 8.38 us  [on_device(): arrived = lax.ppermute(leaving, 'core', SWAP)]
    all_to_all x2 -> x3, waiting for transfers between devices: 17.9 us -> 22.2 us  [exchange(): return lax.all_to_all(blocks, axis, split_axis=0, concat_axis=0, tiled=True)]
    all_to_all x2 -> x3, starting transfers between devices: 14.7 us -> 10.5 us  [exchange(): return lax.all_to_all(blocks, axis, split_axis=0, concat_axis=0, tiled=True)]
    convert_element_type x3 -> x2, other arithmetic: 2.8 us -> 0.14 us  [the longest x1 0.13 us: on_device(): active = row_gather((preact * cdf).astype(jnp.bfloat16))]
  transfers between devices with their start and end apart: 4 -> 7, of which waited for: 4 -> 6; matrix products, arithmetic and copies ran while one was open for 2% -> 3% of each run, Pallas kernels for 0% -> 2%
where the time goes in v3:
time: 163 us; the launch traced here: 161 us
  blocking collectives  79.8 us (49%)
  starting transfers between devices  37.9 us (23%)
  waiting for transfers between devices  27.8 us (17%)
  Pallas kernels  8.35 us (5%)
  matrix products  3.93 us (2%)
    all_gather x2, blocking collectives, row_gather(): return lax.all_gather(part[None], ('zb', 'zc'), axis=0, tiled=True)  30 us
    all_to_all x3, waiting for transfers between devices, exchange(): return lax.all_to_all(blocks, axis, split_axis=0, concat_axis=0, tiled=True)  22.2 us
    all_to_all x1, blocking collectives, exchange(): return lax.all_to_all(blocks, axis, split_axis=0, concat_axis=0, tiled=True)  21.3 us
    all_gather x1, blocking collectives, on_device(): lax.all_gather(jnp.stack([tokens, out_grad]), 'far', axis=1, tiled=True)  16.4 us
    all_gather x1, blocking collectives, on_device(): both_sums = lax.all_gather(plane_sum, 'far', axis=0, tiled=False)  12.2 us
    all_to_all x3, starting transfers between devices, exchange(): return lax.all_to_all(blocks, axis, split_axis=0, concat_axis=0, tiled=True)  10.5 us
    ppermute x1, starting transfers between devices, on_device(): arrived = lax.ppermute(leaving, 'core', SWAP)  8.38 us
    ppermute x1, starting transfers between devices, on_device(): pre_theirs = lax.ppermute(pre_mine, 'za', SWAP)  7.7 us
  transfers between devices with their start and end apart: 7, of which 6 were waited for; matrix products, arithmetic and copies ran while one was open for 3% of the time, Pallas kernels for 2%

profile of v3, /device:TPU:1, one launch (start us, length us, event | category | flops | bytes accessed | tf_op | source)
XLA Modules:
  0.0 161.4 jit_solution(14257656752689381423)
XLA Ops:
  0.6 0.0 copy-start
  0.6 0.8 pad_maximum_fusion
  1.5 16.4 %all_gather.15 = bf16[2,16,928]{2,1,0:T(8,128)(2,1)S(1)} all-gather(bf16[2,8,928]{2,1,0:T(8,128)(2,1)S(1)} %pad_maximum_fusion), channel_id=1, replica_groups=mesh['za'=2,'zb'=2,'zc'=2,'x'=4,'core'=2,'y'=4,'far'=2] {'far'}, dimensions={1}, use_global_device_ids=true | all-gather | bytes 89088 | tf_op jit(solution)/shard_map/gather_tokens/all_gather | solution.py:139
  17.9 0.1 broadcast_in_dim.12
  18.0 21.3 %all_to_all.20.own_ref = bf16[16,2,16,928]{3,2,1,0:T(8,128)(2,1)S(1)} all-to-all(bf16[16,2,16,928]{3,2,1,0:T(8,128)(2,1)S(1)} %broadcast_in_dim.12), channel_id=1, replica_groups=mesh['za'=2,'zb'=2,'zc'=2,'x'=4,'core'=2,'y'=4,'far'=2] {'x','y'}, dimensions={0} | all-to-all | bytes 1900544 | tf_op jit(solution)/shard_map/gather_tokens/all_to_all | solution.py:132
  39.3 5.3 %collective-permute-start = (bf16[16,2,16,928]{3,2,1,0:T(8,128)(2,1)S(1)}, bf16[16,2,16,928]{3,2,1,0:T(8,128)(2,1)S(1)}, u32[]{:S(2)}, u32[]{:S(2)}) collective-permute-start(bf16[16,2,16,928]{3,2,1,0:T(8,128)(2,1)S(1)} %all_to_all.20.own_ref), channel_id=1, source_target_pairs={{0,8},{8,0},{1,9},{9,1},{2,10},{10,2},{3,11},{11,3},{4,12},{12,4},... | collective-permute-start | bytes 2850824 | tf_op jit(solution)/shard_map/gather_tokens/ppermute | solution.py:142
  44.5 2.3 %collective-permute-done.other_ref = bf16[16,2,16,928]{3,2,1,0:T(8,128)(2,1)S(1)} collective-permute-done((bf16[16,2,16,928]{3,2,1,0:T(8,128)(2,1)S(1)}, bf16[16,2,16,928]{3,2,1,0:T(8,128)(2,1)S(1)}, u32[]{:S(2)}, u32[]{:S(2)}) %collective-permute-start) | collective-permute-done | bytes 950304 | tf_op jit(solution)/shard_map/gather_tokens/ppermute | solution.py:142
  46.8 0.0 copy-done
  46.8 3.0 %row_sums.4 = (bf16[4,464,128]{2,1,0:T(8,128)(2,1)}, bf16[512,928]{1,0:T(8,128)(2,1)}) custom-call(bf16[16,2,16,928]{3,2,1,0:T(8,128)(2,1)S(1)} %all_to_all.20.own_ref, bf16[16,2,16,928]{3,2,1,0:T(8,128)(2,1)S(1)} %collective-permute-done.other_ref, bf16[928,464]{1,0:T(8,128)(2,1)S(1)} %copy-done), custom_call_target="tpu_custom_call" | custom-call | tf_op jit(solution)/shard_map/row_sums/pallas_call | solution.py:82
  49.8 3.5 %all-to-all-start.1 = ((bf16[4,464,128]{2,1,0:T(8,128)(2,1)}), bf16[4,464,128]{2,1,0:T(8,128)(2,1)S(1)}, u32[]{:S(2)}, u32[]{:S(2)}) async-start(bf16[4,464,128]{2,1,0:T(8,128)(2,1)} %get-tuple-element.11), calls=%async_computation.1 | async-start | bytes 950272 | tf_op jit(solution)/shard_map/row_sums/all_to_all | solution.py:132
  53.3 0.0 copy-start.1
  53.3 1.2 copy-done.1
  54.5 2.8 %row_sums.5 = (bf16[4,464,128]{2,1,0:T(8,128)(2,1)}, bf16[512,928]{1,0:T(8,128)(2,1)}) custom-call(bf16[16,2,16,928]{3,2,1,0:T(8,128)(2,1)S(1)} %all_to_all.20.own_ref, bf16[16,2,16,928]{3,2,1,0:T(8,128)(2,1)S(1)} %collective-permute-done.other_ref, bf16[464,928]{1,0:T(8,128)(2,1)S(1)} %copy-done.1), custom_call_target="tpu_custom_call" | custom-call | tf_op jit(solution)/shard_map/row_sums/pallas_call | solution.py:82
  57.2 9.2 %all-to-all-done.1.blocks_ref = bf16[4,464,128]{2,1,0:T(8,128)(2,1)S(1)} async-done(((bf16[4,464,128]{2,1,0:T(8,128)(2,1)}), bf16[4,464,128]{2,1,0:T(8,128)(2,1)S(1)}, u32[]{:S(2)}, u32[]{:S(2)}) %all-to-all-start.1) | async-done | bytes 475168 | tf_op jit(solution)/shard_map/row_sums/all_to_all | solution.py:132
  66.4 0.1 row_sums.6
  66.5 3.5 %all-to-all-start.2 = ((bf16[4,464,128]{2,1,0:T(8,128)(2,1)}), bf16[4,464,128]{2,1,0:T(8,128)(2,1)S(1)}, u32[]{:S(2)}, u32[]{:S(2)}) async-start(bf16[4,464,128]{2,1,0:T(8,128)(2,1)} %get-tuple-element.13), calls=%async_computation.2 | async-start | bytes 950272 | tf_op jit(solution)/shard_map/row_sums/all_to_all | solution.py:132
  70.0 7.7 %collective-permute-start.2 = (bf16[464,128]{1,0:T(8,128)(2,1)S(1)}, bf16[464,128]{1,0:T(8,128)(2,1)S(1)}, u32[]{:S(2)}, u32[]{:S(2)}) collective-permute-start(bf16[464,128]{1,0:T(8,128)(2,1)S(1)} %get-tuple-element.14), channel_id=1, source_target_pairs={{0,256},{256,0},{1,257},{257,1},{2,258},{258,2},{3,259},{259,3},{4... | collective-permute-start | bytes 356360 | tf_op jit(solution)/shard_map/row_sums/ppermute | solution.py:153
  77.7 2.5 %collective-permute-done.2 = bf16[464,128]{1,0:T(8,128)(2,1)S(1)} collective-permute-done((bf16[464,128]{1,0:T(8,128)(2,1)S(1)}, bf16[464,128]{1,0:T(8,128)(2,1)S(1)}, u32[]{:S(2)}, u32[]{:S(2)}) %collective-permute-start.2) | collective-permute-done | bytes 118816 | tf_op jit(solution)/shard_map/row_sums/ppermute | solution.py:153
  80.2 0.1 multiply_convert_fusion
  80.3 6.8 %all-to-all-done.2.blocks_ref = bf16[4,464,128]{2,1,0:T(8,128)(2,1)S(1)} async-done(((bf16[4,464,128]{2,1,0:T(8,128)(2,1)}), bf16[4,464,128]{2,1,0:T(8,128)(2,1)S(1)}, u32[]{:S(2)}, u32[]{:S(2)}) %all-to-all-start.2) | async-done | bytes 475168 | tf_op jit(solution)/shard_map/row_sums/all_to_all | solution.py:132
  87.1 0.1 row_sums.7.mine_ref
  87.2 6.0 %collective-permute-start.1 = (bf16[464,128]{1,0:T(8,128)(2,1)S(1)}, bf16[464,128]{1,0:T(8,128)(2,1)S(1)}, u32[]{:S(2)}, u32[]{:S(2)}) collective-permute-start(bf16[464,128]{1,0:T(8,128)(2,1)S(1)} %row_sums.7.mine_ref), channel_id=1, source_target_pairs={{0,256},{256,0},{1,257},{257,1},{2,258},{258,2},{3,259},{259,3},{4... | collective-permute-start | bytes 356360 | tf_op jit(solution)/shard_map/row_sums/ppermute | solution.py:155
  93.2 18.2 %all-gather = bf16[1856,128]{1,0:T(8,128)(2,1)S(1)} all-gather(bf16[464,128]{1,0:T(8,128)(2,1)S(1)} %get-tuple-element.19), channel_id=2, replica_groups=mesh['za'=2,'zb'=2,'zc'=2,'x'=4,'core'=2,'y'=4,'far'=2] {'zb','zc'}, dimensions={0}, use_global_device_ids=true | all-gather | bytes 593920 | tf_op jit(solution)/shard_map/activate/all_gather | solution.py:135
  111.4 0.0 collective-permute-done.1.theirs_ref
  111.4 11.8 %all-gather.1 = bf16[1856,128]{1,0:T(8,128)(2,1)S(1)} all-gather(bf16[464,128]{1,0:T(8,128)(2,1)S(1)} %get-tuple-element.15), channel_id=3, replica_groups=mesh['za'=2,'zb'=2,'zc'=2,'x'=4,'core'=2,'y'=4,'far'=2] {'zb','zc'}, dimensions={0}, use_global_device_ids=true | all-gather | bytes 593920 | tf_op jit(solution)/shard_map/activate/all_gather | solution.py:135
  123.2 0.7 token_grad.5
  123.9 0.0 copy-start.2
  123.9 8.4 %collective-permute-start.3 = (bf16[256,928]{1,0:T(8,128)(2,1)S(1)}, bf16[256,928]{1,0:T(8,128)(2,1)S(1)}, u32[]{:S(2)}, u32[]{:S(2)}) collective-permute-start(bf16[256,928]{1,0:T(8,128)(2,1)S(1)} %token_grad.5), channel_id=1, source_target_pairs={{0,8},{8,0},{1,9},{9,1},{2,10},{10,2},{3,11},{11,3},{4,12},{12,4},... | collective-permute-start | bytes 1425416 | tf_op jit(solution)/shard_map/token_grad/ppermute | solution.py:171
  132.3 0.7 token_grad.4.refs_0_
  133.0 0.8 collective-permute-done.3.refs_1_
  133.8 0.9 token_grad.6
  134.8 3.6 %all-to-all-start.3 = ((bf16[16,16,928]{2,1,0:T(8,128)(2,1)}), bf16[16,16,928]{2,1,0:T(8,128)(2,1)S(1)}, u32[]{:S(2)}, u32[]{:S(2)}) async-start(bf16[16,16,928]{2,1,0:T(8,128)(2,1)} %bitcast.4), calls=%async_computation.3 | async-start | bytes 1048576 | tf_op jit(solution)/shard_map/token_grad/all_to_all | solution.py:132
  138.3 0.0 copy-start.3
  138.3 0.0 copy-done.2
  138.4 2.0 %convolution_bitcast_fusion.1 = f32[928,464]{1,0:T(8,128)} fusion(bf16[4,128,928]{2,1,0:T(8,128)(2,1)S(1)} %bitcast.22, bf16[4,464,128]{2,1,0:T(8,128)(2,1)S(1)} %bitcast.20), kind=kOutput, calls=%fused_computation.1 | convolution fusion | flops 440926208 | bytes 3147776 | tf_op jit(solution)/shard_map/weight_grads/btd,bht->dh/dot_general | solution.py:184
  140.4 0.0 copy-done.3
  140.4 1.9 %convolution_bitcast_fusion = f32[464,928]{1,0:T(8,128)} fusion(bf16[4,464,128]{2,1,0:T(8,128)(2,1)S(1)} %get-tuple-element.17, bf16[4,128,928]{2,1,0:T(8,128)(2,1)S(1)} %bitcast.23), kind=kOutput, calls=%fused_computation | convolution fusion | flops 440926208 | bytes 3147776 | tf_op jit(solution)/shard_map/weight_grads/bht,btd->hd/dot_general | solution.py:190
  142.3 6.3 %all-to-all-done.3.blocks_ref = bf16[16,16,928]{2,1,0:T(8,128)(2,1)S(1)} async-done(((bf16[16,16,928]{2,1,0:T(8,128)(2,1)}), bf16[16,16,928]{2,1,0:T(8,128)(2,1)S(1)}, u32[]{:S(2)}, u32[]{:S(2)}) %all-to-all-start.3) | async-done | bytes 475168 | tf_op jit(solution)/shard_map/token_grad/all_to_all | solution.py:132
  148.6 0.1 token_grad.7
  148.6 12.2 %all-gather.2 = bf16[32,928]{1,0:T(8,128)(2,1)S(1)} all-gather(bf16[16,928]{1,0:T(8,128)(2,1)S(1)} %token_grad.7), channel_id=4, replica_groups=mesh['za'=2,'zb'=2,'zc'=2,'x'=4,'core'=2,'y'=4,'far'=2] {'far'}, dimensions={0}, use_global_device_ids=true | all-gather | bytes 89088 | tf_op jit(solution)/shard_map/token_grad/all_gather | solution.py:178
  160.8 0.6 fusion.5
  (2 shorter events, 0.1 us)
Async XLA Ops:
  0.6 46.2 %copy-start = (bf16[928,464]{1,0:T(8,128)(2,1)S(1)}, bf16[928,464]{1,0:T(8,128)(2,1)}, u32[]{:S(2)}) copy-start(bf16[928,464]{1,0:T(8,128)(2,1)} %up_ref.3) | copy-start | bytes 2583556
  39.3 7.5 %collective-permute-start = (bf16[16,2,16,928]{3,2,1,0:T(8,128)(2,1)S(1)}, bf16[16,2,16,928]{3,2,1,0:T(8,128)(2,1)S(1)}, u32[]{:S(2)}, u32[]{:S(2)}) collective-permute-start(bf16[16,2,16,928]{3,2,1,0:T(8,128)(2,1)S(1)} %all_to_all.20.own_ref), channel_id=1, source_target_pairs={{0,8},{8,0},{1,9},{9,1},{2,10},{10,2},{3,11},{11,3},{4,12},{12,4},... | collective-permute-start | bytes 2850824 | tf_op jit(solution)/shard_map/gather_tokens/ppermute | solution.py:142
  49.8 16.6 %all-to-all-start.1 = ((bf16[4,464,128]{2,1,0:T(8,128)(2,1)}), bf16[4,464,128]{2,1,0:T(8,128)(2,1)S(1)}, u32[]{:S(2)}, u32[]{:S(2)}) async-start(bf16[4,464,128]{2,1,0:T(8,128)(2,1)} %get-tuple-element.11), calls=%async_computation.1 | async-start | bytes 950272 | tf_op jit(solution)/shard_map/row_sums/all_to_all | solution.py:132
  53.3 1.2 copy-start.1
  66.5 20.6 %all-to-all-start.2 = ((bf16[4,464,128]{2,1,0:T(8,128)(2,1)}), bf16[4,464,128]{2,1,0:T(8,128)(2,1)S(1)}, u32[]{:S(2)}, u32[]{:S(2)}) async-start(bf16[4,464,128]{2,1,0:T(8,128)(2,1)} %get-tuple-element.13), calls=%async_computation.2 | async-start | bytes 950272 | tf_op jit(solution)/shard_map/row_sums/all_to_all | solution.py:132
  70.0 10.2 %collective-permute-start.2 = (bf16[464,128]{1,0:T(8,128)(2,1)S(1)}, bf16[464,128]{1,0:T(8,128)(2,1)S(1)}, u32[]{:S(2)}, u32[]{:S(2)}) collective-permute-start(bf16[464,128]{1,0:T(8,128)(2,1)S(1)} %get-tuple-element.14), channel_id=1, source_target_pairs={{0,256},{256,0},{1,257},{257,1},{2,258},{258,2},{3,259},{259,3},{4... | collective-permute-start | bytes 356360 | tf_op jit(solution)/shard_map/row_sums/ppermute | solution.py:153
  87.2 24.2 %collective-permute-start.1 = (bf16[464,128]{1,0:T(8,128)(2,1)S(1)}, bf16[464,128]{1,0:T(8,128)(2,1)S(1)}, u32[]{:S(2)}, u32[]{:S(2)}) collective-permute-start(bf16[464,128]{1,0:T(8,128)(2,1)S(1)} %row_sums.7.mine_ref), channel_id=1, source_target_pairs={{0,256},{256,0},{1,257},{257,1},{2,258},{258,2},{3,259},{259,3},{4... | collective-permute-start | bytes 356360 | tf_op jit(solution)/shard_map/row_sums/ppermute | solution.py:155
  123.9 14.5 %copy-start.2 = (bf16[512,928]{1,0:T(8,128)(2,1)S(1)}, bf16[512,928]{1,0:T(8,128)(2,1)}, u32[]{:S(2)}) copy-start(bf16[512,928]{1,0:T(8,128)(2,1)} %get-tuple-element.16) | copy-start | bytes 2850820
  123.9 9.9 %collective-permute-start.3 = (bf16[256,928]{1,0:T(8,128)(2,1)S(1)}, bf16[256,928]{1,0:T(8,128)(2,1)S(1)}, u32[]{:S(2)}, u32[]{:S(2)}) collective-permute-start(bf16[256,928]{1,0:T(8,128)(2,1)S(1)} %token_grad.5), channel_id=1, source_target_pairs={{0,8},{8,0},{1,9},{9,1},{2,10},{10,2},{3,11},{11,3},{4,12},{12,4},... | collective-permute-start | bytes 1425416 | tf_op jit(solution)/shard_map/token_grad/ppermute | solution.py:171
  134.8 13.8 %all-to-all-start.3 = ((bf16[16,16,928]{2,1,0:T(8,128)(2,1)}), bf16[16,16,928]{2,1,0:T(8,128)(2,1)S(1)}, u32[]{:S(2)}, u32[]{:S(2)}) async-start(bf16[16,16,928]{2,1,0:T(8,128)(2,1)} %bitcast.4), calls=%async_computation.3 | async-start | bytes 1048576 | tf_op jit(solution)/shard_map/token_grad/all_to_all | solution.py:132
  138.3 2.0 %copy-start.3 = (bf16[512,928]{1,0:T(8,128)(2,1)S(1)}, bf16[512,928]{1,0:T(8,128)(2,1)}, u32[]{:S(2)}) copy-start(bf16[512,928]{1,0:T(8,128)(2,1)} %get-tuple-element.18) | copy-start | bytes 2850820

commit v4 on v3

v4 whole, which is shorter than its diff:
```python
import functools

import jax
import jax.numpy as jnp
from jax import lax
from jax.experimental import pallas as pl
from jax.experimental.pallas import tpu as pltpu
from jax.sharding import Mesh, PartitionSpec as P

AXES = ("za", "zb", "zc", "x", "core", "y", "far")
SIZES = (2, 2, 2, 4, 2, 4, 2)
ROW = ("za", "zb", "zc")
TOKENS_OVER = ("x", "core", "y", "far")
SWAP = [(0, 1), (1, 0)]


def gelu_cdf(preact):
    return 0.5 * (1.0 + lax.erf(preact * 0.7071067811865476))


VMEM = pl.BlockSpec(memory_space=pltpu.VMEM)
ANY = pl.BlockSpec(memory_space=pl.ANY)
PARAMS = pltpu.CompilerParams(vmem_limit_bytes=24 << 20)


def on_core(kernel, out_shape, *operands):
    return pl.pallas_call(
        kernel,
        out_shape=out_shape,
        in_specs=[VMEM] * len(operands),
        out_specs=VMEM,
        compiler_params=PARAMS,
    )(*operands)


def in_order(kernel, out_shape, *operands):
    n = len(operands)
    later = operands[-1]
    return pl.pallas_call(
        kernel,
        out_shape=[out_shape, jax.ShapeDtypeStruct(later.shape, later.dtype)],
        in_specs=[VMEM] * (n - 1) + [ANY],
        out_specs=[VMEM, ANY],
        input_output_aliases={n - 1: 1},
        compiler_params=PARAMS,
    )(*operands)


def partials_kernel(plane_ref, up_ref, down_ref, *refs):
    parts_ref, inputs_ref, upstream_ref = refs[-3:]
    step = pl.program_id(0)
    for array, (weight_ref, rows_ref) in enumerate(
        ((up_ref, inputs_ref), (down_ref, upstream_ref))
    ):
        rows = plane_ref[pl.ds(8 * step, 8), array].reshape(128, -1)
        rows_ref[...] = rows
        parts_ref[0, array] = lax.dot_general(
            weight_ref[...],
            rows,
            (((array,), (1,)), ((), ())),
            preferred_element_type=jnp.float32,
        ).astype(jnp.bfloat16)


def partials(half, plane, up_weight, down_weight, *so_far):
    features, hidden = up_weight.shape
    return pl.pallas_call(
        partials_kernel,
        grid=(2,),
        out_shape=[
            jax.ShapeDtypeStruct((4, 2, hidden, 128), jnp.bfloat16),
            pltpu.HBM((512, features), jnp.bfloat16),
            pltpu.HBM((512, features), jnp.bfloat16),
        ],
        in_specs=[VMEM] * 3 + [ANY] * len(so_far),
        out_specs=[
            pl.BlockSpec((1, 2, hidden, 128), lambda i: (2 * half + i, 0, 0, 0)),
            pl.BlockSpec((128, features), lambda i: (2 * half + i, 0)),
            pl.BlockSpec((128, features), lambda i: (2 * half + i, 0)),
        ],
        input_output_aliases={3 + i: i for i in range(len(so_far))},
        compiler_params=PARAMS,
        cost_estimate=pl.CostEstimate(
            flops=2 * 512 * features * hidden, bytes_accessed=4 << 20, transcendentals=0
        ),
    )(plane, up_weight, down_weight, *so_far)


def token_grad_kernel(first, hidden_grad_ref, up_ref, *refs):
    out_ref = refs[-2] if len(refs) == 3 else refs[0]
    for piece in range(2):
        out_ref[pl.ds(128 * piece, 128)] = lax.dot_general(
            hidden_grad_ref[first + piece],
            up_ref[...],
            (((0,), (1,)), ((), ())),
            preferred_element_type=jnp.float32,
        ).astype(jnp.bfloat16)


def total_kernel(blocks_ref, out_ref):
    acc = blocks_ref[0].astype(jnp.float32)
    for i in range(1, blocks_ref.shape[0]):
        acc = acc + blocks_ref[i].astype(jnp.float32)
    out_ref[...] = acc.astype(jnp.bfloat16)


def add_kernel(*refs):
    acc = refs[0][...].astype(jnp.float32)
    for ref in refs[1:-1]:
        acc = acc + ref[...].astype(jnp.float32)
    refs[-1][...] = acc.astype(jnp.bfloat16)


def weight_grads_kernel(
    place_ref,
    inputs_ref,
    upstream_ref,
    hidden_grad_ref,
    *refs,
):
    parts, (up_out, down_out, active_ref, up_ref, down_ref, sems) = refs[:4], refs[4:]

    def whole(ref):
        return jnp.concatenate([ref[i] for i in range(4)], axis=1)

    copies = [
        pltpu.make_async_copy(up_ref, up_out, sems.at[0]),
        pltpu.make_async_copy(down_ref, down_out, sems.at[1]),
    ]
    up_ref[...] = lax.dot_general(
        inputs_ref[...],
        whole(hidden_grad_ref),
        (((0,), (1,)), ((), ())),
        preferred_element_type=jnp.float32,
    )
    copies[0].start()
    for k in range(4):
        active_ref[place_ref[0] ^ k] = parts[k][...]
    down_ref[...] = jnp.dot(
        whole(active_ref), upstream_ref[...], preferred_element_type=jnp.float32
    )
    copies[1].start()
    for copy in copies:
        copy.wait()


def weight_grads(place, inputs, upstream, hidden_grad, active_parts):
    tokens, features = inputs.shape
    hidden = hidden_grad.shape[1]
    up = (features, hidden)
    down = (hidden, features)
    return pl.pallas_call(
        weight_grads_kernel,
        out_shape=[pltpu.HBM(up, jnp.float32), pltpu.HBM(down, jnp.float32)],
        in_specs=[pl.BlockSpec(memory_space=pltpu.SMEM)] + [VMEM] * 7,
        out_specs=[ANY, ANY],
        scratch_shapes=[
            pltpu.VMEM(hidden_grad.shape, jnp.bfloat16),
            pltpu.VMEM(up, jnp.float32),
            pltpu.VMEM(down, jnp.float32),
            pltpu.SemaphoreType.DMA((2,)),
        ],
        compiler_params=PARAMS,
        cost_estimate=pl.CostEstimate(
            flops=4 * tokens * features * hidden, bytes_accessed=8 << 20, transcendentals=0
        ),
    )(place.reshape(1), inputs, upstream, hidden_grad, *active_parts)


def on_device(tokens, out_grad, up_weight, down_weight):
    rows, features = tokens.shape
    hidden = up_weight.shape[1]

    def exchange(blocks, axis):
        return lax.all_to_all(blocks, axis, split_axis=0, concat_axis=0, tiled=True)

    def row_gather(part):
        return lax.all_gather(part[None], ("zb", "zc"), axis=0, tiled=True)

    with jax.named_scope("gather_tokens"):
        pair = lax.all_gather(jnp.stack([tokens, out_grad]), "far", axis=1, tiled=True)
        copies = jnp.broadcast_to(pair[None], (16,) + pair.shape)
        own = exchange(copies, ("x", "y"))
        other = lax.ppermute(own, "core", SWAP)
    with jax.named_scope("row_sums"):
        first = partials(0, own, up_weight, down_weight)
        parts, inputs, upstream = partials(1, other, up_weight, down_weight, *first)
        place = lax.axis_index(("zb", "zc"))
        quarter = jax.ShapeDtypeStruct((hidden, 128), jnp.bfloat16)
        sums = []
        for array in range(2):
            pieces = [
                lax.dynamic_index_in_dim(parts[:, array], place ^ k, 0, keepdims=False)
                for k in range(4)
            ]
            for k in (1, 2, 3):
                pieces[k] = lax.ppermute(
                    pieces[k], ("zb", "zc"), [(i, i ^ k) for i in range(4)]
                )
            mine = on_core(add_kernel, quarter, *pieces)
            theirs = lax.ppermute(mine, "za", SWAP)
            sums.append(mine.astype(jnp.float32) + theirs.astype(jnp.float32))
        preact, grad_active = sums
    with jax.named_scope("activate"):
        cdf = 0.5 * (1.0 + lax.erf(preact * 0.7071067811865476))
        slope = cdf + preact * jnp.exp(-0.5 * preact * preact) * 0.3989422804014327
        hidden_grad = row_gather((grad_active * slope).astype(jnp.bfloat16))
        active = (preact * cdf).astype(jnp.bfloat16)
    with jax.named_scope("token_grad"):
        half = jax.ShapeDtypeStruct((256, features), jnp.bfloat16)
        leaving, active = in_order(
            functools.partial(token_grad_kernel, 2), half, hidden_grad, up_weight, active
        )
        staying = on_core(functools.partial(token_grad_kernel, 0), half, hidden_grad, up_weight)
        arrived = lax.ppermute(leaving, "core", SWAP)
        chip_sum = on_core(add_kernel, half, staying, arrived)
        plane_sum = on_core(
            total_kernel,
            jax.ShapeDtypeStruct((2 * rows, features), jnp.bfloat16),
            exchange(chip_sum.reshape(16, -1, features), ("x", "y")),
        )
        far = lax.axis_index("far")
        mine, theirs = (
            lax.dynamic_slice_in_dim(plane_sum, rows * side, rows, axis=0)
            for side in (far, 1 - far)
        )
        token_grad = on_core(
            add_kernel,
            jax.ShapeDtypeStruct((rows, features), jnp.bfloat16),
            mine,
            lax.ppermute(theirs, "far", SWAP),
        )
    with jax.named_scope("weight_grads"):
        place = lax.axis_index(("zb", "zc"))
        active_parts = [active] + [
            lax.ppermute(active, ("zb", "zc"), [(i, i ^ k) for i in range(4)])
            for k in (1, 2, 3)
        ]
        up_grad, down_grad = weight_grads(place, inputs, upstream, hidden_grad, active_parts)
    return (token_grad, up_grad, down_grad)


def solution(mesh):
    fine = Mesh(mesh.devices.reshape(SIZES), AXES)
    return jax.shard_map(
        on_device,
        mesh=fine,
        in_specs=(P(TOKENS_OVER, ROW), P(TOKENS_OVER, ROW), P(ROW, TOKENS_OVER), P(TOKENS_OVER, ROW)),
        out_specs=(P(TOKENS_OVER, ROW), P(ROW, TOKENS_OVER), P(TOKENS_OVER, ROW)),
        check_vma=False,
    )
```

time: 163 us -> 151 us (0.926)
  blocking collectives: 79.8 us -> 50 us
  starting transfers between devices: 37.9 us -> 65.7 us
  waiting for transfers between devices: 27.8 us -> 19.7 us
  matrix products: 3.93 us -> 0 us
  Pallas kernels: 8.35 us -> 11.7 us
    ppermute x2 -> x12, starting transfers between devices: 13.7 us -> 50.8 us  [the longest x6 18.5 us: on_device(): lax.ppermute(pieces[k], ('zb', 'zc'), [(i, i ^ k) for i in range(4)])]
    all_to_all x3 -> x1, waiting for transfers between devices: 22.2 us -> 1.04 us  [exchange(): return lax.all_to_all(blocks, axis, split_axis=0, concat_axis=0, tiled=True)]
    all_gather x2 -> x1, blocking collectives: 30 us -> 12.3 us  [row_gather(): return lax.all_gather(part[None], ('zb', 'zc'), axis=0, tiled=True)]
    ppermute x2 -> x12, waiting for transfers between devices: 2.51 us -> 17.4 us  [the longest x2 17.4 us: on_device(): theirs = lax.ppermute(mine, 'za', SWAP)]
    all_gather x1 -> x0, blocking collectives: 12.2 us -> none  [on_device(): both_sums = lax.all_gather(plane_sum, 'far', axis=0, tiled=False)]
    all_to_all x3 -> x1, starting transfers between devices: 10.5 us -> 3.96 us  [exchange(): return lax.all_to_all(blocks, axis, split_axis=0, concat_axis=0, tiled=True)]
    dot_general x2 -> x0, matrix products: 3.93 us -> none  [the longest x1 2.02 us: on_device(): jnp.einsum('btd,bht->dh', inputs.reshape(4, -1, features), hidden_grad, p...]
    pallas_call x4, Pallas kernels: 5.87 us -> 9.21 us  [the longest x2 4.85 us: partials(): pl.pallas_call(partials_kernel, grid=(2,), out_shape=[jax.ShapeDtypeStruc...]
  transfers between devices with their start and end apart: 7 -> 15, of which waited for: 6 -> 4; matrix products, arithmetic and copies ran while one was open for 3% -> 0% of each run, Pallas kernels for 2% -> 4%
where the time goes in v4:
time: 151 us; the launch traced here: 150 us
  starting transfers between devices  65.7 us (44%)
  blocking collectives  50 us (33%)
  waiting for transfers between devices  19.7 us (13%)
  Pallas kernels  11.7 us (8%)
    all_to_all x1, blocking collectives, exchange(): return lax.all_to_all(blocks, axis, split_axis=0, concat_axis=0, tiled=True)  21.3 us
    ppermute x6, starting transfers between devices, on_device(): lax.ppermute(pieces[k], ('zb', 'zc'), [(i, i ^ k) for i in range(4)])  18.5 us
    ppermute x2, waiting for transfers between devices, on_device(): theirs = lax.ppermute(mine, 'za', SWAP)  17.4 us
    all_gather x1, blocking collectives, on_device(): lax.all_gather(jnp.stack([tokens, out_grad]), 'far', axis=1, tiled=True)  16.4 us
    all_gather x1, blocking collectives, row_gather(): return lax.all_gather(part[None], ('zb', 'zc'), axis=0, tiled=True)  12.3 us
    ppermute x2, starting transfers between devices, on_device(): theirs = lax.ppermute(mine, 'za', SWAP)  12.3 us
    ppermute x1, starting transfers between devices, on_device(): lax.ppermute(theirs, 'far', SWAP)  10.7 us
    ppermute x3, starting transfers between devices, on_device(): lax.ppermute(active, ('zb', 'zc'), [(i, i ^ k) for i in range(4)])  9.27 us
  transfers between devices with their start and end apart: 15, of which 4 were waited for; matrix products, arithmetic and copies ran while one was open for 0% of the time, Pallas kernels for 4%

profile of v4, /device:TPU:1, one launch (start us, length us, event | category | flops | bytes accessed | tf_op | source)
XLA Modules:
  0.0 150.1 jit_solution(3274249646121135870)
XLA Ops:
  0.6 0.0 copy-start
  0.6 0.0 copy-start.1
  0.7 0.9 pad_maximum_fusion
  1.5 16.4 %all_gather.6 = bf16[2,16,928]{2,1,0:T(8,128)(2,1)S(1)} all-gather(bf16[2,8,928]{2,1,0:T(8,128)(2,1)S(1)} %pad_maximum_fusion), channel_id=1, replica_groups=mesh['za'=2,'zb'=2,'zc'=2,'x'=4,'core'=2,'y'=4,'far'=2] {'far'}, dimensions={1}, use_global_device_ids=true | all-gather | bytes 89088 | tf_op jit(solution)/shard_map/gather_tokens/all_gather | solution.py:181
  17.9 0.1 broadcast_in_dim.4
  18.1 21.3 %all_to_all.10.plane_ref = bf16[16,2,16,928]{3,2,1,0:T(8,128)(2,1)S(1)} all-to-all(bf16[16,2,16,928]{3,2,1,0:T(8,128)(2,1)S(1)} %broadcast_in_dim.4), channel_id=1, replica_groups=mesh['za'=2,'zb'=2,'zc'=2,'x'=4,'core'=2,'y'=4,'far'=2] {'x','y'}, dimensions={0} | all-to-all | bytes 1900544 | tf_op jit(solution)/shard_map/gather_tokens/all_to_all | solution.py:175
  39.3 5.3 %collective-permute-start = (bf16[16,2,16,928]{3,2,1,0:T(8,128)(2,1)S(1)}, bf16[16,2,16,928]{3,2,1,0:T(8,128)(2,1)}, u32[]{:S(2)}, u32[]{:S(2)}) collective-permute-start(bf16[16,2,16,928]{3,2,1,0:T(8,128)(2,1)S(1)} %all_to_all.10.plane_ref), channel_id=1, source_target_pairs={{0,8},{8,0},{1,9},{9,1},{2,10},{10,2},{3,11},{11,3},{4,12},{12,4},... | collective-permute-start | bytes 2850824 | tf_op jit(solution)/shard_map/gather_tokens/ppermute | solution.py:184
  44.6 0.0 copy-done
  44.6 0.0 copy-done.1
  44.6 1.8 %row_sums.4 = (bf16[4,2,464,128]{3,2,1,0:T(8,128)(2,1)S(1)}, bf16[512,928]{1,0:T(8,128)(2,1)}, bf16[512,928]{1,0:T(8,128)(2,1)}) custom-call(bf16[16,2,16,928]{3,2,1,0:T(8,128)(2,1)S(1)} %all_to_all.10.plane_ref, bf16[928,464]{1,0:T(8,128)(2,1)S(1)} %copy-done, bf16[464,928]{1,0:T(8,128)(2,1)S(1)} %copy-done.1), custom_call_target="tpu_custom_call" | custom-call | flops 440926208 | bytes 4194304 | tf_op jit(solution)/shard_map/row_sums/pallas_call | solution.py:67
  46.5 0.5 collective-permute-done.plane_ref
  47.0 3.0 %row_sums.5 = (bf16[4,2,464,128]{3,2,1,0:T(8,128)(2,1)S(1)}, bf16[512,928]{1,0:T(8,128)(2,1)}, bf16[512,928]{1,0:T(8,128)(2,1)}) custom-call(bf16[16,2,16,928]{3,2,1,0:T(8,128)(2,1)} %collective-permute-done.plane_ref, bf16[928,464]{1,0:T(8,128)(2,1)S(1)} %copy-done, ...), custom_call_target="tpu_custom_call", output_to_operand_aliasing={{0}: (3, {}), {1}: (4, {}), {2}: (5, {})} | custom-call | flops 440926208 | bytes 4194304 | tf_op jit(solution)/shard_map/row_sums/pallas_call | solution.py:67
  50.0 0.1 fusion.6
  50.1 2.5 %collective-permute-start.5 = (bf16[464,128]{1,0:T(8,128)(2,1)S(1)}, bf16[464,128]{1,0:T(8,128)(2,1)S(1)}, u32[]{:S(2)}, u32[]{:S(2)}) collective-permute-start(bf16[464,128]{1,0:T(8,128)(2,1)S(1)} %get-tuple-element.27), channel_id=1, source_target_pairs={{0,64},{64,0},{128,192},{192,128},{1,65},{65,1},{129,193},{193,129... | collective-permute-start | bytes 356360 | tf_op jit(solution)/shard_map/row_sums/ppermute | solution.py:197
  52.7 3.2 %collective-permute-start.6 = (bf16[464,128]{1,0:T(8,128)(2,1)S(1)}, bf16[464,128]{1,0:T(8,128)(2,1)S(1)}, u32[]{:S(2)}, u32[]{:S(2)}) collective-permute-start(bf16[464,128]{1,0:T(8,128)(2,1)S(1)} %get-tuple-element.26), channel_id=1, source_target_pairs={{0,128},{64,192},{128,0},{192,64},{1,129},{65,193},{129,1},{193,65... | collective-permute-start | bytes 356360 | tf_op jit(solution)/shard_map/row_sums/ppermute | solution.py:197
  55.9 3.5 %collective-permute-start.7 = (bf16[464,128]{1,0:T(8,128)(2,1)S(1)}, bf16[464,128]{1,0:T(8,128)(2,1)S(1)}, u32[]{:S(2)}, u32[]{:S(2)}) collective-permute-start(bf16[464,128]{1,0:T(8,128)(2,1)S(1)} %get-tuple-element.25), channel_id=1, source_target_pairs={{0,192},{64,128},{128,64},{192,0},{1,193},{65,129},{129,65},{193,1... | collective-permute-start | bytes 356360 | tf_op jit(solution)/shard_map/row_sums/ppermute | solution.py:197
  59.5 1.9 %collective-permute-start.1 = (bf16[464,128]{1,0:T(8,128)(2,1)S(1)}, bf16[464,128]{1,0:T(8,128)(2,1)S(1)}, u32[]{:S(2)}, u32[]{:S(2)}) collective-permute-start(bf16[464,128]{1,0:T(8,128)(2,1)S(1)} %get-tuple-element.31), channel_id=1, source_target_pairs={{0,64},{64,0},{128,192},{192,128},{1,65},{65,1},{129,193},{193,129... | collective-permute-start | bytes 356360 | tf_op jit(solution)/shard_map/row_sums/ppermute | solution.py:197
  61.4 3.8 %collective-permute-start.2 = (bf16[464,128]{1,0:T(8,128)(2,1)S(1)}, bf16[464,128]{1,0:T(8,128)(2,1)S(1)}, u32[]{:S(2)}, u32[]{:S(2)}) collective-permute-start(bf16[464,128]{1,0:T(8,128)(2,1)S(1)} %get-tuple-element.30), channel_id=1, source_target_pairs={{0,128},{64,192},{128,0},{192,64},{1,129},{65,193},{129,1},{193,65... | collective-permute-start | bytes 356360 | tf_op jit(solution)/shard_map/row_sums/ppermute | solution.py:197
  65.2 0.0 collective-permute-done.5.refs_1_
  65.2 3.5 %collective-permute-start.3 = (bf16[464,128]{1,0:T(8,128)(2,1)S(1)}, bf16[464,128]{1,0:T(8,128)(2,1)S(1)}, u32[]{:S(2)}, u32[]{:S(2)}) collective-permute-start(bf16[464,128]{1,0:T(8,128)(2,1)S(1)} %get-tuple-element.29), channel_id=1, source_target_pairs={{0,192},{64,128},{128,64},{192,0},{1,193},{65,129},{129,65},{193,1... | collective-permute-start | bytes 356360 | tf_op jit(solution)/shard_map/row_sums/ppermute | solution.py:197
  68.8 0.0 collective-permute-done.6.refs_2_
  68.8 0.0 collective-permute-done.7.refs_3_
  68.8 0.1 row_sums.7
  68.9 7.7 %collective-permute-start.8 = (bf16[464,128]{1,0:T(8,128)(2,1)S(1)}, bf16[464,128]{1,0:T(8,128)(2,1)S(1)}, u32[]{:S(2)}, u32[]{:S(2)}) collective-permute-start(bf16[464,128]{1,0:T(8,128)(2,1)S(1)} %row_sums.7), channel_id=1, source_target_pairs={{0,256},{256,0},{1,257},{257,1},{2,258},{258,2},{3,259},{259,3},{4... | collective-permute-start | bytes 356360 | tf_op jit(solution)/shard_map/row_sums/ppermute | solution.py:201
  76.6 0.0 collective-permute-done.1.refs_1_
  76.6 0.0 collective-permute-done.2.refs_2_
  76.6 0.0 collective-permute-done.3.refs_3_
  76.6 0.1 row_sums.6
  76.7 4.6 %collective-permute-start.4 = (bf16[464,128]{1,0:T(8,128)(2,1)S(1)}, bf16[464,128]{1,0:T(8,128)(2,1)S(1)}, u32[]{:S(2)}, u32[]{:S(2)}) collective-permute-start(bf16[464,128]{1,0:T(8,128)(2,1)S(1)} %row_sums.6), channel_id=1, source_target_pairs={{0,256},{256,0},{1,257},{257,1},{2,258},{258,2},{3,259},{259,3},{4... | collective-permute-start | bytes 356360 | tf_op jit(solution)/shard_map/row_sums/ppermute | solution.py:201
  81.3 0.0 collective-permute-done.8
  81.3 17.4 %collective-permute-done.4 = bf16[464,128]{1,0:T(8,128)(2,1)S(1)} collective-permute-done((bf16[464,128]{1,0:T(8,128)(2,1)S(1)}, bf16[464,128]{1,0:T(8,128)(2,1)S(1)}, u32[]{:S(2)}, u32[]{:S(2)}) %collective-permute-start.4) | collective-permute-done | bytes 118816 | tf_op jit(solution)/shard_map/row_sums/ppermute | solution.py:201
  98.6 0.2 multiply_convert_fusion
  98.8 12.3 %all-gather = bf16[1856,128]{1,0:T(8,128)(2,1)S(1)} all-gather(bf16[464,128]{1,0:T(8,128)(2,1)S(1)} %get-tuple-element.34), channel_id=2, replica_groups=mesh['za'=2,'zb'=2,'zc'=2,'x'=4,'core'=2,'y'=4,'far'=2] {'zb','zc'}, dimensions={0}, use_global_device_ids=true | all-gather | bytes 593920 | tf_op jit(solution)/shard_map/activate/all_gather | solution.py:178
  111.1 0.7 token_grad.6
  111.8 0.0 copy-start.4
  111.8 0.6 copy-done.4
  112.5 5.7 %collective-permute-start.9 = (bf16[256,928]{1,0:T(8,128)(2,1)S(1)}, bf16[256,928]{1,0:T(8,128)(2,1)S(1)}, u32[]{:S(2)}, u32[]{:S(2)}) collective-permute-start(bf16[256,928]{1,0:T(8,128)(2,1)S(1)} %get-tuple-element.17), channel_id=1, source_target_pairs={{0,8},{8,0},{1,9},{9,1},{2,10},{10,2},{3,11},{11,3},{4,12},{12,4},... | collective-permute-start | bytes 1425416 | tf_op jit(solution)/shard_map/token_grad/ppermute | solution.py:215
  118.2 0.7 token_grad.5.refs_0_
  118.9 0.0 copy-start.5
  118.9 0.0 copy-start.2
  118.9 0.0 copy-start.3
  118.9 0.8 collective-permute-done.9.refs_1_
  119.7 0.9 token_grad.7
  120.6 4.0 %all-to-all-start.1 = ((bf16[16,16,928]{2,1,0:T(8,128)(2,1)}), bf16[16,16,928]{2,1,0:T(8,128)(2,1)S(1)}, u32[]{:S(2)}, u32[]{:S(2)}) async-start(bf16[16,16,928]{2,1,0:T(8,128)(2,1)} %bitcast.11), calls=%async_computation.1 | async-start | bytes 1048576 | tf_op jit(solution)/shard_map/token_grad/all_to_all | solution.py:175
  124.6 0.0 copy-done.5
  124.6 1.9 %collective-permute-start.11 = (bf16[464,128]{1,0:T(8,128)(2,1)S(1)}, bf16[464,128]{1,0:T(8,128)(2,1)S(1)}, u32[]{:S(2)}, u32[]{:S(2)}) collective-permute-start(bf16[464,128]{1,0:T(8,128)(2,1)S(1)} %copy-done.5), channel_id=1, source_target_pairs={{0,64},{64,0},{128,192},{192,128},{1,65},{65,1},{129,193},{193,129... | collective-permute-start | bytes 356360 | tf_op jit(solution)/shard_map/weight_grads/ppermute | solution.py:236
  126.6 2.3 %collective-permute-start.12 = (bf16[464,128]{1,0:T(8,128)(2,1)S(1)}, bf16[464,128]{1,0:T(8,128)(2,1)S(1)}, u32[]{:S(2)}, u32[]{:S(2)}) collective-permute-start(bf16[464,128]{1,0:T(8,128)(2,1)S(1)} %copy-done.5), channel_id=1, source_target_pairs={{0,128},{64,192},{128,0},{192,64},{1,129},{65,193},{129,1},{193,65... | collective-permute-start | bytes 356360 | tf_op jit(solution)/shard_map/weight_grads/ppermute | solution.py:236
  128.9 5.0 %collective-permute-start.13 = (bf16[464,128]{1,0:T(8,128)(2,1)S(1)}, bf16[464,128]{1,0:T(8,128)(2,1)}, u32[]{:S(2)}, u32[]{:S(2)}) collective-permute-start(bf16[464,128]{1,0:T(8,128)(2,1)S(1)} %copy-done.5), channel_id=1, source_target_pairs={{0,192},{64,128},{128,64},{192,0},{1,193},{65,129},{129,65},{193,1... | collective-permute-start | bytes 356360 | tf_op jit(solution)/shard_map/weight_grads/ppermute | solution.py:236
  133.9 1.0 all-to-all-done.1.blocks_ref
  135.0 0.1 token_grad.8
  135.1 10.7 %collective-permute-start.10 = (bf16[8,928]{1,0:T(8,128)(2,1)S(1)}, bf16[8,928]{1,0:T(8,128)(2,1)S(1)}, u32[]{:S(2)}, u32[]{:S(2)}) collective-permute-start(bf16[8,928]{1,0:T(8,128)(2,1)S(1)} %get-tuple-element.35), channel_id=1, source_target_pairs={{0,1},{1,0},{2,3},{3,2},{4,5},{5,4},{6,7},{7,6},{8,9},{9,8},{10,11... | collective-permute-start | bytes 44552 | tf_op jit(solution)/shard_map/token_grad/ppermute | solution.py:231
  145.8 0.0 collective-permute-done.11.refs_1_
  145.8 0.0 collective-permute-done.12.refs_2_
  145.8 0.0 collective-permute-done.13.refs_3_
  145.8 0.0 copy-done.2
  145.8 0.0 copy-done.3
  145.8 3.7 %weight_grads.1 = (f32[928,464]{1,0:T(8,128)}, f32[464,928]{1,0:T(8,128)}) custom-call(s32[1]{0:T(128)} %bitcast.12.place_ref, bf16[512,928]{1,0:T(8,128)(2,1)S(1)} %copy-done.2, bf16[512,928]{1,0:T(8,128)(2,1)S(1)} %copy-done.3, bf16[4,464,128]{2,1,0:T(8,128)(2,1)S(1)} %bitcast.23, bf16[464,128]{1,0:T(8,128)(2,1)S(1)} %copy-done.5, ...), custom_call_target="tpu_custom_call" | custom-call | flops 881852416 | bytes 8388608 | tf_op jit(solution)/shard_map/weight_grads/pallas_call | solution.py:152
  149.5 0.0 collective-permute-done.10.refs_1_
  149.5 0.6 token_grad.9
  (3 shorter events, 0.1 us)
Async XLA Ops:
  0.6 44.0 %copy-start = (bf16[928,464]{1,0:T(8,128)(2,1)S(1)}, bf16[928,464]{1,0:T(8,128)(2,1)}, u32[]{:S(2)}) copy-start(bf16[928,464]{1,0:T(8,128)(2,1)} %up_ref.7) | copy-start | bytes 2583556
  0.6 44.0 %copy-start.1 = (bf16[464,928]{1,0:T(8,128)(2,1)S(1)}, bf16[464,928]{1,0:T(8,128)(2,1)}, u32[]{:S(2)}) copy-start(bf16[464,928]{1,0:T(8,128)(2,1)} %down_ref.3) | copy-start | bytes 2583556
  39.3 7.7 %collective-permute-start = (bf16[16,2,16,928]{3,2,1,0:T(8,128)(2,1)S(1)}, bf16[16,2,16,928]{3,2,1,0:T(8,128)(2,1)}, u32[]{:S(2)}, u32[]{:S(2)}) collective-permute-start(bf16[16,2,16,928]{3,2,1,0:T(8,128)(2,1)S(1)} %all_to_all.10.plane_ref), channel_id=1, source_target_pairs={{0,8},{8,0},{1,9},{9,1},{2,10},{10,2},{3,11},{11,3},{4,12},{12,4},... | collective-permute-start | bytes 2850824 | tf_op jit(solution)/shard_map/gather_tokens/ppermute | solution.py:184
  50.1 15.1 %collective-permute-start.5 = (bf16[464,128]{1,0:T(8,128)(2,1)S(1)}, bf16[464,128]{1,0:T(8,128)(2,1)S(1)}, u32[]{:S(2)}, u32[]{:S(2)}) collective-permute-start(bf16[464,128]{1,0:T(8,128)(2,1)S(1)} %get-tuple-element.27), channel_id=1, source_target_pairs={{0,64},{64,0},{128,192},{192,128},{1,65},{65,1},{129,193},{193,129... | collective-permute-start | bytes 356360 | tf_op jit(solution)/shard_map/row_sums/ppermute | solution.py:197
  52.7 16.1 %collective-permute-start.6 = (bf16[464,128]{1,0:T(8,128)(2,1)S(1)}, bf16[464,128]{1,0:T(8,128)(2,1)S(1)}, u32[]{:S(2)}, u32[]{:S(2)}) collective-permute-start(bf16[464,128]{1,0:T(8,128)(2,1)S(1)} %get-tuple-element.26), channel_id=1, source_target_pairs={{0,128},{64,192},{128,0},{192,64},{1,129},{65,193},{129,1},{193,65... | collective-permute-start | bytes 356360 | tf_op jit(solution)/shard_map/row_sums/ppermute | solution.py:197
  55.9 12.9 %collective-permute-start.7 = (bf16[464,128]{1,0:T(8,128)(2,1)S(1)}, bf16[464,128]{1,0:T(8,128)(2,1)S(1)}, u32[]{:S(2)}, u32[]{:S(2)}) collective-permute-start(bf16[464,128]{1,0:T(8,128)(2,1)S(1)} %get-tuple-element.25), channel_id=1, source_target_pairs={{0,192},{64,128},{128,64},{192,0},{1,193},{65,129},{129,65},{193,1... | collective-permute-start | bytes 356360 | tf_op jit(solution)/shard_map/row_sums/ppermute | solution.py:197
  59.5 17.1 %collective-permute-start.1 = (bf16[464,128]{1,0:T(8,128)(2,1)S(1)}, bf16[464,128]{1,0:T(8,128)(2,1)S(1)}, u32[]{:S(2)}, u32[]{:S(2)}) collective-permute-start(bf16[464,128]{1,0:T(8,128)(2,1)S(1)} %get-tuple-element.31), channel_id=1, source_target_pairs={{0,64},{64,0},{128,192},{192,128},{1,65},{65,1},{129,193},{193,129... | collective-permute-start | bytes 356360 | tf_op jit(solution)/shard_map/row_sums/ppermute | solution.py:197
  61.4 15.2 %collective-permute-start.2 = (bf16[464,128]{1,0:T(8,128)(2,1)S(1)}, bf16[464,128]{1,0:T(8,128)(2,1)S(1)}, u32[]{:S(2)}, u32[]{:S(2)}) collective-permute-start(bf16[464,128]{1,0:T(8,128)(2,1)S(1)} %get-tuple-element.30), channel_id=1, source_target_pairs={{0,128},{64,192},{128,0},{192,64},{1,129},{65,193},{129,1},{193,65... | collective-permute-start | bytes 356360 | tf_op jit(solution)/shard_map/row_sums/ppermute | solution.py:197
  65.2 11.4 %collective-permute-start.3 = (bf16[464,128]{1,0:T(8,128)(2,1)S(1)}, bf16[464,128]{1,0:T(8,128)(2,1)S(1)}, u32[]{:S(2)}, u32[]{:S(2)}) collective-permute-start(bf16[464,128]{1,0:T(8,128)(2,1)S(1)} %get-tuple-element.29), channel_id=1, source_target_pairs={{0,192},{64,128},{128,64},{192,0},{1,193},{65,129},{129,65},{193,1... | collective-permute-start | bytes 356360 | tf_op jit(solution)/shard_map/row_sums/ppermute | solution.py:197
  68.9 12.4 %collective-permute-start.8 = (bf16[464,128]{1,0:T(8,128)(2,1)S(1)}, bf16[464,128]{1,0:T(8,128)(2,1)S(1)}, u32[]{:S(2)}, u32[]{:S(2)}) collective-permute-start(bf16[464,128]{1,0:T(8,128)(2,1)S(1)} %row_sums.7), channel_id=1, source_target_pairs={{0,256},{256,0},{1,257},{257,1},{2,258},{258,2},{3,259},{259,3},{4... | collective-permute-start | bytes 356360 | tf_op jit(solution)/shard_map/row_sums/ppermute | solution.py:201
  76.7 21.9 %collective-permute-start.4 = (bf16[464,128]{1,0:T(8,128)(2,1)S(1)}, bf16[464,128]{1,0:T(8,128)(2,1)S(1)}, u32[]{:S(2)}, u32[]{:S(2)}) collective-permute-start(bf16[464,128]{1,0:T(8,128)(2,1)S(1)} %row_sums.6), channel_id=1, source_target_pairs={{0,256},{256,0},{1,257},{257,1},{2,258},{258,2},{3,259},{259,3},{4... | collective-permute-start | bytes 356360 | tf_op jit(solution)/shard_map/row_sums/ppermute | solution.py:201
  111.8 0.6 copy-start.4
  112.5 7.2 %collective-permute-start.9 = (bf16[256,928]{1,0:T(8,128)(2,1)S(1)}, bf16[256,928]{1,0:T(8,128)(2,1)S(1)}, u32[]{:S(2)}, u32[]{:S(2)}) collective-permute-start(bf16[256,928]{1,0:T(8,128)(2,1)S(1)} %get-tuple-element.17), channel_id=1, source_target_pairs={{0,8},{8,0},{1,9},{9,1},{2,10},{10,2},{3,11},{11,3},{4,12},{12,4},... | collective-permute-start | bytes 1425416 | tf_op jit(solution)/shard_map/token_grad/ppermute | solution.py:215
  118.9 5.7 %copy-start.5 = (bf16[464,128]{1,0:T(8,128)(2,1)S(1)}, bf16[464,128]{1,0:T(8,128)(2,1)}, u32[]{:S(2)}) copy-start(bf16[464,128]{1,0:T(8,128)(2,1)} %copy-done.4) | copy-start | bytes 356356
  118.9 26.9 %copy-start.2 = (bf16[512,928]{1,0:T(8,128)(2,1)S(1)}, bf16[512,928]{1,0:T(8,128)(2,1)}, u32[]{:S(2)}) copy-start(bf16[512,928]{1,0:T(8,128)(2,1)} %get-tuple-element.18.inputs_ref) | copy-start | bytes 2850820
  118.9 26.9 %copy-start.3 = (bf16[512,928]{1,0:T(8,128)(2,1)S(1)}, bf16[512,928]{1,0:T(8,128)(2,1)}, u32[]{:S(2)}) copy-start(bf16[512,928]{1,0:T(8,128)(2,1)} %get-tuple-element.19.upstream_ref) | copy-start | bytes 2850820
  120.6 14.3 %all-to-all-start.1 = ((bf16[16,16,928]{2,1,0:T(8,128)(2,1)}), bf16[16,16,928]{2,1,0:T(8,128)(2,1)S(1)}, u32[]{:S(2)}, u32[]{:S(2)}) async-start(bf16[16,16,928]{2,1,0:T(8,128)(2,1)} %bitcast.11), calls=%async_computation.1 | async-start | bytes 1048576 | tf_op jit(solution)/shard_map/token_grad/all_to_all | solution.py:175
  124.6 21.1 %collective-permute-start.11 = (bf16[464,128]{1,0:T(8,128)(2,1)S(1)}, bf16[464,128]{1,0:T(8,128)(2,1)S(1)}, u32[]{:S(2)}, u32[]{:S(2)}) collective-permute-start(bf16[464,128]{1,0:T(8,128)(2,1)S(1)} %copy-done.5), channel_id=1, source_target_pairs={{0,64},{64,0},{128,192},{192,128},{1,65},{65,1},{129,193},{193,129... | collective-permute-start | bytes 356360 | tf_op jit(solution)/shard_map/weight_grads/ppermute | solution.py:236
  126.6 19.2 %collective-permute-start.12 = (bf16[464,128]{1,0:T(8,128)(2,1)S(1)}, bf16[464,128]{1,0:T(8,128)(2,1)S(1)}, u32[]{:S(2)}, u32[]{:S(2)}) collective-permute-start(bf16[464,128]{1,0:T(8,128)(2,1)S(1)} %copy-done.5), channel_id=1, source_target_pairs={{0,128},{64,192},{128,0},{192,64},{1,129},{65,193},{129,1},{193,65... | collective-permute-start | bytes 356360 | tf_op jit(solution)/shard_map/weight_grads/ppermute | solution.py:236
  128.9 16.9 %collective-permute-start.13 = (bf16[464,128]{1,0:T(8,128)(2,1)S(1)}, bf16[464,128]{1,0:T(8,128)(2,1)}, u32[]{:S(2)}, u32[]{:S(2)}) collective-permute-start(bf16[464,128]{1,0:T(8,128)(2,1)S(1)} %copy-done.5), channel_id=1, source_target_pairs={{0,192},{64,128},{128,64},{192,0},{1,193},{65,129},{129,65},{193,1... | collective-permute-start | bytes 356360 | tf_op jit(solution)/shard_map/weight_grads/ppermute | solution.py:236
  135.1 14.4 %collective-permute-start.10 = (bf16[8,928]{1,0:T(8,128)(2,1)S(1)}, bf16[8,928]{1,0:T(8,128)(2,1)S(1)}, u32[]{:S(2)}, u32[]{:S(2)}) collective-permute-start(bf16[8,928]{1,0:T(8,128)(2,1)S(1)} %get-tuple-element.35), channel_id=1, source_target_pairs={{0,1},{1,0},{2,3},{3,2},{4,5},{5,4},{6,7},{7,6},{8,9},{9,8},{10,11... | collective-permute-start | bytes 44552 | tf_op jit(solution)/shard_map/token_grad/ppermute | solution.py:231

commit v5 on v4

--- a/solution.py
+++ b/solution.py
@@ -46,27 +46,41 @@
     )(*operands)
 
 
+SMEM = pl.BlockSpec(memory_space=pltpu.SMEM)
+
+
+def with_scalars(kernel, out_shape, scalars, *operands):
+    return pl.pallas_call(
+        kernel,
+        out_shape=out_shape,
+        in_specs=[SMEM] + [VMEM] * len(operands),
+        out_specs=[VMEM] * len(out_shape),
+        compiler_params=PARAMS,
+    )(scalars, *operands)
+
+
 def partials_kernel(plane_ref, up_ref, down_ref, *refs):
     parts_ref, inputs_ref, upstream_ref = refs[-3:]
-    step = pl.program_id(0)
     for array, (weight_ref, rows_ref) in enumerate(
         ((up_ref, inputs_ref), (down_ref, upstream_ref))
     ):
-        rows = plane_ref[pl.ds(8 * step, 8), array].reshape(128, -1)
+        rows = plane_ref[:, array].reshape(256, -1)
         rows_ref[...] = rows
-        parts_ref[0, array] = lax.dot_general(
+        both = lax.dot_general(
             weight_ref[...],
             rows,
             (((array,), (1,)), ((), ())),
             preferred_element_type=jnp.float32,
         ).astype(jnp.bfloat16)
+        for block in range(2):
+            parts_ref[block, array] = both[:, 128 * block : 128 * block + 128]
 
 
 def partials(half, plane, up_weight, down_weight, *so_far):
     features, hidden = up_weight.shape
     return pl.pallas_call(
         partials_kernel,
-        grid=(2,),
+        grid=(1,),
         out_shape=[
             jax.ShapeDtypeStruct((4, 2, hidden, 128), jnp.bfloat16),
             pltpu.HBM((512, features), jnp.bfloat16),
@@ -74,9 +88,9 @@
         ],
         in_specs=[VMEM] * 3 + [ANY] * len(so_far),
         out_specs=[
-            pl.BlockSpec((1, 2, hidden, 128), lambda i: (2 * half + i, 0, 0, 0)),
-            pl.BlockSpec((128, features), lambda i: (2 * half + i, 0)),
-            pl.BlockSpec((128, features), lambda i: (2 * half + i, 0)),
+            pl.BlockSpec((2, 2, hidden, 128), lambda i: (half, 0, 0, 0)),
+            pl.BlockSpec((256, features), lambda i: (half, 0)),
+            pl.BlockSpec((256, features), lambda i: (half, 0)),
         ],
         input_output_aliases={3 + i: i for i in range(len(so_far))},
         compiler_params=PARAMS,
@@ -84,6 +98,13 @@
             flops=2 * 512 * features * hidden, bytes_accessed=4 << 20, transcendentals=0
         ),
     )(plane, up_weight, down_weight, *so_far)
+
+
+def halve_kernel(bits_ref, staying_ref, arrived_ref, leaving_out, staying_out):
+    near = bits_ref[0]
+    for side, out_ref in ((1 - near, leaving_out), (near, staying_out)):
+        both = staying_ref[side].astype(jnp.float32) + arrived_ref[side].astype(jnp.float32)
+        out_ref[...] = both.astype(out_ref.dtype)
 
 
 def token_grad_kernel(first, hidden_grad_ref, up_ref, *refs):
@@ -152,7 +173,7 @@
     return pl.pallas_call(
         weight_grads_kernel,
         out_shape=[pltpu.HBM(up, jnp.float32), pltpu.HBM(down, jnp.float32)],
-        in_specs=[pl.BlockSpec(memory_space=pltpu.SMEM)] + [VMEM] * 7,
+        in_specs=[SMEM] + [VMEM] * 7,
         out_specs=[ANY, ANY],
         scratch_shapes=[
             pltpu.VMEM(hidden_grad.shape, jnp.bfloat16),
@@ -185,19 +206,31 @@
     with jax.named_scope("row_sums"):
         first = partials(0, own, up_weight, down_weight)
         parts, inputs, upstream = partials(1, other, up_weight, down_weight, *first)
-        place = lax.axis_index(("zb", "zc"))
-        quarter = jax.ShapeDtypeStruct((hidden, 128), jnp.bfloat16)
+        near, next_to = lax.axis_index("zb"), lax.axis_index("zc")
+        bits = jnp.stack([near, next_to])
+        pair = parts.reshape(2, 2, 2, hidden, 128)
         sums = []
         for array in range(2):
-            pieces = [
-                lax.dynamic_index_in_dim(parts[:, array], place ^ k, 0, keepdims=False)
-                for k in range(4)
-            ]
-            for k in (1, 2, 3):
-                pieces[k] = lax.ppermute(
-                    pieces[k], ("zb", "zc"), [(i, i ^ k) for i in range(4)]
-                )
-            mine = on_core(add_kernel, quarter, *pieces)
+            leaving, staying = (
+                lax.dynamic_index_in_dim(pair[:, :, array], side, 1, keepdims=False)
+                for side in (1 - next_to, next_to)
+            )
+            leaving, staying = with_scalars(
+                halve_kernel,
+                [
+                    jax.ShapeDtypeStruct((hidden, 128), jnp.bfloat16),
+                    jax.ShapeDtypeStruct((hidden, 128), jnp.float32),
+                ],
+                bits,
+                staying,
+                lax.ppermute(leaving, "zc", SWAP),
+            )
+            mine = on_core(
+                add_kernel,
+                jax.ShapeDtypeStruct((hidden, 128), jnp.bfloat16),
+                staying,
+                lax.ppermute(leaving, "zb", SWAP),
+            )
             theirs = lax.ppermute(mine, "za", SWAP)
             sums.append(mine.astype(jnp.float32) + theirs.astype(jnp.float32))
         preact, grad_active = sums

time: 151 us -> 150 us (level)
  starting transfers between devices: 65.7 us -> 63.6 us
  waiting for transfers between devices: 19.7 us -> 21.5 us
    ppermute x6 -> x4, starting transfers between devices: 18.5 us -> 11.5 us  [the longest x2 6.22 us: on_device(): lax.ppermute(leaving, 'zb', SWAP)]
    ppermute x6 -> x4, waiting for transfers between devices: 0.02 us -> 4.83 us  [the longest x2 4.82 us: on_device(): lax.ppermute(leaving, 'zc', SWAP)]
    ppermute x2, starting transfers between devices: 12.3 us -> 16 us  [on_device(): theirs = lax.ppermute(mine, 'za', SWAP)]
    ppermute x2, waiting for transfers between devices: 17.4 us -> 13.9 us  [on_device(): theirs = lax.ppermute(mine, 'za', SWAP)]
    pallas_call x2 -> x4, Pallas kernels: 4.85 us -> 5.14 us  [the longest x2 3.94 us: partials(): pl.pallas_call(partials_kernel, grid=(1,), out_shape=[jax.ShapeDtypeStruc...]
  transfers between devices with their start and end apart: 15 -> 13, of which waited for: 4 -> 6; matrix products, arithmetic and copies ran while one was open for 0% -> 0% of each run, Pallas kernels for 4% -> 5%
where the time goes in v5:
time: 150 us; the launch traced here: 149 us
  starting transfers between devices  63.6 us (42%)
  blocking collectives  49.4 us (33%)
  waiting for transfers between devices  21.5 us (14%)
  Pallas kernels  11.9 us (8%)
    all_to_all x1, blocking collectives, exchange(): return lax.all_to_all(blocks, axis, split_axis=0, concat_axis=0, tiled=True)  21.3 us
    all_gather x1, blocking collectives, on_device(): lax.all_gather(jnp.stack([tokens, out_grad]), 'far', axis=1, tiled=True)  16.4 us
    ppermute x2, starting transfers between devices, on_device(): theirs = lax.ppermute(mine, 'za', SWAP)  16 us
    ppermute x2, waiting for transfers between devices, on_device(): theirs = lax.ppermute(mine, 'za', SWAP)  13.9 us
    all_gather x1, blocking collectives, row_gather(): return lax.all_gather(part[None], ('zb', 'zc'), axis=0, tiled=True)  11.8 us
    ppermute x1, starting transfers between devices, on_device(): lax.ppermute(theirs, 'far', SWAP)  11.2 us
    ppermute x3, starting transfers between devices, on_device(): lax.ppermute(active, ('zb', 'zc'), [(i, i ^ k) for i in range(4)])  9.27 us
    ppermute x1, starting transfers between devices, on_device(): arrived = lax.ppermute(leaving, 'core', SWAP)  6.57 us
  transfers between devices with their start and end apart: 13, of which 6 were waited for; matrix products, arithmetic and copies ran while one was open for 0% of the time, Pallas kernels for 5%

profile of v5, /device:TPU:1, one launch (start us, length us, event | category | flops | bytes accessed | tf_op | source)
XLA Modules:
  0.0 149.5 jit_solution(16077798795399129966)
XLA Ops:
  0.6 0.0 copy-start
  0.6 0.0 copy-start.1
  0.7 0.9 pad_maximum_fusion
  1.5 16.4 %all_gather.6 = bf16[2,16,928]{2,1,0:T(8,128)(2,1)S(1)} all-gather(bf16[2,8,928]{2,1,0:T(8,128)(2,1)S(1)} %pad_maximum_fusion), channel_id=1, replica_groups=mesh['za'=2,'zb'=2,'zc'=2,'x'=4,'core'=2,'y'=4,'far'=2] {'far'}, dimensions={1}, use_global_device_ids=true | all-gather | bytes 89088 | tf_op jit(solution)/shard_map/gather_tokens/all_gather | solution.py:202
  17.9 0.1 broadcast_in_dim.4
  18.1 21.3 %all_to_all.10.plane_ref = bf16[16,2,16,928]{3,2,1,0:T(8,128)(2,1)S(1)} all-to-all(bf16[16,2,16,928]{3,2,1,0:T(8,128)(2,1)S(1)} %broadcast_in_dim.4), channel_id=1, replica_groups=mesh['za'=2,'zb'=2,'zc'=2,'x'=4,'core'=2,'y'=4,'far'=2] {'x','y'}, dimensions={0} | all-to-all | bytes 1900544 | tf_op jit(solution)/shard_map/gather_tokens/all_to_all | solution.py:196
  39.3 5.3 %collective-permute-start = (bf16[16,2,16,928]{3,2,1,0:T(8,128)(2,1)S(1)}, bf16[16,2,16,928]{3,2,1,0:T(8,128)(2,1)}, u32[]{:S(2)}, u32[]{:S(2)}) collective-permute-start(bf16[16,2,16,928]{3,2,1,0:T(8,128)(2,1)S(1)} %all_to_all.10.plane_ref), channel_id=1, source_target_pairs={{0,8},{8,0},{1,9},{9,1},{2,10},{10,2},{3,11},{11,3},{4,12},{12,4},... | collective-permute-start | bytes 2850824 | tf_op jit(solution)/shard_map/gather_tokens/ppermute | solution.py:205
  44.6 0.0 copy-done
  44.6 0.0 copy-done.1
  44.6 1.4 row_sums.6
  46.0 1.0 collective-permute-done.plane_ref
  47.0 2.6 %row_sums.7 = (bf16[4,2,464,128]{3,2,1,0:T(8,128)(2,1)S(1)}, bf16[512,928]{1,0:T(8,128)(2,1)}, bf16[512,928]{1,0:T(8,128)(2,1)}) custom-call(bf16[16,2,16,928]{3,2,1,0:T(8,128)(2,1)} %collective-permute-done.plane_ref, bf16[928,464]{1,0:T(8,128)(2,1)S(1)} %copy-done, ...), custom_call_target="tpu_custom_call", output_to_operand_aliasing={{0}: (3, {}), {1}: (4, {}), {2}: (5, {})} | custom-call | flops 440926208 | bytes 4194304 | tf_op jit(solution)/shard_map/row_sums/pallas_call | solution.py:81
  49.6 0.1 fusion.6
  49.6 0.1 dynamic-slice_bitcast_fusion
  49.7 2.5 %collective-permute-start.4 = (bf16[2,464,128]{2,1,0:T(8,128)(2,1)S(1)}, bf16[2,464,128]{2,1,0:T(8,128)(2,1)S(1)}, u32[]{:S(2)}, u32[]{:S(2)}) collective-permute-start(bf16[2,464,128]{2,1,0:T(8,128)(2,1)S(1)} %get-tuple-element.33), channel_id=1, source_target_pairs={{0,64},{64,0},{1,65},{65,1},{2,66},{66,2},{3,67},{67,3},{4,68},{68... | collective-permute-start | bytes 712712 | tf_op jit(solution)/shard_map/row_sums/ppermute | solution.py:226
  52.2 0.1 dynamic-slice_bitcast_fusion.2
  52.3 2.7 %collective-permute-start.1 = (bf16[2,464,128]{2,1,0:T(8,128)(2,1)S(1)}, bf16[2,464,128]{2,1,0:T(8,128)(2,1)S(1)}, u32[]{:S(2)}, u32[]{:S(2)}) collective-permute-start(bf16[2,464,128]{2,1,0:T(8,128)(2,1)S(1)} %get-tuple-element.35), channel_id=1, source_target_pairs={{0,64},{64,0},{1,65},{65,1},{2,66},{66,2},{3,67},{67,3},{4,68},{68... | collective-permute-start | bytes 712712 | tf_op jit(solution)/shard_map/row_sums/ppermute | solution.py:226
  55.0 0.1 pad_add_fusion.bits_ref
  55.1 3.5 %collective-permute-done.4.arrived_ref = bf16[2,464,128]{2,1,0:T(8,128)(2,1)S(1)} collective-permute-done((bf16[2,464,128]{2,1,0:T(8,128)(2,1)S(1)}, bf16[2,464,128]{2,1,0:T(8,128)(2,1)S(1)}, u32[]{:S(2)}, u32[]{:S(2)}) %collective-permute-start.4) | collective-permute-done | bytes 237600 | tf_op jit(solution)/shard_map/row_sums/ppermute | solution.py:226
  58.6 0.6 row_sums.10
  59.2 3.1 %collective-permute-start.5 = (bf16[464,128]{1,0:T(8,128)(2,1)S(1)}, bf16[464,128]{1,0:T(8,128)(2,1)S(1)}, u32[]{:S(2)}, u32[]{:S(2)}) collective-permute-start(bf16[464,128]{1,0:T(8,128)(2,1)S(1)} %get-tuple-element.24), channel_id=1, source_target_pairs={{0,128},{128,0},{1,129},{129,1},{2,130},{130,2},{3,131},{131,3},{4... | collective-permute-start | bytes 356360 | tf_op jit(solution)/shard_map/row_sums/ppermute | solution.py:232
  62.3 1.4 collective-permute-done.1.arrived_ref
  63.7 0.6 row_sums.8
  64.3 3.1 %collective-permute-start.2 = (bf16[464,128]{1,0:T(8,128)(2,1)S(1)}, bf16[464,128]{1,0:T(8,128)(2,1)S(1)}, u32[]{:S(2)}, u32[]{:S(2)}) collective-permute-start(bf16[464,128]{1,0:T(8,128)(2,1)S(1)} %get-tuple-element.22), channel_id=1, source_target_pairs={{0,128},{128,0},{1,129},{129,1},{2,130},{130,2},{3,131},{131,3},{4... | collective-permute-start | bytes 356360 | tf_op jit(solution)/shard_map/row_sums/ppermute | solution.py:232
  67.4 0.0 collective-permute-done.5.refs_1_
  67.4 8.9 %collective-permute-start.6 = (bf16[464,128]{1,0:T(8,128)(2,1)S(1)}, bf16[464,128]{1,0:T(8,128)(2,1)S(1)}, u32[]{:S(2)}, u32[]{:S(2)}) collective-permute-start(bf16[464,128]{1,0:T(8,128)(2,1)S(1)} %row_sums.11), channel_id=1, source_target_pairs={{0,256},{256,0},{1,257},{257,1},{2,258},{258,2},{3,259},{259,3},{4... | collective-permute-start | bytes 356360 | tf_op jit(solution)/shard_map/row_sums/ppermute | solution.py:234
  76.3 0.0 collective-permute-done.2.refs_1_
  76.4 7.2 %collective-permute-start.3 = (bf16[464,128]{1,0:T(8,128)(2,1)S(1)}, bf16[464,128]{1,0:T(8,128)(2,1)S(1)}, u32[]{:S(2)}, u32[]{:S(2)}) collective-permute-start(bf16[464,128]{1,0:T(8,128)(2,1)S(1)} %row_sums.9), channel_id=1, source_target_pairs={{0,256},{256,0},{1,257},{257,1},{2,258},{258,2},{3,259},{259,3},{4... | collective-permute-start | bytes 356360 | tf_op jit(solution)/shard_map/row_sums/ppermute | solution.py:234
  83.5 0.0 collective-permute-done.6
  83.5 13.8 %collective-permute-done.3 = bf16[464,128]{1,0:T(8,128)(2,1)S(1)} collective-permute-done((bf16[464,128]{1,0:T(8,128)(2,1)S(1)}, bf16[464,128]{1,0:T(8,128)(2,1)S(1)}, u32[]{:S(2)}, u32[]{:S(2)}) %collective-permute-start.3) | collective-permute-done | bytes 118816 | tf_op jit(solution)/shard_map/row_sums/ppermute | solution.py:234
  97.4 0.2 multiply_convert_fusion
  97.6 11.8 %all-gather = bf16[1856,128]{1,0:T(8,128)(2,1)S(1)} all-gather(bf16[464,128]{1,0:T(8,128)(2,1)S(1)} %get-tuple-element.38), channel_id=2, replica_groups=mesh['za'=2,'zb'=2,'zc'=2,'x'=4,'core'=2,'y'=4,'far'=2] {'zb','zc'}, dimensions={0}, use_global_device_ids=true | all-gather | bytes 593920 | tf_op jit(solution)/shard_map/activate/all_gather | solution.py:199
  109.3 0.7 token_grad.6
  110.0 0.0 copy-start.4
  110.0 0.6 copy-done.4
  110.7 6.6 %collective-permute-start.7 = (bf16[256,928]{1,0:T(8,128)(2,1)S(1)}, bf16[256,928]{1,0:T(8,128)(2,1)S(1)}, u32[]{:S(2)}, u32[]{:S(2)}) collective-permute-start(bf16[256,928]{1,0:T(8,128)(2,1)S(1)} %get-tuple-element.25), channel_id=1, source_target_pairs={{0,8},{8,0},{1,9},{9,1},{2,10},{10,2},{3,11},{11,3},{4,12},{12,4},... | collective-permute-start | bytes 1425416 | tf_op jit(solution)/shard_map/token_grad/ppermute | solution.py:248
  117.2 0.7 token_grad.5.refs_0_
  118.0 0.0 copy-start.5
  118.0 0.0 copy-start.2
  118.0 0.0 copy-start.3
  118.0 0.8 collective-permute-done.7.refs_1_
  118.8 0.9 token_grad.7
  119.7 3.8 %all-to-all-start.1 = ((bf16[16,16,928]{2,1,0:T(8,128)(2,1)}), bf16[16,16,928]{2,1,0:T(8,128)(2,1)S(1)}, u32[]{:S(2)}, u32[]{:S(2)}) async-start(bf16[16,16,928]{2,1,0:T(8,128)(2,1)} %bitcast.10), calls=%async_computation.1 | async-start | bytes 1048576 | tf_op jit(solution)/shard_map/token_grad/all_to_all | solution.py:196
  123.5 0.0 copy-done.5
  123.5 1.9 %collective-permute-start.9 = (bf16[464,128]{1,0:T(8,128)(2,1)S(1)}, bf16[464,128]{1,0:T(8,128)(2,1)S(1)}, u32[]{:S(2)}, u32[]{:S(2)}) collective-permute-start(bf16[464,128]{1,0:T(8,128)(2,1)S(1)} %copy-done.5), channel_id=1, source_target_pairs={{0,64},{64,0},{128,192},{192,128},{1,65},{65,1},{129,193},{193,129... | collective-permute-start | bytes 356360 | tf_op jit(solution)/shard_map/weight_grads/ppermute | solution.py:269
  125.4 2.4 %collective-permute-start.10 = (bf16[464,128]{1,0:T(8,128)(2,1)S(1)}, bf16[464,128]{1,0:T(8,128)(2,1)S(1)}, u32[]{:S(2)}, u32[]{:S(2)}) collective-permute-start(bf16[464,128]{1,0:T(8,128)(2,1)S(1)} %copy-done.5), channel_id=1, source_target_pairs={{0,128},{64,192},{128,0},{192,64},{1,129},{65,193},{129,1},{193,65... | collective-permute-start | bytes 356360 | tf_op jit(solution)/shard_map/weight_grads/ppermute | solution.py:269
  127.8 5.0 %collective-permute-start.11 = (bf16[464,128]{1,0:T(8,128)(2,1)S(1)}, bf16[464,128]{1,0:T(8,128)(2,1)}, u32[]{:S(2)}, u32[]{:S(2)}) collective-permute-start(bf16[464,128]{1,0:T(8,128)(2,1)S(1)} %copy-done.5), channel_id=1, source_target_pairs={{0,192},{64,128},{128,64},{192,0},{1,193},{65,129},{129,65},{193,1... | collective-permute-start | bytes 356360 | tf_op jit(solution)/shard_map/weight_grads/ppermute | solution.py:269
  132.8 1.0 all-to-all-done.1.blocks_ref
  133.9 0.1 token_grad.8
  134.0 11.2 %collective-permute-start.8 = (bf16[8,928]{1,0:T(8,128)(2,1)S(1)}, bf16[8,928]{1,0:T(8,128)(2,1)S(1)}, u32[]{:S(2)}, u32[]{:S(2)}) collective-permute-start(bf16[8,928]{1,0:T(8,128)(2,1)S(1)} %get-tuple-element.39), channel_id=1, source_target_pairs={{0,1},{1,0},{2,3},{3,2},{4,5},{5,4},{6,7},{7,6},{8,9},{9,8},{10,11... | collective-permute-start | bytes 44552 | tf_op jit(solution)/shard_map/token_grad/ppermute | solution.py:264
  145.1 0.0 collective-permute-done.9.refs_1_
  145.1 0.0 collective-permute-done.10.refs_2_
  145.2 0.0 collective-permute-done.11.refs_3_
  145.2 0.0 copy-done.2
  145.2 0.0 copy-done.3
  145.2 3.7 %weight_grads.1 = (f32[928,464]{1,0:T(8,128)}, f32[464,928]{1,0:T(8,128)}) custom-call(s32[1]{0:T(128)} %bitcast.11.place_ref, bf16[512,928]{1,0:T(8,128)(2,1)S(1)} %copy-done.2, bf16[512,928]{1,0:T(8,128)(2,1)S(1)} %copy-done.3, bf16[4,464,128]{2,1,0:T(8,128)(2,1)S(1)} %bitcast.26, bf16[464,128]{1,0:T(8,128)(2,1)S(1)} %copy-done.5, ...), custom_call_target="tpu_custom_call" | custom-call | flops 881852416 | bytes 8388608 | tf_op jit(solution)/shard_map/weight_grads/pallas_call | solution.py:173
  148.9 0.0 collective-permute-done.8.refs_1_
  148.9 0.6 token_grad.9
  (3 shorter events, 0.1 us)
Async XLA Ops:
  0.6 44.0 %copy-start = (bf16[928,464]{1,0:T(8,128)(2,1)S(1)}, bf16[928,464]{1,0:T(8,128)(2,1)}, u32[]{:S(2)}) copy-start(bf16[928,464]{1,0:T(8,128)(2,1)} %up_ref.7) | copy-start | bytes 2583556
  0.6 44.0 %copy-start.1 = (bf16[464,928]{1,0:T(8,128)(2,1)S(1)}, bf16[464,928]{1,0:T(8,128)(2,1)}, u32[]{:S(2)}) copy-start(bf16[464,928]{1,0:T(8,128)(2,1)} %down_ref.3) | copy-start | bytes 2583556
  39.3 7.7 %collective-permute-start = (bf16[16,2,16,928]{3,2,1,0:T(8,128)(2,1)S(1)}, bf16[16,2,16,928]{3,2,1,0:T(8,128)(2,1)}, u32[]{:S(2)}, u32[]{:S(2)}) collective-permute-start(bf16[16,2,16,928]{3,2,1,0:T(8,128)(2,1)S(1)} %all_to_all.10.plane_ref), channel_id=1, source_target_pairs={{0,8},{8,0},{1,9},{9,1},{2,10},{10,2},{3,11},{11,3},{4,12},{12,4},... | collective-permute-start | bytes 2850824 | tf_op jit(solution)/shard_map/gather_tokens/ppermute | solution.py:205
  49.7 8.9 %collective-permute-start.4 = (bf16[2,464,128]{2,1,0:T(8,128)(2,1)S(1)}, bf16[2,464,128]{2,1,0:T(8,128)(2,1)S(1)}, u32[]{:S(2)}, u32[]{:S(2)}) collective-permute-start(bf16[2,464,128]{2,1,0:T(8,128)(2,1)S(1)} %get-tuple-element.33), channel_id=1, source_target_pairs={{0,64},{64,0},{1,65},{65,1},{2,66},{66,2},{3,67},{67,3},{4,68},{68... | collective-permute-start | bytes 712712 | tf_op jit(solution)/shard_map/row_sums/ppermute | solution.py:226
  52.3 11.4 %collective-permute-start.1 = (bf16[2,464,128]{2,1,0:T(8,128)(2,1)S(1)}, bf16[2,464,128]{2,1,0:T(8,128)(2,1)S(1)}, u32[]{:S(2)}, u32[]{:S(2)}) collective-permute-start(bf16[2,464,128]{2,1,0:T(8,128)(2,1)S(1)} %get-tuple-element.35), channel_id=1, source_target_pairs={{0,64},{64,0},{1,65},{65,1},{2,66},{66,2},{3,67},{67,3},{4,68},{68... | collective-permute-start | bytes 712712 | tf_op jit(solution)/shard_map/row_sums/ppermute | solution.py:226
  59.2 8.2 %collective-permute-start.5 = (bf16[464,128]{1,0:T(8,128)(2,1)S(1)}, bf16[464,128]{1,0:T(8,128)(2,1)S(1)}, u32[]{:S(2)}, u32[]{:S(2)}) collective-permute-start(bf16[464,128]{1,0:T(8,128)(2,1)S(1)} %get-tuple-element.24), channel_id=1, source_target_pairs={{0,128},{128,0},{1,129},{129,1},{2,130},{130,2},{3,131},{131,3},{4... | collective-permute-start | bytes 356360 | tf_op jit(solution)/shard_map/row_sums/ppermute | solution.py:232
  64.3 12.0 %collective-permute-start.2 = (bf16[464,128]{1,0:T(8,128)(2,1)S(1)}, bf16[464,128]{1,0:T(8,128)(2,1)S(1)}, u32[]{:S(2)}, u32[]{:S(2)}) collective-permute-start(bf16[464,128]{1,0:T(8,128)(2,1)S(1)} %get-tuple-element.22), channel_id=1, source_target_pairs={{0,128},{128,0},{1,129},{129,1},{2,130},{130,2},{3,131},{131,3},{4... | collective-permute-start | bytes 356360 | tf_op jit(solution)/shard_map/row_sums/ppermute | solution.py:232
  67.4 16.1 %collective-permute-start.6 = (bf16[464,128]{1,0:T(8,128)(2,1)S(1)}, bf16[464,128]{1,0:T(8,128)(2,1)S(1)}, u32[]{:S(2)}, u32[]{:S(2)}) collective-permute-start(bf16[464,128]{1,0:T(8,128)(2,1)S(1)} %row_sums.11), channel_id=1, source_target_pairs={{0,256},{256,0},{1,257},{257,1},{2,258},{258,2},{3,259},{259,3},{4... | collective-permute-start | bytes 356360 | tf_op jit(solution)/shard_map/row_sums/ppermute | solution.py:234
  76.4 21.0 %collective-permute-start.3 = (bf16[464,128]{1,0:T(8,128)(2,1)S(1)}, bf16[464,128]{1,0:T(8,128)(2,1)S(1)}, u32[]{:S(2)}, u32[]{:S(2)}) collective-permute-start(bf16[464,128]{1,0:T(8,128)(2,1)S(1)} %row_sums.9), channel_id=1, source_target_pairs={{0,256},{256,0},{1,257},{257,1},{2,258},{258,2},{3,259},{259,3},{4... | collective-permute-start | bytes 356360 | tf_op jit(solution)/shard_map/row_sums/ppermute | solution.py:234
  110.0 0.6 copy-start.4
  110.7 8.1 %collective-permute-start.7 = (bf16[256,928]{1,0:T(8,128)(2,1)S(1)}, bf16[256,928]{1,0:T(8,128)(2,1)S(1)}, u32[]{:S(2)}, u32[]{:S(2)}) collective-permute-start(bf16[256,928]{1,0:T(8,128)(2,1)S(1)} %get-tuple-element.25), channel_id=1, source_target_pairs={{0,8},{8,0},{1,9},{9,1},{2,10},{10,2},{3,11},{11,3},{4,12},{12,4},... | collective-permute-start | bytes 1425416 | tf_op jit(solution)/shard_map/token_grad/ppermute | solution.py:248
  118.0 5.6 %copy-start.5 = (bf16[464,128]{1,0:T(8,128)(2,1)S(1)}, bf16[464,128]{1,0:T(8,128)(2,1)}, u32[]{:S(2)}) copy-start(bf16[464,128]{1,0:T(8,128)(2,1)} %copy-done.4) | copy-start | bytes 356356
  118.0 27.2 %copy-start.2 = (bf16[512,928]{1,0:T(8,128)(2,1)S(1)}, bf16[512,928]{1,0:T(8,128)(2,1)}, u32[]{:S(2)}) copy-start(bf16[512,928]{1,0:T(8,128)(2,1)} %get-tuple-element.26.inputs_ref) | copy-start | bytes 2850820
  118.0 27.2 %copy-start.3 = (bf16[512,928]{1,0:T(8,128)(2,1)S(1)}, bf16[512,928]{1,0:T(8,128)(2,1)}, u32[]{:S(2)}) copy-start(bf16[512,928]{1,0:T(8,128)(2,1)} %get-tuple-element.27.upstream_ref) | copy-start | bytes 2850820
  119.7 14.2 %all-to-all-start.1 = ((bf16[16,16,928]{2,1,0:T(8,128)(2,1)}), bf16[16,16,928]{2,1,0:T(8,128)(2,1)S(1)}, u32[]{:S(2)}, u32[]{:S(2)}) async-start(bf16[16,16,928]{2,1,0:T(8,128)(2,1)} %bitcast.10), calls=%async_computation.1 | async-start | bytes 1048576 | tf_op jit(solution)/shard_map/token_grad/all_to_all | solution.py:196
  123.5 21.6 %collective-permute-start.9 = (bf16[464,128]{1,0:T(8,128)(2,1)S(1)}, bf16[464,128]{1,0:T(8,128)(2,1)S(1)}, u32[]{:S(2)}, u32[]{:S(2)}) collective-permute-start(bf16[464,128]{1,0:T(8,128)(2,1)S(1)} %copy-done.5), channel_id=1, source_target_pairs={{0,64},{64,0},{128,192},{192,128},{1,65},{65,1},{129,193},{193,129... | collective-permute-start | bytes 356360 | tf_op jit(solution)/shard_map/weight_grads/ppermute | solution.py:269
  125.4 19.7 %collective-permute-start.10 = (bf16[464,128]{1,0:T(8,128)(2,1)S(1)}, bf16[464,128]{1,0:T(8,128)(2,1)S(1)}, u32[]{:S(2)}, u32[]{:S(2)}) collective-permute-start(bf16[464,128]{1,0:T(8,128)(2,1)S(1)} %copy-done.5), channel_id=1, source_target_pairs={{0,128},{64,192},{128,0},{192,64},{1,129},{65,193},{129,1},{193,65... | collective-permute-start | bytes 356360 | tf_op jit(solution)/shard_map/weight_grads/ppermute | solution.py:269
  127.8 17.3 %collective-permute-start.11 = (bf16[464,128]{1,0:T(8,128)(2,1)S(1)}, bf16[464,128]{1,0:T(8,128)(2,1)}, u32[]{:S(2)}, u32[]{:S(2)}) collective-permute-start(bf16[464,128]{1,0:T(8,128)(2,1)S(1)} %copy-done.5), channel_id=1, source_target_pairs={{0,192},{64,128},{128,64},{192,0},{1,193},{65,129},{129,65},{193,1... | collective-permute-start | bytes 356360 | tf_op jit(solution)/shard_map/weight_grads/ppermute | solution.py:269
  134.0 14.9 %collective-permute-start.8 = (bf16[8,928]{1,0:T(8,128)(2,1)S(1)}, bf16[8,928]{1,0:T(8,128)(2,1)S(1)}, u32[]{:S(2)}, u32[]{:S(2)}) collective-permute-start(bf16[8,928]{1,0:T(8,128)(2,1)S(1)} %get-tuple-element.39), channel_id=1, source_target_pairs={{0,1},{1,0},{2,3},{3,2},{4,5},{5,4},{6,7},{7,6},{8,9},{9,8},{10,11... | collective-permute-start | bytes 44552 | tf_op jit(solution)/shard_map/token_grad/ppermute | solution.py:264

commit v6 on v5

--- a/solution.py
+++ b/solution.py
@@ -59,45 +59,47 @@
     )(scalars, *operands)
 
 
-def partials_kernel(plane_ref, up_ref, down_ref, *refs):
-    parts_ref, inputs_ref, upstream_ref = refs[-3:]
-    for array, (weight_ref, rows_ref) in enumerate(
-        ((up_ref, inputs_ref), (down_ref, upstream_ref))
-    ):
+def partials_kernel(arrays, plane_ref, *refs):
+    weights, outs = refs[: len(arrays)], refs[-2 * len(arrays) :]
+    for i, array in enumerate(arrays):
         rows = plane_ref[:, array].reshape(256, -1)
-        rows_ref[...] = rows
+        outs[2 * i + 1][...] = rows
         both = lax.dot_general(
-            weight_ref[...],
+            weights[i][...],
             rows,
             (((array,), (1,)), ((), ())),
             preferred_element_type=jnp.float32,
         ).astype(jnp.bfloat16)
         for block in range(2):
-            parts_ref[block, array] = both[:, 128 * block : 128 * block + 128]
-
-
-def partials(half, plane, up_weight, down_weight, *so_far):
-    features, hidden = up_weight.shape
-    return pl.pallas_call(
-        partials_kernel,
+            outs[2 * i][block] = both[:, 128 * block : 128 * block + 128]
+
+
+def partials(half, arrays, plane, weights, so_far=()):
+    features = plane.shape[3]
+    hidden = weights[0].size // features
+    first = 1 + len(weights)
+    return pl.pallas_call(
+        functools.partial(partials_kernel, arrays),
         grid=(1,),
         out_shape=[
-            jax.ShapeDtypeStruct((4, 2, hidden, 128), jnp.bfloat16),
+            jax.ShapeDtypeStruct((4, hidden, 128), jnp.bfloat16),
             pltpu.HBM((512, features), jnp.bfloat16),
-            pltpu.HBM((512, features), jnp.bfloat16),
-        ],
-        in_specs=[VMEM] * 3 + [ANY] * len(so_far),
+        ]
+        * len(arrays),
+        in_specs=[VMEM] * first + [ANY] * len(so_far),
         out_specs=[
-            pl.BlockSpec((2, 2, hidden, 128), lambda i: (half, 0, 0, 0)),
+            pl.BlockSpec((2, hidden, 128), lambda i: (half, 0, 0)),
             pl.BlockSpec((256, features), lambda i: (half, 0)),
-            pl.BlockSpec((256, features), lambda i: (half, 0)),
-        ],
-        input_output_aliases={3 + i: i for i in range(len(so_far))},
+        ]
+        * len(arrays),
+        input_output_aliases={first + i: i for i in range(len(so_far))},
         compiler_params=PARAMS,
         cost_estimate=pl.CostEstimate(
-            flops=2 * 512 * features * hidden, bytes_accessed=4 << 20, transcendentals=0
+            flops=len(arrays) * 512 * features * hidden,
+            bytes_accessed=len(arrays) << 21,
+            transcendentals=0,
         ),
-    )(plane, up_weight, down_weight, *so_far)
+    )(plane, *weights, *so_far)
 
 
 def halve_kernel(bits_ref, staying_ref, arrived_ref, leaving_out, staying_out):
@@ -204,15 +206,17 @@
         own = exchange(copies, ("x", "y"))
         other = lax.ppermute(own, "core", SWAP)
     with jax.named_scope("row_sums"):
-        first = partials(0, own, up_weight, down_weight)
-        parts, inputs, upstream = partials(1, other, up_weight, down_weight, *first)
+        weights = (up_weight, down_weight)
+        begun = partials(0, (0, 1), own, weights)
+        pre_parts, inputs = partials(1, (0,), other, weights[:1], begun[:2])
+        grad_parts, upstream = partials(1, (1,), other, weights[1:], begun[2:])
         near, next_to = lax.axis_index("zb"), lax.axis_index("zc")
         bits = jnp.stack([near, next_to])
-        pair = parts.reshape(2, 2, 2, hidden, 128)
         sums = []
-        for array in range(2):
+        for parts in (pre_parts, grad_parts):
+            pair = parts.reshape(2, 2, hidden, 128)
             leaving, staying = (
-                lax.dynamic_index_in_dim(pair[:, :, array], side, 1, keepdims=False)
+                lax.dynamic_index_in_dim(pair, side, 1, keepdims=False)
                 for side in (1 - next_to, next_to)
             )
             leaving, staying = with_scalars(
@@ -241,10 +245,12 @@
         active = (preact * cdf).astype(jnp.bfloat16)
     with jax.named_scope("token_grad"):
         half = jax.ShapeDtypeStruct((256, features), jnp.bfloat16)
-        leaving, active = in_order(
-            functools.partial(token_grad_kernel, 2), half, hidden_grad, up_weight, active
-        )
-        staying = on_core(functools.partial(token_grad_kernel, 0), half, hidden_grad, up_weight)
+        leaving = on_core(
+            functools.partial(token_grad_kernel, 2), half, hidden_grad, up_weight
+        )
+        staying, active = in_order(
+            functools.partial(token_grad_kernel, 0), half, hidden_grad, up_weight, active
+        )
         arrived = lax.ppermute(leaving, "core", SWAP)
         chip_sum = on_core(add_kernel, half, staying, arrived)
         plane_sum = on_core(

time: 150 us -> 148 us (0.987)
    ppermute x2, waiting for transfers between devices: 0.01 us -> 1.81 us  [on_device(): lax.ppermute(leaving, 'zb', SWAP)]
    pallas_call x2 -> x3, Pallas kernels: 3.94 us -> 3.53 us  [partials(): pl.pallas_call(functools.partial(partials_kernel, arrays), grid=(1,), out...]
where the time goes in v6:
time: 148 us
  starting transfers between devices  62.8 us (42%)
  blocking collectives  49.8 us (34%)
  waiting for transfers between devices  20.3 us (14%)
  Pallas kernels  10.6 us (7%)
  local copies, waits for them, and re-layouts  2.32 us (2%)
    all_to_all x1, blocking collectives, exchange(): return lax.all_to_all(blocks, axis, split_axis=0, concat_axis=0, tiled=True)  21.3 us
    all_gather x1, blocking collectives, on_device(): lax.all_gather(jnp.stack([tokens, out_grad]), 'far', axis=1, tiled=True)  16.4 us
    ppermute x2, starting transfers between devices, on_device(): theirs = lax.ppermute(mine, 'za', SWAP)  15.7 us
    ppermute x2, waiting for transfers between devices, on_device(): theirs = lax.ppermute(mine, 'za', SWAP)  12.6 us
    all_gather x1, blocking collectives, row_gather(): return lax.all_gather(part[None], ('zb', 'zc'), axis=0, tiled=True)  12.1 us
    ppermute x1, starting transfers between devices, on_device(): lax.ppermute(theirs, 'far', SWAP)  11 us
    ppermute x3, starting transfers between devices, on_device(): lax.ppermute(active, ('zb', 'zc'), [(i, i ^ k) for i in range(4)])  9.27 us
    ppermute x2, starting transfers between devices, on_device(): lax.ppermute(leaving, 'zb', SWAP)  6.22 us
  transfers between devices with their start and end apart: 13, of which 6 were waited for; matrix products, arithmetic and copies ran while one was open for 0% of the time, Pallas kernels for 5%

profile of v6, /device:TPU:1, one launch (start us, length us, event | category | flops | bytes accessed | tf_op | source)
XLA Modules:
  0.0 147.8 jit_solution(10986300955599010685)
XLA Ops:
  0.6 0.0 copy-start
  0.6 0.8 pad_maximum_fusion
  1.5 16.4 %all_gather.6 = bf16[2,16,928]{2,1,0:T(8,128)(2,1)S(1)} all-gather(bf16[2,8,928]{2,1,0:T(8,128)(2,1)S(1)} %pad_maximum_fusion), channel_id=1, replica_groups=mesh['za'=2,'zb'=2,'zc'=2,'x'=4,'core'=2,'y'=4,'far'=2] {'far'}, dimensions={1}, use_global_device_ids=true | all-gather | bytes 89088 | tf_op jit(solution)/shard_map/gather_tokens/all_gather | solution.py:204
  17.9 0.1 broadcast_in_dim.4
  18.0 21.3 %all_to_all.10.plane_ref = bf16[16,2,16,928]{3,2,1,0:T(8,128)(2,1)S(1)} all-to-all(bf16[16,2,16,928]{3,2,1,0:T(8,128)(2,1)S(1)} %broadcast_in_dim.4), channel_id=1, replica_groups=mesh['za'=2,'zb'=2,'zc'=2,'x'=4,'core'=2,'y'=4,'far'=2] {'x','y'}, dimensions={0} | all-to-all | bytes 1900544 | tf_op jit(solution)/shard_map/gather_tokens/all_to_all | solution.py:198
  39.3 5.3 %collective-permute-start = (bf16[16,2,16,928]{3,2,1,0:T(8,128)(2,1)S(1)}, bf16[16,2,16,928]{3,2,1,0:T(8,128)(2,1)S(1)}, u32[]{:S(2)}, u32[]{:S(2)}) collective-permute-start(bf16[16,2,16,928]{3,2,1,0:T(8,128)(2,1)S(1)} %all_to_all.10.plane_ref), channel_id=1, source_target_pairs={{0,8},{8,0},{1,9},{9,1},{2,10},{10,2},{3,11},{11,3},{4,12},{12,4},... | collective-permute-start | bytes 2850824 | tf_op jit(solution)/shard_map/gather_tokens/ppermute | solution.py:207
  44.5 0.0 copy-done
  44.5 0.0 copy-start.1
  44.6 1.2 copy-done.1
  45.7 1.4 row_sums.7
  47.1 0.0 collective-permute-done.plane_ref
  47.1 1.1 row_sums.8
  48.2 2.5 %collective-permute-start.1 = (bf16[2,464,128]{2,1,0:T(8,128)(2,1)S(1)}, bf16[2,464,128]{2,1,0:T(8,128)(2,1)S(1)}, u32[]{:S(2)}, u32[]{:S(2)}) collective-permute-start(bf16[2,464,128]{2,1,0:T(8,128)(2,1)S(1)} %get-tuple-element.37), channel_id=1, source_target_pairs={{0,64},{64,0},{1,65},{65,1},{2,66},{66,2},{3,67},{67,3},{4,68},{68... | collective-permute-start | bytes 712712 | tf_op jit(solution)/shard_map/row_sums/ppermute | solution.py:230
  50.8 1.1 row_sums.11
  51.9 2.8 %collective-permute-start.4 = (bf16[2,464,128]{2,1,0:T(8,128)(2,1)S(1)}, bf16[2,464,128]{2,1,0:T(8,128)(2,1)S(1)}, u32[]{:S(2)}, u32[]{:S(2)}) collective-permute-start(bf16[2,464,128]{2,1,0:T(8,128)(2,1)S(1)} %get-tuple-element.35), channel_id=1, source_target_pairs={{0,64},{64,0},{1,65},{65,1},{2,66},{66,2},{3,67},{67,3},{4,68},{68... | collective-permute-start | bytes 712712 | tf_op jit(solution)/shard_map/row_sums/ppermute | solution.py:230
  54.7 0.1 pad_add_fusion.bits_ref
  54.7 2.7 %collective-permute-done.1.arrived_ref = bf16[2,464,128]{2,1,0:T(8,128)(2,1)S(1)} collective-permute-done((bf16[2,464,128]{2,1,0:T(8,128)(2,1)S(1)}, bf16[2,464,128]{2,1,0:T(8,128)(2,1)S(1)}, u32[]{:S(2)}, u32[]{:S(2)}) %collective-permute-start.1) | collective-permute-done | bytes 237600 | tf_op jit(solution)/shard_map/row_sums/ppermute | solution.py:230
  57.5 0.6 row_sums.9
  58.1 3.1 %collective-permute-start.2 = (bf16[464,128]{1,0:T(8,128)(2,1)S(1)}, bf16[464,128]{1,0:T(8,128)(2,1)S(1)}, u32[]{:S(2)}, u32[]{:S(2)}) collective-permute-start(bf16[464,128]{1,0:T(8,128)(2,1)S(1)} %get-tuple-element.23), channel_id=1, source_target_pairs={{0,128},{128,0},{1,129},{129,1},{2,130},{130,2},{3,131},{131,3},{4... | collective-permute-start | bytes 356360 | tf_op jit(solution)/shard_map/row_sums/ppermute | solution.py:236
  61.2 1.4 collective-permute-done.4.arrived_ref
  62.6 0.6 row_sums.12
  63.2 3.1 %collective-permute-start.5 = (bf16[464,128]{1,0:T(8,128)(2,1)S(1)}, bf16[464,128]{1,0:T(8,128)(2,1)S(1)}, u32[]{:S(2)}, u32[]{:S(2)}) collective-permute-start(bf16[464,128]{1,0:T(8,128)(2,1)S(1)} %get-tuple-element.28), channel_id=1, source_target_pairs={{0,128},{128,0},{1,129},{129,1},{2,130},{130,2},{3,131},{131,3},{4... | collective-permute-start | bytes 356360 | tf_op jit(solution)/shard_map/row_sums/ppermute | solution.py:236
  66.3 1.8 %collective-permute-done.2.refs_1_ = bf16[464,128]{1,0:T(8,128)(2,1)S(1)} collective-permute-done((bf16[464,128]{1,0:T(8,128)(2,1)S(1)}, bf16[464,128]{1,0:T(8,128)(2,1)S(1)}, u32[]{:S(2)}, u32[]{:S(2)}) %collective-permute-start.2) | collective-permute-done | bytes 118816 | tf_op jit(solution)/shard_map/row_sums/ppermute | solution.py:236
  68.1 7.1 %collective-permute-start.3 = (bf16[464,128]{1,0:T(8,128)(2,1)S(1)}, bf16[464,128]{1,0:T(8,128)(2,1)S(1)}, u32[]{:S(2)}, u32[]{:S(2)}) collective-permute-start(bf16[464,128]{1,0:T(8,128)(2,1)S(1)} %row_sums.10), channel_id=1, source_target_pairs={{0,256},{256,0},{1,257},{257,1},{2,258},{258,2},{3,259},{259,3},{4... | collective-permute-start | bytes 356360 | tf_op jit(solution)/shard_map/row_sums/ppermute | solution.py:238
  75.2 0.0 collective-permute-done.5.refs_1_
  75.2 8.6 %collective-permute-start.6 = (bf16[464,128]{1,0:T(8,128)(2,1)S(1)}, bf16[464,128]{1,0:T(8,128)(2,1)S(1)}, u32[]{:S(2)}, u32[]{:S(2)}) collective-permute-start(bf16[464,128]{1,0:T(8,128)(2,1)S(1)} %row_sums.13), channel_id=1, source_target_pairs={{0,256},{256,0},{1,257},{257,1},{2,258},{258,2},{3,259},{259,3},{4... | collective-permute-start | bytes 356360 | tf_op jit(solution)/shard_map/row_sums/ppermute | solution.py:238
  83.9 0.0 collective-permute-done.3
  83.9 12.6 %collective-permute-done.6 = bf16[464,128]{1,0:T(8,128)(2,1)S(1)} collective-permute-done((bf16[464,128]{1,0:T(8,128)(2,1)S(1)}, bf16[464,128]{1,0:T(8,128)(2,1)S(1)}, u32[]{:S(2)}, u32[]{:S(2)}) %collective-permute-start.6) | collective-permute-done | bytes 118816 | tf_op jit(solution)/shard_map/row_sums/ppermute | solution.py:238
  96.5 0.2 multiply_convert_fusion
  96.6 12.1 %all-gather = bf16[1856,128]{1,0:T(8,128)(2,1)S(1)} all-gather(bf16[464,128]{1,0:T(8,128)(2,1)S(1)} %get-tuple-element.40), channel_id=2, replica_groups=mesh['za'=2,'zb'=2,'zc'=2,'x'=4,'core'=2,'y'=4,'far'=2] {'zb','zc'}, dimensions={0}, use_global_device_ids=true | all-gather | bytes 593920 | tf_op jit(solution)/shard_map/activate/all_gather | solution.py:201
  108.8 0.7 token_grad.6
  109.5 6.2 %collective-permute-start.7 = (bf16[256,928]{1,0:T(8,128)(2,1)S(1)}, bf16[256,928]{1,0:T(8,128)(2,1)S(1)}, u32[]{:S(2)}, u32[]{:S(2)}) collective-permute-start(bf16[256,928]{1,0:T(8,128)(2,1)S(1)} %token_grad.6), channel_id=1, source_target_pairs={{0,8},{8,0},{1,9},{9,1},{2,10},{10,2},{3,11},{11,3},{4,12},{12,4},... | collective-permute-start | bytes 1425416 | tf_op jit(solution)/shard_map/token_grad/ppermute | solution.py:254
  115.7 0.7 token_grad.5
  116.4 0.0 copy-start.4
  116.4 0.0 copy-start.2
  116.4 0.0 copy-start.3
  116.4 0.8 collective-permute-done.7.refs_1_
  117.2 0.9 token_grad.7
  118.1 0.0 copy-done.4
  118.1 3.8 %all-to-all-start.1 = ((bf16[16,16,928]{2,1,0:T(8,128)(2,1)}), bf16[16,16,928]{2,1,0:T(8,128)(2,1)S(1)}, u32[]{:S(2)}, u32[]{:S(2)}) async-start(bf16[16,16,928]{2,1,0:T(8,128)(2,1)} %bitcast.11), calls=%async_computation.1 | async-start | bytes 1048576 | tf_op jit(solution)/shard_map/token_grad/all_to_all | solution.py:198
  122.0 1.9 %collective-permute-start.11 = (bf16[464,128]{1,0:T(8,128)(2,1)}, bf16[464,128]{1,0:T(8,128)(2,1)S(1)}, u32[]{:S(2)}, u32[]{:S(2)}) collective-permute-start(bf16[464,128]{1,0:T(8,128)(2,1)} %copy-done.4), channel_id=1, source_target_pairs={{0,192},{64,128},{128,64},{192,0},{1,193},{65,129},{129,65},{193,1... | collective-permute-start | bytes 356360 | tf_op jit(solution)/shard_map/weight_grads/ppermute | solution.py:275
  123.9 2.3 %collective-permute-start.10 = (bf16[464,128]{1,0:T(8,128)(2,1)}, bf16[464,128]{1,0:T(8,128)(2,1)S(1)}, u32[]{:S(2)}, u32[]{:S(2)}) collective-permute-start(bf16[464,128]{1,0:T(8,128)(2,1)} %copy-done.4), channel_id=1, source_target_pairs={{0,128},{64,192},{128,0},{192,64},{1,129},{65,193},{129,1},{193,65... | collective-permute-start | bytes 356360 | tf_op jit(solution)/shard_map/weight_grads/ppermute | solution.py:275
  126.2 5.0 %collective-permute-start.9 = (bf16[464,128]{1,0:T(8,128)(2,1)}, bf16[464,128]{1,0:T(8,128)(2,1)S(1)}, u32[]{:S(2)}, u32[]{:S(2)}) collective-permute-start(bf16[464,128]{1,0:T(8,128)(2,1)} %copy-done.4), channel_id=1, source_target_pairs={{0,64},{64,0},{128,192},{192,128},{1,65},{65,1},{129,193},{193,129... | collective-permute-start | bytes 356360 | tf_op jit(solution)/shard_map/weight_grads/ppermute | solution.py:275
  131.3 1.0 all-to-all-done.1.blocks_ref
  132.3 0.1 token_grad.8
  132.4 11.0 %collective-permute-start.8 = (bf16[8,928]{1,0:T(8,128)(2,1)S(1)}, bf16[8,928]{1,0:T(8,128)(2,1)S(1)}, u32[]{:S(2)}, u32[]{:S(2)}) collective-permute-start(bf16[8,928]{1,0:T(8,128)(2,1)S(1)} %get-tuple-element.41), channel_id=1, source_target_pairs={{0,1},{1,0},{2,3},{3,2},{4,5},{5,4},{6,7},{7,6},{8,9},{9,8},{10,11... | collective-permute-start | bytes 44552 | tf_op jit(solution)/shard_map/token_grad/ppermute | solution.py:270
  143.5 0.0 collective-permute-done.11.refs_3_
  143.5 0.0 collective-permute-done.10.refs_2_
  143.5 0.0 collective-permute-done.9.refs_1_
  143.5 0.0 copy-done.2
  143.5 0.0 copy-done.3
  143.5 0.0 copy-start.5
  143.5 0.9 copy-done.5
  144.4 2.8 %weight_grads.1 = (f32[928,464]{1,0:T(8,128)}, f32[464,928]{1,0:T(8,128)}) custom-call(s32[1]{0:T(128)} %bitcast.12.place_ref, bf16[512,928]{1,0:T(8,128)(2,1)S(1)} %copy-done.2, bf16[512,928]{1,0:T(8,128)(2,1)S(1)} %copy-done.3, bf16[4,464,128]{2,1,0:T(8,128)(2,1)S(1)} %bitcast.27, bf16[464,128]{1,0:T(8,128)(2,1)S(1)} %copy-done.5, ...), custom_call_target="tpu_custom_call" | custom-call | flops 881852416 | bytes 8388608 | tf_op jit(solution)/shard_map/weight_grads/pallas_call | solution.py:175
  147.2 0.0 collective-permute-done.8.refs_1_
  147.2 0.6 token_grad.9
  (5 shorter events, 0.2 us)
Async XLA Ops:
  0.6 43.9 %copy-start = (bf16[928,464]{1,0:T(8,128)(2,1)S(1)}, bf16[928,464]{1,0:T(8,128)(2,1)}, u32[]{:S(2)}) copy-start(bf16[928,464]{1,0:T(8,128)(2,1)} %up_ref.3) | copy-start | bytes 2583556
  39.3 7.8 %collective-permute-start = (bf16[16,2,16,928]{3,2,1,0:T(8,128)(2,1)S(1)}, bf16[16,2,16,928]{3,2,1,0:T(8,128)(2,1)S(1)}, u32[]{:S(2)}, u32[]{:S(2)}) collective-permute-start(bf16[16,2,16,928]{3,2,1,0:T(8,128)(2,1)S(1)} %all_to_all.10.plane_ref), channel_id=1, source_target_pairs={{0,8},{8,0},{1,9},{9,1},{2,10},{10,2},{3,11},{11,3},{4,12},{12,4},... | collective-permute-start | bytes 2850824 | tf_op jit(solution)/shard_map/gather_tokens/ppermute | solution.py:207
  44.5 1.2 copy-start.1
  48.2 9.2 %collective-permute-start.1 = (bf16[2,464,128]{2,1,0:T(8,128)(2,1)S(1)}, bf16[2,464,128]{2,1,0:T(8,128)(2,1)S(1)}, u32[]{:S(2)}, u32[]{:S(2)}) collective-permute-start(bf16[2,464,128]{2,1,0:T(8,128)(2,1)S(1)} %get-tuple-element.37), channel_id=1, source_target_pairs={{0,64},{64,0},{1,65},{65,1},{2,66},{66,2},{3,67},{67,3},{4,68},{68... | collective-permute-start | bytes 712712 | tf_op jit(solution)/shard_map/row_sums/ppermute | solution.py:230
  51.9 10.7 %collective-permute-start.4 = (bf16[2,464,128]{2,1,0:T(8,128)(2,1)S(1)}, bf16[2,464,128]{2,1,0:T(8,128)(2,1)S(1)}, u32[]{:S(2)}, u32[]{:S(2)}) collective-permute-start(bf16[2,464,128]{2,1,0:T(8,128)(2,1)S(1)} %get-tuple-element.35), channel_id=1, source_target_pairs={{0,64},{64,0},{1,65},{65,1},{2,66},{66,2},{3,67},{67,3},{4,68},{68... | collective-permute-start | bytes 712712 | tf_op jit(solution)/shard_map/row_sums/ppermute | solution.py:230
  58.1 10.0 %collective-permute-start.2 = (bf16[464,128]{1,0:T(8,128)(2,1)S(1)}, bf16[464,128]{1,0:T(8,128)(2,1)S(1)}, u32[]{:S(2)}, u32[]{:S(2)}) collective-permute-start(bf16[464,128]{1,0:T(8,128)(2,1)S(1)} %get-tuple-element.23), channel_id=1, source_target_pairs={{0,128},{128,0},{1,129},{129,1},{2,130},{130,2},{3,131},{131,3},{4... | collective-permute-start | bytes 356360 | tf_op jit(solution)/shard_map/row_sums/ppermute | solution.py:236
  63.2 12.0 %collective-permute-start.5 = (bf16[464,128]{1,0:T(8,128)(2,1)S(1)}, bf16[464,128]{1,0:T(8,128)(2,1)S(1)}, u32[]{:S(2)}, u32[]{:S(2)}) collective-permute-start(bf16[464,128]{1,0:T(8,128)(2,1)S(1)} %get-tuple-element.28), channel_id=1, source_target_pairs={{0,128},{128,0},{1,129},{129,1},{2,130},{130,2},{3,131},{131,3},{4... | collective-permute-start | bytes 356360 | tf_op jit(solution)/shard_map/row_sums/ppermute | solution.py:236
  68.1 15.8 %collective-permute-start.3 = (bf16[464,128]{1,0:T(8,128)(2,1)S(1)}, bf16[464,128]{1,0:T(8,128)(2,1)S(1)}, u32[]{:S(2)}, u32[]{:S(2)}) collective-permute-start(bf16[464,128]{1,0:T(8,128)(2,1)S(1)} %row_sums.10), channel_id=1, source_target_pairs={{0,256},{256,0},{1,257},{257,1},{2,258},{258,2},{3,259},{259,3},{4... | collective-permute-start | bytes 356360 | tf_op jit(solution)/shard_map/row_sums/ppermute | solution.py:238
  75.2 21.2 %collective-permute-start.6 = (bf16[464,128]{1,0:T(8,128)(2,1)S(1)}, bf16[464,128]{1,0:T(8,128)(2,1)S(1)}, u32[]{:S(2)}, u32[]{:S(2)}) collective-permute-start(bf16[464,128]{1,0:T(8,128)(2,1)S(1)} %row_sums.13), channel_id=1, source_target_pairs={{0,256},{256,0},{1,257},{257,1},{2,258},{258,2},{3,259},{259,3},{4... | collective-permute-start | bytes 356360 | tf_op jit(solution)/shard_map/row_sums/ppermute | solution.py:238
  109.5 7.7 %collective-permute-start.7 = (bf16[256,928]{1,0:T(8,128)(2,1)S(1)}, bf16[256,928]{1,0:T(8,128)(2,1)S(1)}, u32[]{:S(2)}, u32[]{:S(2)}) collective-permute-start(bf16[256,928]{1,0:T(8,128)(2,1)S(1)} %token_grad.6), channel_id=1, source_target_pairs={{0,8},{8,0},{1,9},{9,1},{2,10},{10,2},{3,11},{11,3},{4,12},{12,4},... | collective-permute-start | bytes 1425416 | tf_op jit(solution)/shard_map/token_grad/ppermute | solution.py:254
  116.4 1.8 %copy-start.4 = (bf16[464,128]{1,0:T(8,128)(2,1)}, bf16[464,128]{1,0:T(8,128)(2,1)S(1)}, u32[]{:S(2)}) copy-start(bf16[464,128]{1,0:T(8,128)(2,1)S(1)} %get-tuple-element.32.refs_0_) | copy-start | bytes 356356
  116.4 27.1 %copy-start.2 = (bf16[512,928]{1,0:T(8,128)(2,1)S(1)}, bf16[512,928]{1,0:T(8,128)(2,1)}, u32[]{:S(2)}) copy-start(bf16[512,928]{1,0:T(8,128)(2,1)} %get-tuple-element.30.inputs_ref) | copy-start | bytes 2850820
  116.4 27.1 %copy-start.3 = (bf16[512,928]{1,0:T(8,128)(2,1)S(1)}, bf16[512,928]{1,0:T(8,128)(2,1)}, u32[]{:S(2)}) copy-start(bf16[512,928]{1,0:T(8,128)(2,1)} %get-tuple-element.31.upstream_ref) | copy-start | bytes 2850820
  118.1 14.2 %all-to-all-start.1 = ((bf16[16,16,928]{2,1,0:T(8,128)(2,1)}), bf16[16,16,928]{2,1,0:T(8,128)(2,1)S(1)}, u32[]{:S(2)}, u32[]{:S(2)}) async-start(bf16[16,16,928]{2,1,0:T(8,128)(2,1)} %bitcast.11), calls=%async_computation.1 | async-start | bytes 1048576 | tf_op jit(solution)/shard_map/token_grad/all_to_all | solution.py:198
  122.0 21.5 %collective-permute-start.11 = (bf16[464,128]{1,0:T(8,128)(2,1)}, bf16[464,128]{1,0:T(8,128)(2,1)S(1)}, u32[]{:S(2)}, u32[]{:S(2)}) collective-permute-start(bf16[464,128]{1,0:T(8,128)(2,1)} %copy-done.4), channel_id=1, source_target_pairs={{0,192},{64,128},{128,64},{192,0},{1,193},{65,129},{129,65},{193,1... | collective-permute-start | bytes 356360 | tf_op jit(solution)/shard_map/weight_grads/ppermute | solution.py:275
  123.9 19.6 %collective-permute-start.10 = (bf16[464,128]{1,0:T(8,128)(2,1)}, bf16[464,128]{1,0:T(8,128)(2,1)S(1)}, u32[]{:S(2)}, u32[]{:S(2)}) collective-permute-start(bf16[464,128]{1,0:T(8,128)(2,1)} %copy-done.4), channel_id=1, source_target_pairs={{0,128},{64,192},{128,0},{192,64},{1,129},{65,193},{129,1},{193,65... | collective-permute-start | bytes 356360 | tf_op jit(solution)/shard_map/weight_grads/ppermute | solution.py:275
  126.2 17.2 %collective-permute-start.9 = (bf16[464,128]{1,0:T(8,128)(2,1)}, bf16[464,128]{1,0:T(8,128)(2,1)S(1)}, u32[]{:S(2)}, u32[]{:S(2)}) collective-permute-start(bf16[464,128]{1,0:T(8,128)(2,1)} %copy-done.4), channel_id=1, source_target_pairs={{0,64},{64,0},{128,192},{192,128},{1,65},{65,1},{129,193},{193,129... | collective-permute-start | bytes 356360 | tf_op jit(solution)/shard_map/weight_grads/ppermute | solution.py:275
  132.4 14.8 %collective-permute-start.8 = (bf16[8,928]{1,0:T(8,128)(2,1)S(1)}, bf16[8,928]{1,0:T(8,128)(2,1)S(1)}, u32[]{:S(2)}, u32[]{:S(2)}) collective-permute-start(bf16[8,928]{1,0:T(8,128)(2,1)S(1)} %get-tuple-element.41), channel_id=1, source_target_pairs={{0,1},{1,0},{2,3},{3,2},{4,5},{5,4},{6,7},{7,6},{8,9},{9,8},{10,11... | collective-permute-start | bytes 44552 | tf_op jit(solution)/shard_map/token_grad/ppermute | solution.py:270
  143.5 0.9 copy-start.5

commit v7 on v6

--- a/solution.py
+++ b/solution.py
@@ -120,11 +120,14 @@
         ).astype(jnp.bfloat16)
 
 
-def total_kernel(blocks_ref, out_ref):
+def split_total_kernel(far_ref, blocks_ref, mine_ref, theirs_ref):
     acc = blocks_ref[0].astype(jnp.float32)
     for i in range(1, blocks_ref.shape[0]):
         acc = acc + blocks_ref[i].astype(jnp.float32)
-    out_ref[...] = acc.astype(jnp.bfloat16)
+    rows = mine_ref.shape[0]
+    low, high, near = acc[:rows], acc[rows:], far_ref[0] == 0
+    mine_ref[...] = jnp.where(near, low, high)
+    theirs_ref[...] = jnp.where(near, high, low).astype(jnp.bfloat16)
 
 
 def add_kernel(*refs):
@@ -253,15 +256,14 @@
         )
         arrived = lax.ppermute(leaving, "core", SWAP)
         chip_sum = on_core(add_kernel, half, staying, arrived)
-        plane_sum = on_core(
-            total_kernel,
-            jax.ShapeDtypeStruct((2 * rows, features), jnp.bfloat16),
+        mine, theirs = with_scalars(
+            split_total_kernel,
+            [
+                jax.ShapeDtypeStruct((rows, features), jnp.float32),
+                jax.ShapeDtypeStruct((rows, features), jnp.bfloat16),
+            ],
+            lax.axis_index("far").reshape(1),
             exchange(chip_sum.reshape(16, -1, features), ("x", "y")),
-        )
-        far = lax.axis_index("far")
-        mine, theirs = (
-            lax.dynamic_slice_in_dim(plane_sum, rows * side, rows, axis=0)
-            for side in (far, 1 - far)
         )
         token_grad = on_core(
             add_kernel,

time: 148 us -> 148 us (level)
  no operation moved by 1% of the time
where the time goes in v7:
time: 148 us
  starting transfers between devices  62.8 us (42%)
  blocking collectives  49.8 us (34%)
  waiting for transfers between devices  20.3 us (14%)
  Pallas kernels  10.6 us (7%)
  local copies, waits for them, and re-layouts  2.31 us (2%)
    all_to_all x1, blocking collectives, exchange(): return lax.all_to_all(blocks, axis, split_axis=0, concat_axis=0, tiled=True)  21.3 us
    all_gather x1, blocking collectives, on_device(): lax.all_gather(jnp.stack([tokens, out_grad]), 'far', axis=1, tiled=True)  16.4 us
    ppermute x2, starting transfers between devices, on_device(): theirs = lax.ppermute(mine, 'za', SWAP)  15.7 us
    ppermute x2, waiting for transfers between devices, on_device(): theirs = lax.ppermute(mine, 'za', SWAP)  12.6 us
    all_gather x1, blocking collectives, row_gather(): return lax.all_gather(part[None], ('zb', 'zc'), axis=0, tiled=True)  12.1 us
    ppermute x1, starting transfers between devices, on_device(): lax.ppermute(theirs, 'far', SWAP)  11 us
    ppermute x3, starting transfers between devices, on_device(): lax.ppermute(active, ('zb', 'zc'), [(i, i ^ k) for i in range(4)])  9.27 us
    ppermute x2, starting transfers between devices, on_device(): lax.ppermute(leaving, 'zb', SWAP)  6.22 us
  transfers between devices with their start and end apart: 13, of which 6 were waited for; matrix products, arithmetic and copies ran while one was open for 0% of the time, Pallas kernels for 5%

profile of v7, /device:TPU:1, one launch (start us, length us, event | category | flops | bytes accessed | tf_op | source)
XLA Modules:
  0.0 147.8 jit_solution(2415112370748740374)
XLA Ops:
  0.6 0.0 copy-start
  0.6 0.8 pad_maximum_fusion
  1.5 16.4 %all_gather.6 = bf16[2,16,928]{2,1,0:T(8,128)(2,1)S(1)} all-gather(bf16[2,8,928]{2,1,0:T(8,128)(2,1)S(1)} %pad_maximum_fusion), channel_id=1, replica_groups=mesh['za'=2,'zb'=2,'zc'=2,'x'=4,'core'=2,'y'=4,'far'=2] {'far'}, dimensions={1}, use_global_device_ids=true | all-gather | bytes 89088 | tf_op jit(solution)/shard_map/gather_tokens/all_gather | solution.py:207
  17.9 0.1 broadcast_in_dim.4
  18.0 21.3 %all_to_all.10.plane_ref = bf16[16,2,16,928]{3,2,1,0:T(8,128)(2,1)S(1)} all-to-all(bf16[16,2,16,928]{3,2,1,0:T(8,128)(2,1)S(1)} %broadcast_in_dim.4), channel_id=1, replica_groups=mesh['za'=2,'zb'=2,'zc'=2,'x'=4,'core'=2,'y'=4,'far'=2] {'x','y'}, dimensions={0} | all-to-all | bytes 1900544 | tf_op jit(solution)/shard_map/gather_tokens/all_to_all | solution.py:201
  39.3 5.3 %collective-permute-start = (bf16[16,2,16,928]{3,2,1,0:T(8,128)(2,1)S(1)}, bf16[16,2,16,928]{3,2,1,0:T(8,128)(2,1)S(1)}, u32[]{:S(2)}, u32[]{:S(2)}) collective-permute-start(bf16[16,2,16,928]{3,2,1,0:T(8,128)(2,1)S(1)} %all_to_all.10.plane_ref), channel_id=1, source_target_pairs={{0,8},{8,0},{1,9},{9,1},{2,10},{10,2},{3,11},{11,3},{4,12},{12,4},... | collective-permute-start | bytes 2850824 | tf_op jit(solution)/shard_map/gather_tokens/ppermute | solution.py:210
  44.5 0.0 copy-done
  44.5 0.0 copy-start.1
  44.6 1.2 copy-done.1
  45.7 1.4 row_sums.7
  47.1 0.0 collective-permute-done.plane_ref
  47.1 1.1 row_sums.8
  48.2 2.5 %collective-permute-start.1 = (bf16[2,464,128]{2,1,0:T(8,128)(2,1)S(1)}, bf16[2,464,128]{2,1,0:T(8,128)(2,1)S(1)}, u32[]{:S(2)}, u32[]{:S(2)}) collective-permute-start(bf16[2,464,128]{2,1,0:T(8,128)(2,1)S(1)} %get-tuple-element.41), channel_id=1, source_target_pairs={{0,64},{64,0},{1,65},{65,1},{2,66},{66,2},{3,67},{67,3},{4,68},{68... | collective-permute-start | bytes 712712 | tf_op jit(solution)/shard_map/row_sums/ppermute | solution.py:233
  50.8 1.1 row_sums.11
  51.9 2.8 %collective-permute-start.4 = (bf16[2,464,128]{2,1,0:T(8,128)(2,1)S(1)}, bf16[2,464,128]{2,1,0:T(8,128)(2,1)S(1)}, u32[]{:S(2)}, u32[]{:S(2)}) collective-permute-start(bf16[2,464,128]{2,1,0:T(8,128)(2,1)S(1)} %get-tuple-element.39), channel_id=1, source_target_pairs={{0,64},{64,0},{1,65},{65,1},{2,66},{66,2},{3,67},{67,3},{4,68},{68... | collective-permute-start | bytes 712712 | tf_op jit(solution)/shard_map/row_sums/ppermute | solution.py:233
  54.7 0.1 pad_add_fusion.bits_ref
  54.7 2.7 %collective-permute-done.1.arrived_ref = bf16[2,464,128]{2,1,0:T(8,128)(2,1)S(1)} collective-permute-done((bf16[2,464,128]{2,1,0:T(8,128)(2,1)S(1)}, bf16[2,464,128]{2,1,0:T(8,128)(2,1)S(1)}, u32[]{:S(2)}, u32[]{:S(2)}) %collective-permute-start.1) | collective-permute-done | bytes 237600 | tf_op jit(solution)/shard_map/row_sums/ppermute | solution.py:233
  57.5 0.6 row_sums.9
  58.1 3.1 %collective-permute-start.2 = (bf16[464,128]{1,0:T(8,128)(2,1)S(1)}, bf16[464,128]{1,0:T(8,128)(2,1)S(1)}, u32[]{:S(2)}, u32[]{:S(2)}) collective-permute-start(bf16[464,128]{1,0:T(8,128)(2,1)S(1)} %get-tuple-element.25), channel_id=1, source_target_pairs={{0,128},{128,0},{1,129},{129,1},{2,130},{130,2},{3,131},{131,3},{4... | collective-permute-start | bytes 356360 | tf_op jit(solution)/shard_map/row_sums/ppermute | solution.py:239
  61.2 1.4 collective-permute-done.4.arrived_ref
  62.6 0.6 row_sums.12
  63.2 3.1 %collective-permute-start.5 = (bf16[464,128]{1,0:T(8,128)(2,1)S(1)}, bf16[464,128]{1,0:T(8,128)(2,1)S(1)}, u32[]{:S(2)}, u32[]{:S(2)}) collective-permute-start(bf16[464,128]{1,0:T(8,128)(2,1)S(1)} %get-tuple-element.30), channel_id=1, source_target_pairs={{0,128},{128,0},{1,129},{129,1},{2,130},{130,2},{3,131},{131,3},{4... | collective-permute-start | bytes 356360 | tf_op jit(solution)/shard_map/row_sums/ppermute | solution.py:239
  66.3 1.8 %collective-permute-done.2.refs_1_ = bf16[464,128]{1,0:T(8,128)(2,1)S(1)} collective-permute-done((bf16[464,128]{1,0:T(8,128)(2,1)S(1)}, bf16[464,128]{1,0:T(8,128)(2,1)S(1)}, u32[]{:S(2)}, u32[]{:S(2)}) %collective-permute-start.2) | collective-permute-done | bytes 118816 | tf_op jit(solution)/shard_map/row_sums/ppermute | solution.py:239
  68.1 7.1 %collective-permute-start.3 = (bf16[464,128]{1,0:T(8,128)(2,1)S(1)}, bf16[464,128]{1,0:T(8,128)(2,1)S(1)}, u32[]{:S(2)}, u32[]{:S(2)}) collective-permute-start(bf16[464,128]{1,0:T(8,128)(2,1)S(1)} %row_sums.10), channel_id=1, source_target_pairs={{0,256},{256,0},{1,257},{257,1},{2,258},{258,2},{3,259},{259,3},{4... | collective-permute-start | bytes 356360 | tf_op jit(solution)/shard_map/row_sums/ppermute | solution.py:241
  75.2 0.0 collective-permute-done.5.refs_1_
  75.2 8.6 %collective-permute-start.6 = (bf16[464,128]{1,0:T(8,128)(2,1)S(1)}, bf16[464,128]{1,0:T(8,128)(2,1)S(1)}, u32[]{:S(2)}, u32[]{:S(2)}) collective-permute-start(bf16[464,128]{1,0:T(8,128)(2,1)S(1)} %row_sums.13), channel_id=1, source_target_pairs={{0,256},{256,0},{1,257},{257,1},{2,258},{258,2},{3,259},{259,3},{4... | collective-permute-start | bytes 356360 | tf_op jit(solution)/shard_map/row_sums/ppermute | solution.py:241
  83.9 0.0 collective-permute-done.3
  83.9 12.6 %collective-permute-done.6 = bf16[464,128]{1,0:T(8,128)(2,1)S(1)} collective-permute-done((bf16[464,128]{1,0:T(8,128)(2,1)S(1)}, bf16[464,128]{1,0:T(8,128)(2,1)S(1)}, u32[]{:S(2)}, u32[]{:S(2)}) %collective-permute-start.6) | collective-permute-done | bytes 118816 | tf_op jit(solution)/shard_map/row_sums/ppermute | solution.py:241
  96.5 0.2 multiply_convert_fusion
  96.6 12.1 %all-gather = bf16[1856,128]{1,0:T(8,128)(2,1)S(1)} all-gather(bf16[464,128]{1,0:T(8,128)(2,1)S(1)} %get-tuple-element.44), channel_id=2, replica_groups=mesh['za'=2,'zb'=2,'zc'=2,'x'=4,'core'=2,'y'=4,'far'=2] {'zb','zc'}, dimensions={0}, use_global_device_ids=true | all-gather | bytes 593920 | tf_op jit(solution)/shard_map/activate/all_gather | solution.py:204
  108.8 0.7 token_grad.6
  109.5 6.2 %collective-permute-start.7 = (bf16[256,928]{1,0:T(8,128)(2,1)S(1)}, bf16[256,928]{1,0:T(8,128)(2,1)S(1)}, u32[]{:S(2)}, u32[]{:S(2)}) collective-permute-start(bf16[256,928]{1,0:T(8,128)(2,1)S(1)} %token_grad.6), channel_id=1, source_target_pairs={{0,8},{8,0},{1,9},{9,1},{2,10},{10,2},{3,11},{11,3},{4,12},{12,4},... | collective-permute-start | bytes 1425416 | tf_op jit(solution)/shard_map/token_grad/ppermute | solution.py:257
  115.7 0.7 token_grad.5
  116.4 0.0 copy-start.4
  116.4 0.0 copy-start.2
  116.4 0.0 copy-start.3
  116.4 0.8 collective-permute-done.7.refs_1_
  117.2 0.9 token_grad.7
  118.1 0.0 copy-done.4
  118.1 3.8 %all-to-all-start.1 = ((bf16[16,16,928]{2,1,0:T(8,128)(2,1)}), bf16[16,16,928]{2,1,0:T(8,128)(2,1)S(1)}, u32[]{:S(2)}, u32[]{:S(2)}) async-start(bf16[16,16,928]{2,1,0:T(8,128)(2,1)} %bitcast.12), calls=%async_computation.1 | async-start | bytes 1048576 | tf_op jit(solution)/shard_map/token_grad/all_to_all | solution.py:201
  122.0 1.9 %collective-permute-start.11 = (bf16[464,128]{1,0:T(8,128)(2,1)}, bf16[464,128]{1,0:T(8,128)(2,1)S(1)}, u32[]{:S(2)}, u32[]{:S(2)}) collective-permute-start(bf16[464,128]{1,0:T(8,128)(2,1)} %copy-done.4), channel_id=1, source_target_pairs={{0,192},{64,128},{128,64},{192,0},{1,193},{65,129},{129,65},{193,1... | collective-permute-start | bytes 356360 | tf_op jit(solution)/shard_map/weight_grads/ppermute | solution.py:277
  123.9 2.3 %collective-permute-start.10 = (bf16[464,128]{1,0:T(8,128)(2,1)}, bf16[464,128]{1,0:T(8,128)(2,1)S(1)}, u32[]{:S(2)}, u32[]{:S(2)}) collective-permute-start(bf16[464,128]{1,0:T(8,128)(2,1)} %copy-done.4), channel_id=1, source_target_pairs={{0,128},{64,192},{128,0},{192,64},{1,129},{65,193},{129,1},{193,65... | collective-permute-start | bytes 356360 | tf_op jit(solution)/shard_map/weight_grads/ppermute | solution.py:277
  126.2 5.0 %collective-permute-start.9 = (bf16[464,128]{1,0:T(8,128)(2,1)}, bf16[464,128]{1,0:T(8,128)(2,1)S(1)}, u32[]{:S(2)}, u32[]{:S(2)}) collective-permute-start(bf16[464,128]{1,0:T(8,128)(2,1)} %copy-done.4), channel_id=1, source_target_pairs={{0,64},{64,0},{128,192},{192,128},{1,65},{65,1},{129,193},{193,129... | collective-permute-start | bytes 356360 | tf_op jit(solution)/shard_map/weight_grads/ppermute | solution.py:277
  131.3 1.0 all-to-all-done.1.blocks_ref
  132.3 0.1 token_grad.8
  132.4 11.0 %collective-permute-start.8 = (bf16[8,928]{1,0:T(8,128)(2,1)S(1)}, bf16[8,928]{1,0:T(8,128)(2,1)S(1)}, u32[]{:S(2)}, u32[]{:S(2)}) collective-permute-start(bf16[8,928]{1,0:T(8,128)(2,1)S(1)} %get-tuple-element.33), channel_id=1, source_target_pairs={{0,1},{1,0},{2,3},{3,2},{4,5},{5,4},{6,7},{7,6},{8,9},{9,8},{10,11... | collective-permute-start | bytes 44552 | tf_op jit(solution)/shard_map/token_grad/ppermute | solution.py:272
  143.4 0.0 collective-permute-done.11.refs_3_
  143.4 0.0 collective-permute-done.10.refs_2_
  143.5 0.0 collective-permute-done.9.refs_1_
  143.5 0.0 copy-done.2
  143.5 0.0 copy-done.3
  143.5 0.0 copy-start.5
  143.5 0.9 copy-done.5
  144.4 2.8 %weight_grads.1 = (f32[928,464]{1,0:T(8,128)}, f32[464,928]{1,0:T(8,128)}) custom-call(s32[1]{0:T(128)} %bitcast.13.place_ref, bf16[512,928]{1,0:T(8,128)(2,1)S(1)} %copy-done.2, bf16[512,928]{1,0:T(8,128)(2,1)S(1)} %copy-done.3, bf16[4,464,128]{2,1,0:T(8,128)(2,1)S(1)} %bitcast.28, bf16[464,128]{1,0:T(8,128)(2,1)S(1)} %copy-done.5, ...), custom_call_target="tpu_custom_call" | custom-call | flops 881852416 | bytes 8388608 | tf_op jit(solution)/shard_map/weight_grads/pallas_call | solution.py:178
  147.2 0.0 collective-permute-done.8.refs_1_
  147.2 0.6 token_grad.9
  (4 shorter events, 0.1 us)
Async XLA Ops:
  0.6 43.9 %copy-start = (bf16[928,464]{1,0:T(8,128)(2,1)S(1)}, bf16[928,464]{1,0:T(8,128)(2,1)}, u32[]{:S(2)}) copy-start(bf16[928,464]{1,0:T(8,128)(2,1)} %up_ref.3) | copy-start | bytes 2583556
  39.3 7.8 %collective-permute-start = (bf16[16,2,16,928]{3,2,1,0:T(8,128)(2,1)S(1)}, bf16[16,2,16,928]{3,2,1,0:T(8,128)(2,1)S(1)}, u32[]{:S(2)}, u32[]{:S(2)}) collective-permute-start(bf16[16,2,16,928]{3,2,1,0:T(8,128)(2,1)S(1)} %all_to_all.10.plane_ref), channel_id=1, source_target_pairs={{0,8},{8,0},{1,9},{9,1},{2,10},{10,2},{3,11},{11,3},{4,12},{12,4},... | collective-permute-start | bytes 2850824 | tf_op jit(solution)/shard_map/gather_tokens/ppermute | solution.py:210
  44.5 1.2 copy-start.1
  48.2 9.2 %collective-permute-start.1 = (bf16[2,464,128]{2,1,0:T(8,128)(2,1)S(1)}, bf16[2,464,128]{2,1,0:T(8,128)(2,1)S(1)}, u32[]{:S(2)}, u32[]{:S(2)}) collective-permute-start(bf16[2,464,128]{2,1,0:T(8,128)(2,1)S(1)} %get-tuple-element.41), channel_id=1, source_target_pairs={{0,64},{64,0},{1,65},{65,1},{2,66},{66,2},{3,67},{67,3},{4,68},{68... | collective-permute-start | bytes 712712 | tf_op jit(solution)/shard_map/row_sums/ppermute | solution.py:233
  51.9 10.7 %collective-permute-start.4 = (bf16[2,464,128]{2,1,0:T(8,128)(2,1)S(1)}, bf16[2,464,128]{2,1,0:T(8,128)(2,1)S(1)}, u32[]{:S(2)}, u32[]{:S(2)}) collective-permute-start(bf16[2,464,128]{2,1,0:T(8,128)(2,1)S(1)} %get-tuple-element.39), channel_id=1, source_target_pairs={{0,64},{64,0},{1,65},{65,1},{2,66},{66,2},{3,67},{67,3},{4,68},{68... | collective-permute-start | bytes 712712 | tf_op jit(solution)/shard_map/row_sums/ppermute | solution.py:233
  58.1 10.0 %collective-permute-start.2 = (bf16[464,128]{1,0:T(8,128)(2,1)S(1)}, bf16[464,128]{1,0:T(8,128)(2,1)S(1)}, u32[]{:S(2)}, u32[]{:S(2)}) collective-permute-start(bf16[464,128]{1,0:T(8,128)(2,1)S(1)} %get-tuple-element.25), channel_id=1, source_target_pairs={{0,128},{128,0},{1,129},{129,1},{2,130},{130,2},{3,131},{131,3},{4... | collective-permute-start | bytes 356360 | tf_op jit(solution)/shard_map/row_sums/ppermute | solution.py:239
  63.2 12.0 %collective-permute-start.5 = (bf16[464,128]{1,0:T(8,128)(2,1)S(1)}, bf16[464,128]{1,0:T(8,128)(2,1)S(1)}, u32[]{:S(2)}, u32[]{:S(2)}) collective-permute-start(bf16[464,128]{1,0:T(8,128)(2,1)S(1)} %get-tuple-element.30), channel_id=1, source_target_pairs={{0,128},{128,0},{1,129},{129,1},{2,130},{130,2},{3,131},{131,3},{4... | collective-permute-start | bytes 356360 | tf_op jit(solution)/shard_map/row_sums/ppermute | solution.py:239
  68.1 15.8 %collective-permute-start.3 = (bf16[464,128]{1,0:T(8,128)(2,1)S(1)}, bf16[464,128]{1,0:T(8,128)(2,1)S(1)}, u32[]{:S(2)}, u32[]{:S(2)}) collective-permute-start(bf16[464,128]{1,0:T(8,128)(2,1)S(1)} %row_sums.10), channel_id=1, source_target_pairs={{0,256},{256,0},{1,257},{257,1},{2,258},{258,2},{3,259},{259,3},{4... | collective-permute-start | bytes 356360 | tf_op jit(solution)/shard_map/row_sums/ppermute | solution.py:241
  75.2 21.2 %collective-permute-start.6 = (bf16[464,128]{1,0:T(8,128)(2,1)S(1)}, bf16[464,128]{1,0:T(8,128)(2,1)S(1)}, u32[]{:S(2)}, u32[]{:S(2)}) collective-permute-start(bf16[464,128]{1,0:T(8,128)(2,1)S(1)} %row_sums.13), channel_id=1, source_target_pairs={{0,256},{256,0},{1,257},{257,1},{2,258},{258,2},{3,259},{259,3},{4... | collective-permute-start | bytes 356360 | tf_op jit(solution)/shard_map/row_sums/ppermute | solution.py:241
  109.5 7.7 %collective-permute-start.7 = (bf16[256,928]{1,0:T(8,128)(2,1)S(1)}, bf16[256,928]{1,0:T(8,128)(2,1)S(1)}, u32[]{:S(2)}, u32[]{:S(2)}) collective-permute-start(bf16[256,928]{1,0:T(8,128)(2,1)S(1)} %token_grad.6), channel_id=1, source_target_pairs={{0,8},{8,0},{1,9},{9,1},{2,10},{10,2},{3,11},{11,3},{4,12},{12,4},... | collective-permute-start | bytes 1425416 | tf_op jit(solution)/shard_map/token_grad/ppermute | solution.py:257
  116.4 1.8 %copy-start.4 = (bf16[464,128]{1,0:T(8,128)(2,1)}, bf16[464,128]{1,0:T(8,128)(2,1)S(1)}, u32[]{:S(2)}) copy-start(bf16[464,128]{1,0:T(8,128)(2,1)S(1)} %get-tuple-element.36.refs_0_) | copy-start | bytes 356356
  116.4 27.1 %copy-start.2 = (bf16[512,928]{1,0:T(8,128)(2,1)S(1)}, bf16[512,928]{1,0:T(8,128)(2,1)}, u32[]{:S(2)}) copy-start(bf16[512,928]{1,0:T(8,128)(2,1)} %get-tuple-element.34.inputs_ref) | copy-start | bytes 2850820
  116.4 27.1 %copy-start.3 = (bf16[512,928]{1,0:T(8,128)(2,1)S(1)}, bf16[512,928]{1,0:T(8,128)(2,1)}, u32[]{:S(2)}) copy-start(bf16[512,928]{1,0:T(8,128)(2,1)} %get-tuple-element.35.upstream_ref) | copy-start | bytes 2850820
  118.1 14.2 %all-to-all-start.1 = ((bf16[16,16,928]{2,1,0:T(8,128)(2,1)}), bf16[16,16,928]{2,1,0:T(8,128)(2,1)S(1)}, u32[]{:S(2)}, u32[]{:S(2)}) async-start(bf16[16,16,928]{2,1,0:T(8,128)(2,1)} %bitcast.12), calls=%async_computation.1 | async-start | bytes 1048576 | tf_op jit(solution)/shard_map/token_grad/all_to_all | solution.py:201
  122.0 21.5 %collective-permute-start.11 = (bf16[464,128]{1,0:T(8,128)(2,1)}, bf16[464,128]{1,0:T(8,128)(2,1)S(1)}, u32[]{:S(2)}, u32[]{:S(2)}) collective-permute-start(bf16[464,128]{1,0:T(8,128)(2,1)} %copy-done.4), channel_id=1, source_target_pairs={{0,192},{64,128},{128,64},{192,0},{1,193},{65,129},{129,65},{193,1... | collective-permute-start | bytes 356360 | tf_op jit(solution)/shard_map/weight_grads/ppermute | solution.py:277
  123.9 19.6 %collective-permute-start.10 = (bf16[464,128]{1,0:T(8,128)(2,1)}, bf16[464,128]{1,0:T(8,128)(2,1)S(1)}, u32[]{:S(2)}, u32[]{:S(2)}) collective-permute-start(bf16[464,128]{1,0:T(8,128)(2,1)} %copy-done.4), channel_id=1, source_target_pairs={{0,128},{64,192},{128,0},{192,64},{1,129},{65,193},{129,1},{193,65... | collective-permute-start | bytes 356360 | tf_op jit(solution)/shard_map/weight_grads/ppermute | solution.py:277
  126.2 17.2 %collective-permute-start.9 = (bf16[464,128]{1,0:T(8,128)(2,1)}, bf16[464,128]{1,0:T(8,128)(2,1)S(1)}, u32[]{:S(2)}, u32[]{:S(2)}) collective-permute-start(bf16[464,128]{1,0:T(8,128)(2,1)} %copy-done.4), channel_id=1, source_target_pairs={{0,64},{64,0},{128,192},{192,128},{1,65},{65,1},{129,193},{193,129... | collective-permute-start | bytes 356360 | tf_op jit(solution)/shard_map/weight_grads/ppermute | solution.py:277
  132.4 14.8 %collective-permute-start.8 = (bf16[8,928]{1,0:T(8,128)(2,1)S(1)}, bf16[8,928]{1,0:T(8,128)(2,1)S(1)}, u32[]{:S(2)}, u32[]{:S(2)}) collective-permute-start(bf16[8,928]{1,0:T(8,128)(2,1)S(1)} %get-tuple-element.33), channel_id=1, source_target_pairs={{0,1},{1,0},{2,3},{3,2},{4,5},{5,4},{6,7},{7,6},{8,9},{9,8},{10,11... | collective-permute-start | bytes 44552 | tf_op jit(solution)/shard_map/token_grad/ppermute | solution.py:272
  143.5 0.9 copy-start.5
